TPU v7x, 32 devices: a whole 2x2x4 slice. The times are simulated.
32 devices in a mesh: seq: 2 (over core), row: 4 (over y, x), col: 4 (over z).
Axes of the slice: x: 2, y: 2, z: 4, core: 2. Of those that a mesh axis runs over, the one named last changes fastest.
Arguments:
- layer_in: bfloat16 [2, 1024, 2048], P(None, ('seq', 'col'), 'row'), may hold values from -6 to 6
- per_layer_in: bfloat16 [2, 1024, 256], P(None, ('seq', 'col')), may hold values from -6 to 6
- doc_lengths: int32 [2, 4], replicated, may hold values from 1 to 512, 1024 in all within a row
- w_query: bfloat16 [2048, 2048], P('row', 'col'), may hold values from -0.125 to 0.125
- w_key: bfloat16 [2048, 512], P('row', 'col'), may hold values from -0.125 to 0.125
- w_value: bfloat16 [2048, 512], P('row', 'col'), may hold values from -0.125 to 0.125
- w_out: bfloat16 [2048, 2048], P('col', 'row'), may hold values from -0.125 to 0.125
- w_gate: bfloat16 [2048, 8192], P('row', 'col'), may hold values from -0.125 to 0.125
- w_up: bfloat16 [2048, 8192], P('row', 'col'), may hold values from -0.125 to 0.125
- w_down: bfloat16 [8192, 2048], P('col', 'row'), may hold values from -0.0625 to 0.0625
- laurel_left: bfloat16 [2048, 64], P('row'), may hold values from -0.125 to 0.125
- laurel_right: bfloat16 [64, 2048], P(None, 'row'), may hold values from -0.75 to 0.75
- per_gate: bfloat16 [2048, 256], P('row'), may hold values from -0.125 to 0.125
- per_proj: bfloat16 [256, 2048], P(None, 'row'), may hold values from -0.375 to 0.375
- norm_gains: float32 [6, 2048], P(None, 'row'), may hold values from 0.5 to 1.5
- head_gains: float32 [2, 256], replicated, may hold values from 0.25 to 0.4
- out_grad: bfloat16 [2, 1024, 2048], P(None, ('seq', 'col'), 'row'), may hold values from -6 to 6
Outputs:
- layer_out: bfloat16 [2, 1024, 2048], P(None, ('seq', 'col'), 'row')
- grad_in: bfloat16 [2, 1024, 2048], P(None, ('seq', 'col'), 'row')
- grad_w_query: float32 [2048, 2048], P('row', 'col')
- grad_w_key: float32 [2048, 512], P('row', 'col')
- grad_w_value: float32 [2048, 512], P('row', 'col')
- grad_w_out: float32 [2048, 2048], P('col', 'row')
- grad_w_gate: float32 [2048, 8192], P('row', 'col')
- grad_w_up: float32 [2048, 8192], P('row', 'col')
- grad_w_down: float32 [8192, 2048], P('col', 'row')
- grad_laurel_left: float32 [2048, 64], P('row')
- grad_laurel_right: float32 [64, 2048], P(None, 'row')
- grad_per_gate: float32 [2048, 256], P('row')
- grad_per_proj: float32 [256, 2048], P(None, 'row')
- grad_norm_gains: float32 [6, 2048], P(None, 'row')
- grad_head_gains: float32 [2, 256], replicated
- clipped_gains: float32 [2, 8, 256], replicated
Inputs may be any that keep to these rules, and one draw needn't show every extreme that they name: `doc_lengths`: each row lists the lengths of one sequence's documents in order; they sum to 1024 and the longest is exactly 512.
All inputs are finite; a program needn't handle non-finite values.
Results may differ from a plain program's by a relative error of at most 0.017.
Values may be sent and summed in bfloat16 or wider, within the bound.
A program may use at most 128 MiB of HBM per device.

v0:
```python
import jax
import jax.numpy as jnp
from jax import lax
from jax.sharding import PartitionSpec as P

EPSILON = 1e-06
CLIP_LEVEL = 3.0
ROPE_BASE = 1000000.0
ROOT_HALF = 0.7071067811865476
MASK_FILL = -1e30


def swapped(value, axis, apart):
    mask = 2**apart
    pairs = [(source, source ^ mask) for source in range(lax.axis_size(axis))]
    return lax.ppermute(value, axis, pairs)


def width_total(values):
    return lax.psum(values, "row")


def gather_tokens(values):
    return lax.all_gather(values, "col", axis=1, tiled=True)


def spread_rows(values, project):
    gathered = gather_tokens(values)
    return (gathered, lax.psum_scatter(project(gathered), "row", scatter_dimension=1, tiled=True))


def spread_cols(values, project):
    gathered = lax.all_gather(values, "row", axis=1, tiled=True)
    return (gathered, lax.psum_scatter(project(gathered), "col", scatter_dimension=1, tiled=True))


def times_right(left_side, right_side):
    return jnp.einsum("std,dn->stn", left_side, right_side, preferred_element_type=jnp.float32)


def times_back(left_side, right_side):
    return jnp.einsum("stn,dn->std", left_side, right_side, preferred_element_type=jnp.float32)


def outer_sum(left_side, right_side):
    return jnp.einsum("std,stn->dn", left_side, right_side, preferred_element_type=jnp.float32)


def norm_forward(values, gain_vec, width_all):
    square_sum = width_total(jnp.sum(values * values, axis=-1, keepdims=True))
    factor = lax.rsqrt(square_sum / width_all + EPSILON)
    normed = values * factor
    return (normed * gain_vec, normed, factor)


def norm_backward(grad_values, normed, factor, gain_vec, width_all):
    grad_normed = grad_values * gain_vec
    inner_sum = width_total(jnp.sum(grad_normed * normed, axis=-1, keepdims=True))
    result = factor * (grad_normed - normed * (inner_sum / width_all))
    return (result, jnp.sum(grad_values * normed, axis=(0, 1)))


def head_norm(values, gain_vec):
    return (
        values * lax.rsqrt(jnp.mean(values * values, axis=-1, keepdims=True) + EPSILON) * gain_vec
    )


def rotation(position, width_all):
    half_width = width_all // 2
    frequency = ROPE_BASE ** (-2.0 * jnp.arange(half_width, dtype=jnp.float32) / width_all)
    angles = position.astype(jnp.float32)[..., None] * frequency
    cosine_table = jnp.concatenate([jnp.cos(angles), jnp.cos(angles)], axis=-1)
    sine_table = jnp.concatenate([jnp.sin(angles), jnp.sin(angles)], axis=-1)
    return (cosine_table, sine_table)


def rotate(values, cosine_table, sine_table):
    half_width = values.shape[-1] // 2
    turned = jnp.concatenate([-values[..., half_width:], values[..., :half_width]], axis=-1)
    return values * cosine_table + turned * sine_table


def doc_places(doc_lengths, first_place, place_count):
    doc_ends = jnp.cumsum(doc_lengths, axis=1)
    places = first_place + jnp.arange(place_count, dtype=jnp.int32)
    before = (doc_ends[:, None, :] <= places[None, :, None]).astype(jnp.int32)
    segment = jnp.sum(before, axis=2)
    doc_start = jnp.sum(before * doc_lengths[:, None, :], axis=2)
    return (segment, places, places[None, :] - doc_start)


def block_scores(queries, keys_all, block_start, block_size, query_seg, query_place, key_seg):
    keys_part = lax.dynamic_slice_in_dim(keys_all, block_start, block_size, 1)
    scores = jnp.einsum("sqhd,skd->shqk", queries, keys_part, preferred_element_type=jnp.float32)
    seg_part = lax.dynamic_slice_in_dim(key_seg, block_start, block_size, 1)
    key_place = block_start + jnp.arange(block_size, dtype=jnp.int32)
    allowed = (query_seg[:, None, :, None] == seg_part[:, None, None, :]) & (
        key_place[None, None, None, :] <= query_place[None, None, :, None]
    )
    return (scores, allowed)


def body(
    layer_in,
    per_layer_in,
    doc_lengths,
    w_query,
    w_key,
    w_value,
    w_out,
    w_gate,
    w_up,
    w_down,
    laurel_left,
    laurel_right,
    per_gate,
    per_proj,
    norm_gains,
    head_gains,
    out_grad,
):
    seq_count = layer_in.shape[0]
    width_all = layer_in.shape[2] * lax.axis_size("row")
    head_dim = head_gains.shape[1]
    heads_here = w_query.shape[1] // head_dim
    heads_all = heads_here * lax.axis_size("col")
    key_width = w_key.shape[1]
    ff_here = w_gate.shape[1]
    local_len = layer_in.shape[1] * lax.axis_size("col")
    tokens_row = local_len // lax.axis_size("row")
    seq_len = local_len * lax.axis_size("seq")
    col_index = lax.axis_index("col")
    even_col = col_index % 2 == 0
    q_width = heads_here * head_dim
    partner_key, partner_value = swapped((w_key, w_value), "col", 0)
    key_head = jnp.where(
        even_col,
        jnp.concatenate([w_key, partner_key], axis=1),
        jnp.concatenate([partner_key, w_key], axis=1),
    )
    value_head = jnp.where(
        even_col,
        jnp.concatenate([w_value, partner_value], axis=1),
        jnp.concatenate([partner_value, w_value], axis=1),
    )
    w_heads = jnp.concatenate([w_query, key_head, value_head], axis=1)
    w_back = jnp.concatenate([w_query, w_key, w_value], axis=1)
    w_gate_up = jnp.concatenate([w_gate, w_up], axis=1)
    inputs = layer_in.astype(jnp.float32)
    x_norm, x_normed, x_factor = norm_forward(inputs, norm_gains[0], width_all)
    x_low = x_norm.astype(jnp.bfloat16)
    x_rows, head_raw = spread_rows(x_low, lambda gathered: times_right(gathered, w_heads))
    q_raw = head_raw[:, :, :q_width].reshape(seq_count, tokens_row, heads_here, head_dim)
    k_raw = head_raw[:, :, q_width : q_width + head_dim]
    v_raw = head_raw[:, :, q_width + head_dim :]
    query_seg, query_place, query_pos = doc_places(
        doc_lengths, lax.axis_index(("seq", "row")) * tokens_row, tokens_row
    )
    key_seg, unused_place, unused_pos = doc_places(doc_lengths, 0, seq_len)
    cosine_table, sine_table = rotation(query_pos, head_dim)

    def query_prep(raw_part, gain_vec):
        return rotate(
            head_norm(raw_part, gain_vec), cosine_table[:, :, None], sine_table[:, :, None]
        )

    def key_prep(raw_part, gain_vec):
        return rotate(head_norm(raw_part, gain_vec), cosine_table, sine_table)

    def value_prep(raw_part):
        return head_norm(raw_part, 1.0)

    q_rot, query_back = jax.vjp(query_prep, q_raw, head_gains[0])
    k_rot, key_back = jax.vjp(key_prep, k_raw, head_gains[1])
    v_normed, value_back = jax.vjp(value_prep, v_raw)
    q_low = q_rot.astype(jnp.bfloat16)
    keys_all, values_all = (
        lax.all_gather(k_rot.astype(jnp.bfloat16), ("seq", "row"), axis=1, tiled=True),
        lax.all_gather(v_normed.astype(jnp.bfloat16), ("seq", "row"), axis=1, tiled=True),
    )
    block_size = min(512, seq_len)
    block_count = seq_len // block_size
    blocks = jnp.arange(block_count, dtype=jnp.int32)

    def scored(block_index):
        return block_scores(
            q_low, keys_all, block_index * block_size, block_size, query_seg, query_place, key_seg
        )

    def values_at(block_index):
        return lax.dynamic_slice_in_dim(values_all, block_index * block_size, block_size, 1)

    def stats_step(carry, block_index):
        row_top, row_total = carry
        scores, allowed = scored(block_index)
        new_top = jnp.maximum(row_top, jnp.max(jnp.where(allowed, scores, MASK_FILL), axis=3))
        weights = jnp.where(allowed, jnp.exp(scores - new_top[..., None]), 0.0)
        row_total = row_total * jnp.exp(row_top - new_top) + jnp.sum(weights, axis=3)
        return ((new_top, row_total), None)

    start_top = jnp.full((seq_count, heads_here, tokens_row), MASK_FILL, jnp.float32)
    (row_top, row_total), unused = lax.scan(
        stats_step, (start_top, jnp.zeros_like(start_top)), blocks
    )
    log_total = row_top + jnp.log(row_total)

    def probs_at(block_index):
        scores, allowed = scored(block_index)
        return jnp.where(allowed, jnp.exp(scores - log_total[..., None]), 0.0)

    def out_step(total_out, block_index):
        probs_low = probs_at(block_index).astype(jnp.bfloat16)
        total_out = total_out + jnp.einsum(
            "shqk,skd->sqhd", probs_low, values_at(block_index), preferred_element_type=jnp.float32
        )
        return (total_out, None)

    attended, unused = lax.scan(
        out_step, jnp.zeros((seq_count, tokens_row, heads_here, head_dim), jnp.float32), blocks
    )
    o_low = attended.astype(jnp.bfloat16).reshape(seq_count, tokens_row, q_width)
    head_slots = lax.dynamic_update_slice_in_dim(
        jnp.full((heads_all,), MASK_FILL, jnp.float32),
        jnp.max(row_top, axis=(0, 2)),
        col_index * heads_here,
        0,
    )
    logit_top = lax.pmax(head_slots, ("seq", "row", "col"))
    o_rows, attn_val = spread_cols(o_low, lambda gathered: times_right(gathered, w_out))
    attn_norm, attn_normed, attn_factor = norm_forward(attn_val, norm_gains[1], width_all)
    h_one = inputs + attn_norm
    lr_low = width_total(times_right(x_low, laurel_left)).astype(jnp.bfloat16)
    lo_val = times_right(lr_low, laurel_right)
    lo_norm, lo_normed, lo_factor = norm_forward(lo_val, norm_gains[2], width_all)
    h_two = (h_one + (x_norm + lo_norm)) * ROOT_HALF
    f_norm, f_normed, f_factor = norm_forward(h_two, norm_gains[3], width_all)
    f_low = f_norm.astype(jnp.bfloat16)
    f_rows, gate_up = spread_rows(f_low, lambda gathered: times_right(gathered, w_gate_up))
    gate_val = gate_up[:, :, :ff_here]
    up_val = gate_up[:, :, ff_here:]

    def geglu(gate_part, up_part):
        return jax.nn.gelu(gate_part, approximate=True) * up_part

    hidden, geglu_back = jax.vjp(geglu, gate_val, up_val)
    hid_low = hidden.astype(jnp.bfloat16)
    hid_rows, ff_val = spread_cols(hid_low, lambda gathered: times_right(gathered, w_down))
    ff_norm, ff_normed, ff_factor = norm_forward(ff_val, norm_gains[4], width_all)
    h_three = h_two + ff_norm
    h_low = h_three.astype(jnp.bfloat16)
    pg_val = width_total(times_right(h_low, per_gate))
    per_input = per_layer_in.astype(jnp.float32)

    def per_mix(gate_part):
        return jax.nn.gelu(gate_part, approximate=True) * per_input

    gp_val, per_back = jax.vjp(per_mix, pg_val)
    gp_low = gp_val.astype(jnp.bfloat16)
    pp_val = times_right(gp_low, per_proj)
    pp_norm, pp_normed, pp_factor = norm_forward(pp_val, norm_gains[5], width_all)
    layer_out = (h_three + pp_norm).astype(jnp.bfloat16)
    grad_top = out_grad.astype(jnp.float32)
    d_pp, gain_five = norm_backward(grad_top, pp_normed, pp_factor, norm_gains[5], width_all)
    d_pp_low = d_pp.astype(jnp.bfloat16)
    grad_per_proj = outer_sum(gp_low, d_pp_low)
    (d_pg,) = per_back(width_total(times_back(d_pp_low, per_proj)))
    d_pg_low = d_pg.astype(jnp.bfloat16)
    grad_per_gate = outer_sum(h_low, d_pg_low)
    d_three = grad_top + times_back(d_pg_low, per_gate)
    d_ff, gain_four = norm_backward(d_three, ff_normed, ff_factor, norm_gains[4], width_all)
    d_ff_low = d_ff.astype(jnp.bfloat16)
    dff_rows, d_hidden = spread_rows(d_ff_low, lambda gathered: times_back(gathered, w_down))
    grad_down = outer_sum(hid_rows, dff_rows)
    d_gate, d_up = geglu_back(d_hidden)
    d_gate_up = jnp.concatenate([d_gate, d_up], axis=2).astype(jnp.bfloat16)
    dgu_rows, d_f_low = spread_cols(d_gate_up, lambda gathered: times_back(gathered, w_gate_up))
    grad_gate_up = outer_sum(f_rows, dgu_rows)
    d_f, gain_three = norm_backward(d_f_low, f_normed, f_factor, norm_gains[3], width_all)
    d_half = (d_three + d_f) * ROOT_HALF
    d_lo, gain_two = norm_backward(d_half, lo_normed, lo_factor, norm_gains[2], width_all)
    d_lo_low = d_lo.astype(jnp.bfloat16)
    grad_laurel_right = outer_sum(lr_low, d_lo_low)
    d_lr_low = width_total(times_back(d_lo_low, laurel_right)).astype(jnp.bfloat16)
    grad_laurel_left = outer_sum(x_low, d_lr_low)
    d_attn, gain_one = norm_backward(d_half, attn_normed, attn_factor, norm_gains[1], width_all)
    d_attn_low = d_attn.astype(jnp.bfloat16)
    dattn_rows, d_o = spread_rows(d_attn_low, lambda gathered: times_back(gathered, w_out))
    grad_w_out = outer_sum(o_rows, dattn_rows)
    d_o_low = d_o.astype(jnp.bfloat16).reshape(seq_count, tokens_row, heads_here, head_dim)

    def delta_step(total_delta, block_index):
        d_probs = jnp.einsum(
            "sqhd,skd->shqk", d_o_low, values_at(block_index), preferred_element_type=jnp.float32
        )
        return (total_delta + jnp.sum(probs_at(block_index) * d_probs, axis=3), None)

    row_delta, unused = lax.scan(delta_step, jnp.zeros_like(log_total), blocks)

    def grad_step(carry, block_index):
        d_query, d_keys, d_values = carry
        block_start = block_index * block_size
        prob_vals = probs_at(block_index)
        d_probs = jnp.einsum(
            "sqhd,skd->shqk", d_o_low, values_at(block_index), preferred_element_type=jnp.float32
        )
        d_scores = (prob_vals * (d_probs - row_delta[..., None])).astype(jnp.bfloat16)
        keys_part = lax.dynamic_slice_in_dim(keys_all, block_start, block_size, 1)
        d_query = d_query + jnp.einsum(
            "shqk,skd->sqhd", d_scores, keys_part, preferred_element_type=jnp.float32
        )
        key_part = jnp.einsum("shqk,sqhd->skd", d_scores, q_low, preferred_element_type=jnp.float32)
        value_part = jnp.einsum(
            "shqk,sqhd->skd",
            prob_vals.astype(jnp.bfloat16),
            d_o_low,
            preferred_element_type=jnp.float32,
        )
        d_keys = lax.dynamic_update_slice_in_dim(d_keys, key_part, block_start, 1)
        d_values = lax.dynamic_update_slice_in_dim(d_values, value_part, block_start, 1)
        return ((d_query, d_keys, d_values), None)

    zero_keys = jnp.zeros((seq_count, seq_len, head_dim), jnp.float32)
    (d_query, d_keys, d_values), unused = lax.scan(
        grad_step, (jnp.zeros_like(attended), zero_keys, zero_keys), blocks
    )
    own_keys, own_values = (
        lax.psum_scatter(d_keys, ("seq", "row"), scatter_dimension=1, tiled=True),
        lax.psum_scatter(d_values, ("seq", "row"), scatter_dimension=1, tiled=True),
    )
    pair_keys, pair_values = swapped((own_keys, own_values), "col", 0)
    d_q_raw, d_q_gain = query_back(d_query)
    d_k_raw, d_k_gain = key_back(own_keys + pair_keys)
    (d_v_raw,) = value_back(own_values + pair_values)
    key_offset = col_index % 2 * key_width
    d_heads_low = jnp.concatenate(
        [
            d_q_raw.reshape(seq_count, tokens_row, q_width),
            lax.dynamic_slice_in_dim(d_k_raw, key_offset, key_width, 2),
            lax.dynamic_slice_in_dim(d_v_raw, key_offset, key_width, 2),
        ],
        axis=2,
    ).astype(jnp.bfloat16)
    dhead_rows, d_x_heads = spread_cols(d_heads_low, lambda gathered: times_back(gathered, w_back))
    grad_heads = outer_sum(x_rows, dhead_rows)
    d_x_low = d_x_heads + times_back(d_lr_low, laurel_left)
    d_x_part, gain_zero = norm_backward(
        d_half + d_x_low, x_normed, x_factor, norm_gains[0], width_all
    )
    grad_in = (d_half + d_x_part).astype(jnp.bfloat16)
    head_part = width_total(jnp.stack([d_q_gain, d_k_gain * 0.5]))
    sum_heads, sum_out, sum_gate_up, sum_down = lax.psum(
        (grad_heads, grad_w_out, grad_gate_up, grad_down), "seq"
    )
    sum_left, sum_right, sum_per_gate, sum_per_proj, sum_gains, sum_head_gains = lax.psum(
        (
            grad_laurel_left,
            grad_laurel_right,
            grad_per_gate,
            grad_per_proj,
            jnp.stack([gain_zero, gain_one, gain_two, gain_three, gain_four, gain_five]),
            head_part,
        ),
        ("seq", "col"),
    )
    clip_factor = jnp.sqrt(CLIP_LEVEL / jnp.maximum(logit_top, CLIP_LEVEL))
    clipped_gains = jnp.stack(
        [
            clip_factor[:, None] * head_gains[0][None, :],
            clip_factor[:, None] * head_gains[1][None, :],
        ]
    )
    return (
        layer_out,
        grad_in,
        sum_heads[:, :q_width],
        sum_heads[:, q_width : q_width + key_width],
        sum_heads[:, q_width + key_width :],
        sum_out,
        sum_gate_up[:, :ff_here],
        sum_gate_up[:, ff_here:],
        sum_down,
        sum_left,
        sum_right,
        sum_per_gate,
        sum_per_proj,
        sum_gains,
        sum_head_gains,
        clipped_gains,
    )


def solution(mesh):
    return jax.shard_map(
        body,
        mesh=mesh,
        in_specs=(
            P(None, ("seq", "col"), "row"),
            P(None, ("seq", "col"), None),
            P(),
            P("row", "col"),
            P("row", "col"),
            P("row", "col"),
            P("col", "row"),
            P("row", "col"),
            P("row", "col"),
            P("col", "row"),
            P("row", None),
            P(None, "row"),
            P("row", None),
            P(None, "row"),
            P(None, "row"),
            P(),
            P(None, ("seq", "col"), "row"),
        ),
        out_specs=(
            P(None, ("seq", "col"), "row"),
            P(None, ("seq", "col"), "row"),
            P("row", "col"),
            P("row", "col"),
            P("row", "col"),
            P("col", "row"),
            P("row", "col"),
            P("row", "col"),
            P("col", "row"),
            P("row", None),
            P(None, "row"),
            P("row", None),
            P(None, "row"),
            P(None, "row"),
            P(),
            P(),
        ),
        check_vma=False,
    )
```

profile of v0, /device:TPU:1, one launch (start us, length us, event | category | flops | bytes accessed | tf_op | source)
XLA Modules:
  0.0 1421.2 jit_solution(11726077256931787590)
XLA Ops:
  9.9 8.7 psum.189
  27.1 22.7 %all-gather.11.cloned.1.call-done = bf16[2,512,512]{2,1,0:T(8,128)(2,1)} async-done(((bf16[2,128,512]{2,1,0:T(8,128)(2,1)}), bf16[2,512,512]{2,1,0:T(8,128)(2,1)}) %all-gather.11.cloned.1.call-update) | async-done | bytes 1048592 | tf_op jit(solution)/shard_map/all_gather | solution.py:24
  56.4 50.4 %reduce-scatter.11.cloned.1.call-done = f32[2,128,1024]{2,1,0:T(8,128)} async-done(((f32[2,512,1024]{2,1,0:T(8,128)}), f32[2,128,1024]{2,1,0:T(8,128)}) %reduce-scatter.11.cloned.1.call-update) | async-done | bytes 1048592 | tf_op jit(solution)/shard_map/reduce_scatter | solution.py:29
  115.9 19.5 %all-gather.15.cloned.1.call-done = bf16[2,1024,256]{2,1,0:T(8,128)(2,1)} async-done(((bf16[2,128,256]{2,1,0:T(8,128)(2,1)}), bf16[2,1024,256]{2,1,0:T(8,128)(2,1)}) %all-gather.15.cloned.1.call-update) | async-done | bytes 1048592 | tf_op jit(solution)/shard_map/all_gather | solution.py:179
  135.9 12.2 while.50
  149.5 11.9 all-gather.13.cloned.1.call-done
  161.4 8.6 while.51
  172.7 26.3 %all-gather.17.cloned.1.call-done = bf16[2,512,512]{2,1,0:T(8,128)(2,1)} async-done(((bf16[2,128,512]{2,1,0:T(8,128)(2,1)}), bf16[2,512,512]{2,1,0:T(8,128)(2,1)}) %all-gather.17.cloned.1.call-update) | async-done | bytes 1048592 | tf_op jit(solution)/shard_map/all_gather | solution.py:33
  202.5 12.8 psum.191
  215.7 30.4 %reduce-scatter.13.cloned.1.call-done = f32[2,128,512]{2,1,0:T(8,128)} async-done(((f32[2,512,512]{2,1,0:T(8,128)}), f32[2,128,512]{2,1,0:T(8,128)}) %reduce-scatter.13.cloned.1.call-update) | async-done | bytes 524304 | tf_op jit(solution)/shard_map/reduce_scatter | solution.py:34
  247.3 7.8 all-reduce.8
  256.6 6.3 psum.193
  263.8 30.3 %all-gather.19.cloned.1.call-done = bf16[2,512,512]{2,1,0:T(8,128)(2,1)} async-done(((bf16[2,128,512]{2,1,0:T(8,128)(2,1)}), bf16[2,512,512]{2,1,0:T(8,128)(2,1)}) %all-gather.19.cloned.1.call-update) | async-done | bytes 1048592 | tf_op jit(solution)/shard_map/all_gather | solution.py:24
  294.0 12.8 fusion.63
  307.1 153.4 %reduce-scatter.15.cloned.1.call-done = f32[2,128,4096]{2,1,0:T(8,128)} async-done(((f32[2,512,4096]{2,1,0:T(8,128)}), f32[2,128,4096]{2,1,0:T(8,128)}) %reduce-scatter.15.cloned.1.call-update) | async-done | bytes 4194320 | tf_op jit(solution)/shard_map/reduce_scatter | solution.py:29
  464.5 52.8 %all-gather.21.cloned.1.call-done = bf16[2,512,2048]{2,1,0:T(8,128)(2,1)} async-done(((bf16[2,128,2048]{2,1,0:T(8,128)(2,1)}), bf16[2,512,2048]{2,1,0:T(8,128)(2,1)}) %all-gather.21.cloned.1.call-update) | async-done | bytes 4194320 | tf_op jit(solution)/shard_map/all_gather | solution.py:33
  517.3 5.8 fusion.73
  523.2 43.8 %reduce-scatter.17.cloned.1.call-done = f32[2,128,512]{2,1,0:T(8,128)} async-done(((f32[2,512,512]{2,1,0:T(8,128)}), f32[2,128,512]{2,1,0:T(8,128)}) %reduce-scatter.17.cloned.1.call-update) | async-done | bytes 524304 | tf_op jit(solution)/shard_map/reduce_scatter | solution.py:34
  568.8 8.5 psum.194
  582.4 42.3 %all-reduce.15.cloned.1.call-done = f32[2,128,256]{2,1,0:T(8,128)} async-done(((f32[2,128,256]{2,1,0:T(8,128)}), f32[2,128,256]{2,1,0:T(8,128)}) %all-reduce.15.cloned.1.call-update) | async-done | bytes 262160 | tf_op jit(solution)/shard_map/psum | solution.py:20
  627.3 7.0 psum.196
  636.3 6.7 psum.197
  647.0 47.2 %all-reduce.17.cloned.1.call-done = f32[2,128,256]{2,1,0:T(8,128)} async-done(((f32[2,128,256]{2,1,0:T(8,128)}), f32[2,128,256]{2,1,0:T(8,128)}) %all-reduce.17.cloned.1.call-update) | async-done | bytes 262160 | tf_op jit(solution)/shard_map/psum | solution.py:20
  698.3 7.6 psum.199
  709.1 30.3 %all-gather.23.cloned.1.call-done = bf16[2,512,512]{2,1,0:T(8,128)(2,1)} async-done(((bf16[2,128,512]{2,1,0:T(8,128)(2,1)}), bf16[2,512,512]{2,1,0:T(8,128)(2,1)}) %all-gather.23.cloned.1.call-update) | async-done | bytes 1048592 | tf_op jit(solution)/shard_map/all_gather | solution.py:24
  739.4 6.9 fusion.71
  746.3 86.1 %reduce-scatter.19.cloned.1.call-done = f32[2,128,2048]{2,1,0:T(8,128)} async-done(((f32[2,512,2048]{2,1,0:T(8,128)}), f32[2,128,2048]{2,1,0:T(8,128)}) %reduce-scatter.19.cloned.1.call-update) | async-done | bytes 2097168 | tf_op jit(solution)/shard_map/reduce_scatter | solution.py:29
  837.7 87.8 %all-gather.25.cloned.1.call-done = bf16[2,512,4096]{2,1,0:T(8,128)(2,1)} async-done(((bf16[2,128,4096]{2,1,0:T(8,128)(2,1)}), bf16[2,512,4096]{2,1,0:T(8,128)(2,1)}) %all-gather.25.cloned.1.call-update) | async-done | bytes 8388624 | tf_op jit(solution)/shard_map/all_gather | solution.py:33
  925.5 9.8 fusion.62
  936.0 43.2 %reduce-scatter.21.cloned.1.call-done = f32[2,128,512]{2,1,0:T(8,128)} async-done(((f32[2,512,512]{2,1,0:T(8,128)}), f32[2,128,512]{2,1,0:T(8,128)}) %reduce-scatter.21.cloned.1.call-update) | async-done | bytes 524304 | tf_op jit(solution)/shard_map/reduce_scatter | solution.py:34
  981.1 7.8 psum.200
  991.1 6.4 psum.202
  997.9 13.7 all-reduce.7
  1012.5 33.7 %all-gather.27.cloned.1.call-done = bf16[2,512,512]{2,1,0:T(8,128)(2,1)} async-done(((bf16[2,128,512]{2,1,0:T(8,128)(2,1)}), bf16[2,512,512]{2,1,0:T(8,128)(2,1)}) %all-gather.27.cloned.1.call-update) | async-done | bytes 1048592 | tf_op jit(solution)/shard_map/all_gather | solution.py:24
  1049.6 35.1 %reduce-scatter.23.cloned.1.call-done = f32[2,128,512]{2,1,0:T(8,128)} async-done(((f32[2,512,512]{2,1,0:T(8,128)}), f32[2,128,512]{2,1,0:T(8,128)}) %reduce-scatter.23.cloned.1.call-update) | async-done | bytes 524304 | tf_op jit(solution)/shard_map/reduce_scatter | solution.py:29
  1093.6 13.1 while.53
  1108.9 39.2 %reduce-scatter.25.cloned.1.call-done = f32[2,128,256]{2,1,0:T(8,128)} async-done(((f32[2,1024,256]{2,1,0:T(8,128)}), f32[2,128,256]{2,1,0:T(8,128)}) %reduce-scatter.25.cloned.1.call-update) | async-done | bytes 262160 | tf_op jit(solution)/shard_map/reduce_scatter | solution.py:328
  1150.3 43.1 %reduce-scatter.27.cloned.1.call-done = f32[2,128,256]{2,1,0:T(8,128)} async-done(((f32[2,1024,256]{2,1,0:T(8,128)}), f32[2,128,256]{2,1,0:T(8,128)}) %reduce-scatter.27.cloned.1.call-update) | async-done | bytes 262160 | tf_op jit(solution)/shard_map/reduce_scatter | solution.py:329
  1195.6 5.2 collective-permute-done.3
  1203.8 32.0 %all-gather.29.cloned.1.call-done = bf16[2,512,768]{2,1,0:T(8,128)(2,1)} async-done(((bf16[2,128,768]{2,1,0:T(8,128)(2,1)}), bf16[2,512,768]{2,1,0:T(8,128)(2,1)}) %all-gather.29.cloned.1.call-update) | async-done | bytes 1572880 | tf_op jit(solution)/shard_map/all_gather | solution.py:33
  1240.8 6.6 convolution_bitcast_fusion.10
  1247.4 10.3 convolution_bitcast_fusion.9
  1262.5 39.7 %pmax.7 = f32[8]{0:T(128)S(1)} all-reduce(f32[8]{0:T(128)S(1)} %dynamic_update_slice.9), channel_id=1, replica_groups=mesh['seq'=2,'row'=4,'col'=4] {'seq','row','col'}, use_global_device_ids=true, to_apply=%region_79.80 | all-reduce | flops 8 | bytes 64 | tf_op jit(solution)/shard_map/pmax | solution.py:229
  1308.6 7.6 all-reduce.6
  1316.3 31.7 %all-reduce.4 = (f32[6,512]{1,0:T(8,128)}, f32[2,256]{1,0:T(2,128)}) all-reduce(f32[6,512]{1,0:T(8,128)S(1)} %stack.39, f32[2,256]{1,0:T(2,128)S(1)} %get-tuple-element.748), channel_id=1, replica_groups=mesh['seq'=2,'row'=4,'col'=4] {'seq','col'}, use_global_device_ids=true, to_apply=%region_73.74 | all-reduce | flops 3584 | bytes 28672 | tf_op jit(solution)/shard_map/psum | solution.py:355
  1353.0 8.1 fusion.156
  1361.1 44.1 %all-reduce.19.cloned.1.call-done = (f32[512,64]{0,1:T(8,128)}, f32[64,512]{1,0:T(8,128)}, f32[512,256]{1,0:T(8,128)}, f32[256,512]{1,0:T(8,128)}) async-done(((f32[512,64]{0,1:T(8,128)}, f32[64,512]{1,0:T(8,128)}, f32[512,256]{1,0:T(8,128)}, f32[256,512]{1,0:T(8,128)}), (f32[512,64]{0,1:T(8,128)}, f32[64,512]{1,0:T(8,128)}, f32[512,256]{1,0:T(8,128)}, f32[256,512]{1,0:T(8,128)})) %all-reduce.19.cloned.1.call-update) | async-done | bytes 1310736 | tf_op jit(solution)/shard_map/psum | solution.py:355
  1406.1 4.8 copy.230
  (470 shorter events, 156.3 us)
Async XLA Ops:
  7.2 510.1 %copy-start = (bf16[2048,512]{1,0:T(8,128)(2,1)S(1)}, bf16[2048,512]{1,0:T(8,128)(2,1)}, u32[]{:S(2)}) copy-start(bf16[2048,512]{1,0:T(8,128)(2,1)} %param.34) | copy-start | bytes 6291460
  7.2 42.6 %all-gather.11.cloned.1.call-start = ((), (), s32[]{:S(2)}) async-start(), calls=%async_computation.10 | async-start | bytes 1310720 | tf_op jit(solution)/shard_map/all_gather | solution.py:24
  20.5 86.4 %reduce-scatter.11.cloned.1.call-start = ((), (), s32[]{:S(2)}) async-start(), calls=%async_computation.11 | async-start | bytes 5242880 | tf_op jit(solution)/shard_map/reduce_scatter | solution.py:29
  20.5 4.1 collective-permute-start
  21.9 4.1 collective-permute-start.1
  54.3 81.0 %all-gather.15.cloned.1.call-start = ((), (), s32[]{:S(2)}) async-start(), calls=%async_computation.13 | async-start | bytes 1179648 | tf_op jit(solution)/shard_map/all_gather | solution.py:179
  55.9 55.6 %copy-start.79 = (f32[1,256]{1,0:T(1,128)}, f32[1,256]{1,0:T(1,128)S(1)}, u32[]{:S(2)}) copy-start(f32[1,256]{1,0:T(1,128)S(1)} %get-tuple-element.797) | copy-start | bytes 3076
  56.4 55.1 %copy-start.27 = (f32[2,128,128]{2,1,0:T(8,128)}, f32[2,128,128]{2,1,0:T(8,128)S(1)}, u32[]{:S(2)}) copy-start(f32[2,128,128]{2,1,0:T(8,128)S(1)} %get-tuple-element.798) | copy-start | bytes 393220
  56.4 55.1 %copy-start.29 = (f32[2,128,128]{2,1,0:T(8,128)}, f32[2,128,128]{2,1,0:T(8,128)S(1)}, u32[]{:S(2)}) copy-start(f32[2,128,128]{2,1,0:T(8,128)S(1)} %get-tuple-element.799) | copy-start | bytes 393220
  111.3 50.1 %all-gather.13.cloned.1.call-start = ((), (), s32[]{:S(2)}) async-start(), calls=%async_computation.12 | async-start | bytes 1179648 | tf_op jit(solution)/shard_map/all_gather | solution.py:180
  115.8 83.1 %all-gather.17.cloned.1.call-start = ((), (), s32[]{:S(2)}) async-start(), calls=%async_computation.14 | async-start | bytes 1310720 | tf_op jit(solution)/shard_map/all_gather | solution.py:33
  172.6 73.5 %reduce-scatter.13.cloned.1.call-start = ((), (), s32[]{:S(2)}) async-start(), calls=%async_computation.15 | async-start | bytes 2621440 | tf_op jit(solution)/shard_map/reduce_scatter | solution.py:34
  202.2 52.9 %copy-start.62 = (f32[2,128]{1,0:T(2,128)S(1)}, f32[2,128]{1,0:T(2,128)}, u32[]{:S(2)}) copy-start(f32[2,128]{1,0:T(2,128)} %copy-done.61) | copy-start | bytes 3076
  202.2 52.9 %copy-start.66 = (f32[1,512]{1,0:T(1,128)S(1)}, f32[1,512]{1,0:T(1,128)}, u32[]{:S(2)}) copy-start(f32[1,512]{1,0:T(1,128)} %get-tuple-element.791) | copy-start | bytes 6148
  202.2 52.9 %copy-start.68 = (f32[1,512]{1,0:T(1,128)S(1)}, f32[1,512]{1,0:T(1,128)}, u32[]{:S(2)}) copy-start(f32[1,512]{1,0:T(1,128)} %get-tuple-element.790) | copy-start | bytes 6148
  202.2 60.6 %copy-start.59 = (f32[1,512]{1,0:T(1,128)S(1)}, f32[1,512]{1,0:T(1,128)}, u32[]{:S(2)}) copy-start(f32[1,512]{1,0:T(1,128)} %get-tuple-element.789) | copy-start | bytes 6148
  202.2 91.8 %all-gather.19.cloned.1.call-start = ((), (), s32[]{:S(2)}) async-start(), calls=%async_computation.16 | async-start | bytes 1310720 | tf_op jit(solution)/shard_map/all_gather | solution.py:24
  215.3 91.5 %copy-start.45 = (bf16[2,128,64]{1,2,0:T(8,128)(2,1)}, bf16[2,128,64]{1,2,0:T(8,128)(2,1)S(1)}, u32[]{:S(2)}) copy-start(bf16[2,128,64]{1,2,0:T(8,128)(2,1)S(1)} %psum.191) | copy-start | bytes 98308
  263.7 196.8 %reduce-scatter.15.cloned.1.call-start = ((), (), s32[]{:S(2)}) async-start(), calls=%async_computation.17 | async-start | bytes 20971520 | tf_op jit(solution)/shard_map/reduce_scatter | solution.py:29
  306.9 210.4 %all-gather.21.cloned.1.call-start = ((), (), s32[]{:S(2)}) async-start(), calls=%async_computation.18 | async-start | bytes 5242880 | tf_op jit(solution)/shard_map/all_gather | solution.py:33
  464.4 102.6 %reduce-scatter.17.cloned.1.call-start = ((), (), s32[]{:S(2)}) async-start(), calls=%async_computation.19 | async-start | bytes 2621440 | tf_op jit(solution)/shard_map/reduce_scatter | solution.py:34
  523.2 101.5 %copy-start.43 = (bf16[2,128,256]{2,1,0:T(8,128)(2,1)S(1)}, bf16[2,128,256]{2,1,0:T(8,128)(2,1)}, u32[]{:S(2)}) copy-start(bf16[2,128,256]{2,1,0:T(8,128)(2,1)} %param.26) | copy-start | bytes 393220
  523.2 101.5 %all-reduce.15.cloned.1.call-start = ((), (), s32[]{:S(2)}) async-start(), calls=%async_computation.20 | async-start | bytes 524288 | tf_op jit(solution)/shard_map/psum | solution.py:20
  582.3 111.8 %all-reduce.17.cloned.1.call-start = ((), (), s32[]{:S(2)}) async-start(), calls=%async_computation.21 | async-start | bytes 524288 | tf_op jit(solution)/shard_map/psum | solution.py:20
  646.9 92.5 %all-gather.23.cloned.1.call-start = ((), (), s32[]{:S(2)}) async-start(), calls=%async_computation.22 | async-start | bytes 1310720 | tf_op jit(solution)/shard_map/all_gather | solution.py:24
  709.0 123.5 %reduce-scatter.19.cloned.1.call-start = ((), (), s32[]{:S(2)}) async-start(), calls=%async_computation.23 | async-start | bytes 10485760 | tf_op jit(solution)/shard_map/reduce_scatter | solution.py:29
  746.3 179.2 %all-gather.25.cloned.1.call-start = ((), (), s32[]{:S(2)}) async-start(), calls=%async_computation.24 | async-start | bytes 10485760 | tf_op jit(solution)/shard_map/all_gather | solution.py:33
  837.6 87.8 %copy-start.102 = (bf16[512,2048]{1,0:T(8,128)(2,1)S(1)}, bf16[512,2048]{1,0:T(8,128)(2,1)}, u32[]{:S(2)}) copy-start(bf16[512,2048]{1,0:T(8,128)(2,1)} %param.33) | copy-start | bytes 6291460
  837.7 141.6 %reduce-scatter.21.cloned.1.call-start = ((), (), s32[]{:S(2)}) async-start(), calls=%async_computation.25 | async-start | bytes 2621440 | tf_op jit(solution)/shard_map/reduce_scatter | solution.py:34
  935.3 53.6 %copy-start.9 = (f32[2,128,512]{2,1,0:T(8,128)S(1)}, f32[2,128,512]{2,1,0:T(8,128)}, u32[]{:S(2)}) copy-start(f32[2,128,512]{2,1,0:T(8,128)} %reduce-scatter.13.cloned.1.call-done) | copy-start | bytes 1572868
  935.3 53.6 %copy-start.11 = (f32[2,128,512]{2,1,0:T(8,128)S(1)}, f32[2,128,512]{2,1,0:T(8,128)}, u32[]{:S(2)}) copy-start(f32[2,128,512]{2,1,0:T(8,128)} %get-tuple-element.806) | copy-start | bytes 1572868
  935.3 53.6 %copy-start.71 = (f32[2,128]{1,0:T(2,128)S(1)}, f32[2,128]{1,0:T(2,128)}, u32[]{:S(2)}) copy-start(f32[2,128]{1,0:T(2,128)} %copy-done.70) | copy-start | bytes 3076
  935.3 53.5 %copy-start.73 = (f32[2,128]{1,0:T(2,128)S(1)}, f32[2,128]{1,0:T(2,128)}, u32[]{:S(2)}) copy-start(f32[2,128]{1,0:T(2,128)} %copy-done.72) | copy-start | bytes 3076
  935.4 110.8 %all-gather.27.cloned.1.call-start = ((), (), s32[]{:S(2)}) async-start(), calls=%async_computation.26 | async-start | bytes 1310720 | tf_op jit(solution)/shard_map/all_gather | solution.py:24
  991.1 55.1 %copy-start.5 = (f32[2,128,512]{2,1,0:T(8,128)}, f32[2,128,512]{2,1,0:T(8,128)S(1)}, u32[]{:S(2)}) copy-start(f32[2,128,512]{2,1,0:T(8,128)S(1)} %get-tuple-element.760) | copy-start | bytes 1572868
  991.1 55.1 %copy-start.26 = (bf16[512,512]{1,0:T(8,128)(2,1)S(1)}, bf16[512,512]{1,0:T(8,128)(2,1)}, u32[]{:S(2)}) copy-start(bf16[512,512]{1,0:T(8,128)(2,1)} %param.31) | copy-start | bytes 1572868
  1012.5 72.2 %reduce-scatter.23.cloned.1.call-start = ((), (), s32[]{:S(2)}) async-start(), calls=%async_computation.27 | async-start | bytes 2621440 | tf_op jit(solution)/shard_map/reduce_scatter | solution.py:29
  1049.5 98.5 %reduce-scatter.25.cloned.1.call-start = ((), (), s32[]{:S(2)}) async-start(), calls=%async_computation.28 | async-start | bytes 2359296 | tf_op jit(solution)/shard_map/reduce_scatter | solution.py:328
  1106.7 86.6 %reduce-scatter.27.cloned.1.call-start = ((), (), s32[]{:S(2)}) async-start(), calls=%async_computation.29 | async-start | bytes 2359296 | tf_op jit(solution)/shard_map/reduce_scatter | solution.py:329
  1107.3 128.4 %all-gather.29.cloned.1.call-start = ((), (), s32[]{:S(2)}) async-start(), calls=%async_computation.30 | async-start | bytes 1966080 | tf_op jit(solution)/shard_map/all_gather | solution.py:33
  1108.1 86.5 %copy-start.30 = (f32[2,128,128]{2,1,0:T(8,128)S(1)}, f32[2,128,128]{2,1,0:T(8,128)}, u32[]{:S(2)}) copy-start(f32[2,128,128]{2,1,0:T(8,128)} %copy-done.29) | copy-start | bytes 393220
  1108.9 91.9 %copy-start.12 = (f32[2,128,1024]{2,1,0:T(8,128)S(1)}, f32[2,128,1024]{2,1,0:T(8,128)}, u32[]{:S(2)}) copy-start(f32[2,128,1024]{2,1,0:T(8,128)} %reduce-scatter.11.cloned.1.call-done) | copy-start | bytes 3145732
  1108.9 91.9 %copy-start.28 = (f32[2,128,128]{2,1,0:T(8,128)S(1)}, f32[2,128,128]{2,1,0:T(8,128)}, u32[]{:S(2)}) copy-start(f32[2,128,128]{2,1,0:T(8,128)} %copy-done.27) | copy-start | bytes 393220
  1148.0 46.5 %collective-permute-start.2 = (f32[2,128,256]{2,1,0:T(8,128)}, f32[2,128,256]{2,1,0:T(8,128)S(1)}, u32[]{:S(2)}, u32[]{:S(2)}) collective-permute-start(f32[2,128,256]{2,1,0:T(8,128)} %reduce-scatter.25.cloned.1.call-done), channel_id=1, source_target_pairs={{0,1},{1,0},{2,3},{3,2},{4,5},{5,4},{6,7},{7,6},{8,9},{9,8},{10,11... | collective-permute-start | bytes 786440 | tf_op jit(solution)/shard_map/ppermute | solution.py:16
  1193.4 7.4 collective-permute-start.3
  1203.7 103.1 %reduce-scatter.29.cloned.1.call-start = ((), (), s32[]{:S(2)}) async-start(), calls=%async_computation.31 | async-start | bytes 2621440 | tf_op jit(solution)/shard_map/reduce_scatter | solution.py:34
  1239.6 109.3 %all-reduce.21.cloned.1.call-start = ((), (), s32[]{:S(2)}) async-start(), calls=%async_computation.33 | async-start | bytes 30408704 | tf_op jit(solution)/shard_map/psum | solution.py:352
  1261.8 143.4 %all-reduce.19.cloned.1.call-start = ((), (), s32[]{:S(2)}) async-start(), calls=%async_computation.32 | async-start | bytes 2621440 | tf_op jit(solution)/shard_map/psum | solution.py:355
  (86 other events, 1547.2 us)
Sparse Core Ops, SparseCore 0:
  20.6 29.1 all-gather.10
  54.5 52.3 reduce-scatter.10
  111.4 23.8 all-gather.14
  137.9 23.4 all-gather.12
  172.7 26.1 all-gather.16
  202.4 43.6 reduce-scatter.12
  263.9 30.1 all-gather.18
  307.0 153.4 reduce-scatter.14
  464.5 52.7 all-gather.20
  523.3 43.7 reduce-scatter.16
  582.4 42.1 all-reduce.14
  647.0 47.0 all-reduce.16
  709.1 30.2 all-gather.22
  746.4 86.0 reduce-scatter.18
  837.8 87.6 all-gather.24
  935.5 43.7 reduce-scatter.20
  1012.6 33.5 all-gather.26
  1049.9 34.8 reduce-scatter.22
  1106.8 41.1 reduce-scatter.24
  1152.1 41.2 reduce-scatter.26
  1203.9 31.8 all-gather.28
  1239.7 43.8 reduce-scatter.28
  1287.8 54.6 all-reduce.20
  1345.8 59.3 all-reduce.18
where the time goes:
time: 1430 us; the launch traced here: 1420 us
  waiting for transfers between devices  1010 us (71%)
  blocking collectives  172 us (12%)
  matrix products  107 us (7%)
  other arithmetic  57.9 us (4%)
  local copies, waits for them, and re-layouts  42.3 us (3%)
  between operations  16.1 us (1%)
    reduce_scatter x4, waiting for transfers between devices, spread_rows(): lax.psum_scatter(project(gathered), 'row', scatter_dimension=1, tiled=True)  325 us
    all_gather x4, waiting for transfers between devices, spread_cols(): gathered = lax.all_gather(values, 'row', axis=1, tiled=True)  199 us
    reduce_scatter x4, waiting for transfers between devices, spread_cols(): lax.psum_scatter(project(gathered), 'col', scatter_dimension=1, tiled=True)  118 us
    all_gather x4, waiting for transfers between devices, gather_tokens(): return lax.all_gather(values, 'col', axis=1, tiled=True)  117 us
    psum x12, blocking collectives, width_total(): return lax.psum(values, 'row')  101 us
    psum x2, waiting for transfers between devices, width_total(): return lax.psum(values, 'row')  89.5 us
    psum x1, waiting for transfers between devices, body(): lax.psum((grad_laurel_left, grad_laurel_right, grad_per_gate, grad_per_pr...  44.1 us
    reduce_scatter x1, waiting for transfers between devices, body(): lax.psum_scatter(d_values, ('seq', 'row'), scatter_dimension=1, tiled=True)  43.1 us
  transfers between devices with their start and end apart: 28, of which 25 were waited for; matrix products, arithmetic and copies ran while one was open for 5% of the time, Pallas kernels for 0%

commit v1 on v0

--- a/solution.py
+++ b/solution.py
@@ -1,6 +1,10 @@
+import functools
+
 import jax
 import jax.numpy as jnp
 from jax import lax
+from jax.experimental import pallas as pl
+from jax.experimental.pallas import tpu as pltpu
 from jax.sharding import PartitionSpec as P
 
 EPSILON = 1e-06
@@ -8,6 +12,9 @@
 ROPE_BASE = 1000000.0
 ROOT_HALF = 0.7071067811865476
 MASK_FILL = -1e30
+MESH = pl.DeviceIdType.MESH
+BF = jnp.bfloat16
+F32 = jnp.float32
 
 
 def swapped(value, axis, apart):
@@ -82,7 +89,8 @@
 
 
 def doc_places(doc_lengths, first_place, place_count):
-    doc_ends = jnp.cumsum(doc_lengths, axis=1)
+    upto = jnp.tril(jnp.ones((doc_lengths.shape[1], doc_lengths.shape[1]), jnp.int32))
+    doc_ends = jnp.sum(doc_lengths[:, None, :] * upto[None], axis=2)
     places = first_place + jnp.arange(place_count, dtype=jnp.int32)
     before = (doc_ends[:, None, :] <= places[None, :, None]).astype(jnp.int32)
     segment = jnp.sum(before, axis=2)
@@ -101,7 +109,7 @@
     return (scores, allowed)
 
 
-def body(
+def body_any(
     layer_in,
     per_layer_in,
     doc_lengths,
@@ -390,7 +398,1023 @@
     )
 
 
+def group_gather(values):
+    return lax.all_gather(values, ("seq", "col"), axis=0, tiled=True)
+
+
+def group_scatter(partial):
+    return lax.psum_scatter(
+        partial.astype(jnp.bfloat16), ("seq", "col"), scatter_dimension=0, tiled=True
+    ).astype(jnp.float32)
+
+
+def to_owner(values):
+    seq_count, tokens, width = values.shape
+    rows = lax.axis_size("row")
+    parts = values.reshape(rows, seq_count * tokens // rows, width)
+    moved = lax.all_to_all(parts, "row", split_axis=0, concat_axis=0)
+    return moved.transpose(1, 0, 2).reshape(parts.shape[1], rows * width)
+
+
+def from_owner(values, seq_count):
+    tokens, width = values.shape
+    rows = lax.axis_size("row")
+    parts = values.reshape(tokens, rows, width // rows).transpose(1, 0, 2)
+    moved = lax.all_to_all(parts, "row", split_axis=0, concat_axis=0)
+    return moved.reshape(seq_count, rows * tokens // seq_count, width // rows)
+
+
+def mm(left_side, right_side):
+    return jnp.dot(left_side, right_side, preferred_element_type=jnp.float32)
+
+
+def mm_nt(left_side, right_side):
+    return lax.dot_general(
+        left_side, right_side, (((1,), (1,)), ((), ())), preferred_element_type=jnp.float32
+    )
+
+
+def mm_tn(left_side, right_side):
+    return lax.dot_general(
+        left_side, right_side, (((0,), (0,)), ((), ())), preferred_element_type=jnp.float32
+    )
+
+
+def rms(values):
+    factor = lax.rsqrt(jnp.mean(values * values, axis=-1, keepdims=True) + EPSILON)
+    return values * factor, factor
+
+
+def rms_back(grad_values, normed, factor, gain_vec):
+    grad_normed = grad_values * gain_vec
+    inner = jnp.mean(grad_normed * normed, axis=-1, keepdims=True)
+    return (
+        factor * (grad_normed - normed * inner),
+        jnp.sum(grad_values * normed, axis=0, keepdims=True),
+    )
+
+
+def gather_rows(values, axis):
+    return lax.all_gather(values, "row", axis=axis, tiled=True)
+
+
+def scatter_rows(values, axis):
+    return lax.psum_scatter(
+        values.astype(jnp.bfloat16), "row", scatter_dimension=axis, tiled=True
+    ).astype(jnp.float32)
+
+
+def both_cores(values, axis):
+    return lax.all_gather(values, "seq", axis=axis, tiled=True)
+
+
+def remote(src, dst, send_sem, recv_sem, device):
+    return pltpu.make_async_remote_copy(
+        src_ref=src,
+        dst_ref=dst,
+        send_sem=send_sem,
+        recv_sem=recv_sem,
+        device_id=device,
+        device_id_type=MESH,
+    )
+
+
+def greet(core, row, col):
+    barrier = pltpu.get_barrier_semaphore()
+    near = [(core, row ^ 1, col), (core, row ^ 2, col), (core, row ^ 3, col), (1 - core, row, col)]
+    for device in near:
+        pl.semaphore_signal(barrier, inc=1, device_id=device, device_id_type=MESH)
+
+    @pl.when(col > 0)
+    def _():
+        pl.semaphore_signal(barrier, inc=1, device_id=(core, row, col - 1), device_id_type=MESH)
+
+    @pl.when(col < 3)
+    def _():
+        pl.semaphore_signal(barrier, inc=1, device_id=(core, row, col + 1), device_id_type=MESH)
+
+    ends = jnp.where((col == 0) | (col == 3), 1, 2)
+    pl.semaphore_wait(barrier, 4 + ends)
+
+
+class Gather:
+    def __init__(self, place, buf, rows, sems):
+        self.core, self.row, self.col = place
+        self.buf, self.rows = buf, rows
+        self.send_z, self.recv_z, self.send_s, self.recv_s = sems
+
+    def part(self, core, col):
+        return self.buf.at[pl.ds(pl.multiple_of((core * 4 + col) * self.rows, self.rows), self.rows)]
+
+    def to_right(self, dist):
+        part = self.part(self.core, self.col - dist)
+        return remote(
+            part, part, self.send_z.at[dist], self.recv_z.at[dist], (self.core, self.row, self.col + 1)
+        )
+
+    def to_left(self, dist):
+        part = self.part(self.core, self.col + dist)
+        return remote(
+            part,
+            part,
+            self.send_z.at[3 + dist],
+            self.recv_z.at[3 + dist],
+            (self.core, self.row, self.col - 1),
+        )
+
+    def to_sibling(self, col):
+        part = self.part(self.core, col)
+        return remote(
+            part, part, self.send_s.at[col], self.recv_s.at[col], (1 - self.core, self.row, self.col)
+        )
+
+    def start(self):
+        col = self.col
+
+        @pl.when(col < 3)
+        def _():
+            self.to_right(0).start()
+
+        @pl.when(col > 0)
+        def _():
+            self.to_left(0).start()
+
+        self.to_sibling(col).start()
+
+    def forward(self):
+        col = self.col
+        for dist in (1, 2, 3):
+
+            @pl.when(col >= dist)
+            def _():
+                part = self.part(self.core, col - dist)
+                remote(
+                    part, part, self.send_z.at[0], self.recv_z.at[dist - 1], (self.core, self.row, col)
+                ).wait_recv()
+
+                @pl.when(col < 3)
+                def _():
+                    if dist < 3:
+                        self.to_right(dist).start()
+
+                self.to_sibling(col - dist).start()
+
+            @pl.when(col + dist <= 3)
+            def _():
+                part = self.part(self.core, col + dist)
+                remote(
+                    part,
+                    part,
+                    self.send_z.at[0],
+                    self.recv_z.at[3 + dist - 1],
+                    (self.core, self.row, col),
+                ).wait_recv()
+
+                @pl.when(col > 0)
+                def _():
+                    if dist < 3:
+                        self.to_left(dist).start()
+
+                self.to_sibling(col + dist).start()
+
+    def finish(self):
+        for col in range(4):
+            part = self.part(1 - self.core, col)
+            remote(
+                part, part, self.send_s.at[col], self.recv_s.at[col], (1 - self.core, self.row, self.col)
+            ).wait_recv()
+        for col in range(4):
+            self.to_sibling(col).wait_send()
+        for dist in (0, 1, 2):
+
+            @pl.when((self.col < 3) & (self.col >= dist))
+            def _():
+                self.to_right(dist).wait_send()
+
+            @pl.when((self.col > 0) & (self.col + dist <= 3))
+            def _():
+                self.to_left(dist).wait_send()
+
+
+class Scatter:
+    def __init__(self, place, rows, bufs, sems):
+        self.core, self.row, self.col = place
+        self.rows = rows
+        self.give, self.keep, self.got, self.sent, self.left, self.right = bufs
+        self.send_z, self.recv_z, self.send_s, self.recv_s = sems
+
+    def sibling(self):
+        return remote(
+            self.give,
+            self.got,
+            self.send_s.at[0],
+            self.recv_s.at[0],
+            (1 - self.core, self.row, self.col),
+        )
+
+    def mine(self, dest):
+        rows = pl.ds(dest * self.rows, self.rows)
+        return self.keep[rows] + self.got[rows].astype(F32)
+
+    def hop(self, dest, right):
+        step = 1 if right else -1
+        lane = 0 if right else 4
+        return remote(
+            self.sent.at[dest],
+            (self.left if right else self.right).at[dest],
+            self.send_z.at[lane + dest],
+            self.recv_z.at[lane + dest],
+            (self.core, self.row, self.col + step),
+        )
+
+    def chain(self, dest, right):
+        col = self.col
+        inner = (col > 0) if right else (col < 3)
+
+        @pl.when((col < dest) if right else (col > dest))
+        def _():
+            @pl.when(inner)
+            def _():
+                self.hop(dest, right).wait_recv()
+                came = (self.left if right else self.right)[dest].astype(F32)
+                self.sent[dest] = (self.mine(dest) + came).astype(BF)
+
+            @pl.when(jnp.logical_not(inner))
+            def _():
+                self.sent[dest] = self.mine(dest).astype(BF)
+
+            self.hop(dest, right).start()
+
+    def run(self, result):
+        col = self.col
+        self.sibling().wait_recv()
+        for dest in (3, 2, 1):
+            self.chain(dest, True)
+            self.chain(3 - dest, False)
+        own = pl.ds(pl.multiple_of(col * self.rows, self.rows), self.rows)
+        result[...] = self.keep[own] + self.got[own].astype(F32)
+        for dest in range(4):
+
+            @pl.when((col == dest) & (dest > 0))
+            def _():
+                self.hop(dest, True).wait_recv()
+                result[...] += self.left[dest].astype(F32)
+
+            @pl.when((col == dest) & (dest < 3))
+            def _():
+                self.hop(dest, False).wait_recv()
+                result[...] += self.right[dest].astype(F32)
+
+        self.sibling().wait_send()
+        for dest in range(4):
+
+            @pl.when(col < dest)
+            def _():
+                self.hop(dest, True).wait_send()
+
+            @pl.when(col > dest)
+            def _():
+                self.hop(dest, False).wait_send()
+
+
+class RowGather:
+    def __init__(self, place, source, block, halves, sems):
+        self.core, self.row, self.col = place
+        self.source, self.block, self.halves = source, block, halves
+        self.sems = sems
+
+    def neighbour(self, mask):
+        return (self.core, self.row ^ mask, self.col)
+
+    def own(self):
+        return pltpu.make_async_copy(self.source, self.block(self.row), self.sems.at[8])
+
+    def first(self, mask, block=None):
+        lane = mask - 1
+        return remote(
+            self.source,
+            self.block(self.row) if block is None else block,
+            self.sems.at[lane],
+            self.sems.at[4 + lane],
+            self.neighbour(mask),
+        )
+
+    def second(self, mask):
+        part = self.halves(self.row ^ (3 - mask))[mask - 1]
+        return remote(
+            part, part, self.sems.at[1 + mask], self.sems.at[5 + mask], self.neighbour(mask)
+        )
+
+    def start(self):
+        self.first(1).start()
+        self.first(2).start()
+        self.own().start()
+
+    def forward(self):
+        self.first(1, self.block(self.row ^ 1)).wait_recv()
+        self.second(2).start()
+        self.first(2, self.block(self.row ^ 2)).wait_recv()
+        self.second(1).start()
+
+    def finish(self):
+        for mask in (1, 2):
+            part = self.halves(self.row ^ 3)[mask - 1]
+            remote(
+                part, part, self.sems.at[1 + mask], self.sems.at[5 + mask], self.neighbour(mask)
+            ).wait_recv()
+        self.own().wait()
+        self.first(1).wait_send()
+        self.first(2).wait_send()
+        self.second(1).wait_send()
+        self.second(2).wait_send()
+
+
+def by_rows(buf, block_rows):
+    half = block_rows // 2
+
+    def block(index):
+        return buf.at[pl.ds(pl.multiple_of(index * block_rows, block_rows), block_rows)]
+
+    def halves(index):
+        return [
+            buf.at[pl.ds(pl.multiple_of(index * block_rows + part * half, half), half)]
+            for part in range(2)
+        ]
+
+    return block, halves
+
+
+def by_cols(buf, block_cols):
+    rows = buf.shape[0] // 2
+
+    def block(index):
+        return buf.at[:, pl.ds(pl.multiple_of(index * block_cols, block_cols), block_cols)]
+
+    def halves(index):
+        cols = pl.ds(pl.multiple_of(index * block_cols, block_cols), block_cols)
+        return [buf.at[pl.ds(part * rows, rows), cols] for part in range(2)]
+
+    return block, halves
+
+
+def gelu(values):
+    inner = 0.7978845608028654 * (values + 0.044715 * values * values * values)
+    return 0.5 * values * (1.0 + jnp.tanh(inner))
+
+
+def head_parts(raw, gain, cosine, sine):
+    factor = lax.rsqrt(jnp.mean(raw * raw, axis=1, keepdims=True) + EPSILON)
+    half = raw.shape[1] // 2
+    scaled = raw * factor * gain
+    first, second = scaled[:, :half], scaled[:, half:]
+    return jnp.concatenate([first * cosine - second * sine, second * cosine + first * sine], axis=1)
+
+
+def forward_kernel(
+    x_in,
+    gains_in,
+    w_query,
+    w_kv,
+    w_out,
+    w_gate,
+    w_up,
+    w_down,
+    small_in,
+    small_out,
+    cosine,
+    sine,
+    start,
+    head_gains,
+    x_own,
+    gains,
+    xg,
+    raw_q,
+    raw_kv,
+    q_low,
+    kv,
+    lse,
+    top,
+    o_low,
+    attn_val,
+    lr_low,
+    fg,
+    gate,
+    up,
+    hid,
+    ff_val,
+    wq_all,
+    wkv_all,
+    wo_all,
+    wg_all,
+    wu_all,
+    wd_all,
+    si_all,
+    so_all,
+    w_kv_pair,
+    gains_pad,
+    vq,
+    vkv,
+    vo,
+    vg,
+    vu,
+    vd,
+    vsi,
+    vso,
+    give,
+    keep,
+    got,
+    sent,
+    left,
+    right,
+    give2,
+    keep2,
+    got2,
+    sent2,
+    left2,
+    right2,
+    row_sems,
+    z_send,
+    z_recv,
+    s_send,
+    s_recv,
+    misc_send,
+    misc_recv,
+    out_sems,
+):
+    core, row, col = lax.axis_index("seq"), lax.axis_index("row"), lax.axis_index("col")
+    place = (core, row, col)
+    own_tokens, width = x_own.shape
+    block = x_in.shape[2]
+    head_dim = head_gains.shape[1]
+    tokens = xg.shape[0]
+    ff_part = gate.shape[1]
+    chunk = 2 * own_tokens
+    key_width = w_kv.shape[1]
+    half = row % 2
+    greet(core, row, col)
+
+    my_cols = pl.ds(pl.multiple_of(row * block, block), block)
+
+    def hand_over(mask):
+        return remote(
+            x_in.at[row ^ mask],
+            x_own.at[:, my_cols],
+            misc_send.at[mask],
+            misc_recv.at[mask],
+            (core, row ^ mask, col),
+        )
+
+    def hand_gains(mask):
+        return remote(
+            gains_pad,
+            gains.at[:, my_cols],
+            misc_send.at[3 + mask],
+            misc_recv.at[3 + mask],
+            (core, row ^ mask, col),
+        )
+
+    for mask in (3, 1, 2):
+        hand_over(mask).start()
+    gains_pad[pl.ds(0, 6)] = gains_in[...]
+    gains_pad[pl.ds(6, 2)] = jnp.zeros((2, block), F32)
+    for mask in (3, 1, 2):
+        hand_gains(mask).start()
+    x_own[:, my_cols] = x_in[row]
+    gains[:, my_cols] = gains_pad[...]
+
+    pair_cols = pl.ds(pl.multiple_of(col % 2 * key_width, key_width), key_width)
+    pair = remote(
+        w_kv, w_kv_pair.at[:, pair_cols], misc_send.at[7], misc_recv.at[7], (core, row, col ^ 1)
+    )
+    pair.start()
+    w_kv_pair[:, pair_cols] = w_kv[...]
+
+    def rows_of(array, source, buf, lane, split=by_rows, size=None):
+        block_of, halves_of = split(buf, size)
+        return RowGather(place, source, block_of, halves_of, row_sems.at[lane])
+
+    core_head = pl.ds(pl.multiple_of(core * head_dim, head_dim), head_dim)
+    core_ff = pl.ds(pl.multiple_of(core * ff_part, ff_part), ff_part)
+    get_q = rows_of(0, w_query.at[:, core_head], vq, 0, by_rows, block)
+    get_kv = rows_of(0, w_kv_pair, vkv, 1, by_rows, block)
+    get_o = rows_of(0, w_out.at[core_head], vo, 2, by_cols, block)
+    get_g = rows_of(0, w_gate.at[:, core_ff], vg, 3, by_rows, block)
+    get_u = rows_of(0, w_up.at[:, core_ff], vu, 4, by_rows, block)
+    get_d = rows_of(0, w_down.at[core_ff], vd, 5, by_cols, block)
+    get_si = rows_of(0, small_in, vsi, 6, by_rows, block)
+    get_so = rows_of(0, small_out, vso, 7, by_cols, block)
+    get_q.start()
+    pair.wait_recv()
+    get_kv.start()
+    get_o.start()
+
+    for mask in (1, 2, 3):
+        remote(
+            x_in.at[row],
+            x_own.at[:, pl.ds(pl.multiple_of((row ^ mask) * block, block), block)],
+            misc_send.at[mask],
+            misc_recv.at[mask],
+            (core, row, col),
+        ).wait_recv()
+        remote(
+            gains_pad,
+            gains.at[:, pl.ds(pl.multiple_of((row ^ mask) * block, block), block)],
+            misc_send.at[3 + mask],
+            misc_recv.at[3 + mask],
+            (core, row, col),
+        ).wait_recv()
+
+    def own_norm():
+        values = x_own[...].astype(F32)
+        factor = lax.rsqrt(jnp.mean(values * values, axis=1, keepdims=True) + EPSILON)
+        return values, values * factor * gains[pl.ds(0, 1)]
+
+    mine = pl.ds(pl.multiple_of((core * 4 + col) * own_tokens, own_tokens), own_tokens)
+    xg[mine] = own_norm()[1].astype(BF)
+    sems = lambda lane: (z_send.at[lane], z_recv.at[lane], s_send.at[lane], s_recv.at[lane])
+    gather_x = Gather(place, xg, own_tokens, sems(0))
+    gather_x.start()
+    get_q.forward()
+    get_kv.forward()
+    get_o.forward()
+    get_si.start()
+    get_so.start()
+    get_g.start()
+    gather_x.forward()
+    gather_x.finish()
+    get_q.finish()
+    get_kv.finish()
+
+    raw_q[...] = mm(xg[...], vq[...])
+    raw_kv[...] = mm(xg[...], vkv[...])
+    q_low[...] = head_parts(raw_q[...], head_gains[pl.ds(0, 1)], cosine[...], sine[...]).astype(BF)
+    is_key = core == 0
+    kv_here = head_parts(
+        raw_kv[...],
+        jnp.where(is_key, head_gains[pl.ds(1, 1)], 1.0),
+        jnp.where(is_key, cosine[...], 1.0),
+        jnp.where(is_key, sine[...], 0.0),
+    ).astype(BF)
+
+    def kv_part(kind, which):
+        return kv.at[kind, pl.ds(pl.multiple_of(which * tokens, tokens), tokens)]
+
+    kv[core, pl.ds(pl.multiple_of(half * tokens, tokens), tokens)] = kv_here
+    here = kv_part(core, half)
+    to_x = remote(here, here, misc_send.at[8], misc_recv.at[8], (core, row ^ 1, col))
+    to_s = remote(here, here, misc_send.at[9], misc_recv.at[9], (1 - core, row, col))
+    to_x.start()
+    to_s.start()
+    came = kv_part(core, half ^ 1)
+    remote(here, came, misc_send.at[8], misc_recv.at[8], (core, row, col)).wait_recv()
+    on_s = remote(came, came, misc_send.at[10], misc_recv.at[10], (1 - core, row, col))
+    on_s.start()
+    other = kv_part(1 - core, half)
+    remote(other, other, misc_send.at[9], misc_recv.at[9], (core, row, col)).wait_recv()
+    other_came = kv_part(1 - core, half ^ 1)
+    remote(other_came, other_came, misc_send.at[10], misc_recv.at[10], (core, row, col)).wait_recv()
+
+    q_rows = 128
+    key_token = lax.broadcasted_iota(jnp.int32, (1, 2 * tokens), 1)
+    in_half = key_token % tokens
+    key_place = in_half // own_tokens * chunk + key_token // tokens * own_tokens + in_half % own_tokens
+    top[...] = jnp.full(top.shape, MASK_FILL, F32)
+
+    def attend(step, carry):
+        first = pl.multiple_of(step * q_rows, q_rows)
+        rows = pl.ds(first, q_rows)
+        token = first + lax.broadcasted_iota(jnp.int32, (q_rows, 1), 0)
+        q_place = token // own_tokens * chunk + half * own_tokens + token % own_tokens
+        allowed = (key_place <= q_place) & (key_place >= start[rows])
+        scores = jnp.where(allowed, mm_nt(q_low[rows], kv[0]), MASK_FILL)
+        row_top = jnp.max(scores, axis=1, keepdims=True)
+        weights = jnp.exp(scores - row_top)
+        total = jnp.sum(weights, axis=1, keepdims=True)
+        probs = (weights * (1.0 / total)).astype(BF)
+        o_low[rows] = mm(probs, kv[1]).astype(BF)
+        lse[rows] = row_top + jnp.log(total)
+        top[...] = jnp.maximum(top[...], jnp.max(row_top))
+        return carry
+
+    lax.fori_loop(0, tokens // q_rows, attend, 0)
+    get_si.forward()
+    get_so.forward()
+    get_g.forward()
+    get_u.start()
+    get_o.finish()
+
+    away = pl.multiple_of((1 - core) * 4 * own_tokens, 4 * own_tokens)
+    home = pl.multiple_of(core * 4 * own_tokens, 4 * own_tokens)
+    scatter = Scatter(place, own_tokens, (give, keep, got, sent, left, right), sems(1))
+
+    def project(source, weights, target, first):
+        def step(index, carry):
+            cols = pl.ds(pl.multiple_of(index * block, block), block)
+            value = mm(source[pl.ds(first, 4 * own_tokens)], weights[:, cols])
+            target[:, cols] = value.astype(target.dtype)
+            return carry
+
+        lax.fori_loop(0, width // block, step, 0)
+
+    project(o_low, vo, give, away)
+    scatter.sibling().start()
+    project(o_low, vo, keep, home)
+    scatter.run(attn_val)
+
+    get_si.finish()
+    get_so.finish()
+    inputs, x_norm = own_norm()
+    attn_normed = rms(attn_val[...])[0]
+    rank = lr_low.shape[1]
+    lr_low[...] = mm(xg[mine], vsi[:, pl.ds(0, rank)]).astype(BF)
+    lo_normed = rms(mm(lr_low[...], vso[pl.ds(0, rank)]))[0]
+    h_two = (
+        inputs + attn_normed * gains[pl.ds(1, 1)] + (x_norm + lo_normed * gains[pl.ds(2, 1)])
+    ) * ROOT_HALF
+    fg[mine] = (rms(h_two)[0] * gains[pl.ds(3, 1)]).astype(BF)
+    gather_f = Gather(place, fg, own_tokens, sems(2))
+    gather_f.start()
+    get_u.forward()
+    get_d.start()
+    get_g.finish()
+    gather_f.forward()
+    gather_f.finish()
+    get_u.finish()
+
+    tile = 256
+
+    def units(index, carry):
+        cols = pl.ds(pl.multiple_of(index * tile, tile), tile)
+        gate_part = mm(fg[...], vg[:, cols])
+        gate[:, cols] = gate_part
+        up_part = mm(fg[...], vu[:, cols])
+        up[:, cols] = up_part
+        hid[:, cols] = (gelu(gate_part) * up_part).astype(BF)
+        return carry
+
+    lax.fori_loop(0, ff_part // tile, units, 0)
+    get_d.forward()
+    keep_weights = [
+        pltpu.make_async_copy(source, target, out_sems.at[lane])
+        for lane, (source, target) in enumerate(
+            [
+                (vq, wq_all),
+                (vkv, wkv_all),
+                (vo, wo_all),
+                (vg, wg_all),
+                (vu, wu_all),
+                (vd, wd_all),
+                (vsi, si_all),
+                (vso, so_all),
+            ]
+        )
+    ]
+    get_d.finish()
+    for copy in keep_weights:
+        copy.start()
+    scatter_ff = Scatter(place, own_tokens, (give2, keep2, got2, sent2, left2, right2), sems(3))
+    project(hid, vd, give2, away)
+    scatter_ff.sibling().start()
+    project(hid, vd, keep2, home)
+    scatter_ff.run(ff_val)
+
+    for mask in (1, 2, 3):
+        hand_over(mask).wait_send()
+        hand_gains(mask).wait_send()
+    pair.wait_send()
+    to_x.wait_send()
+    to_s.wait_send()
+    on_s.wait_send()
+    for copy in keep_weights:
+        copy.wait()
+
+
+def run_forward(x_in, gains_in, w_query, w_kv, w_out, w_gate, w_up, w_down, small_in, small_out, tables, head_gains):
+    cosine, sine, start = tables
+    block = x_in.shape[2]
+    own, width = x_in.shape[1], 4 * block
+    tokens, head_dim, ff_part = 8 * own, head_gains.shape[1], w_gate.shape[1] // 2
+    rank = small_in.shape[1] - small_out.shape[0]
+    vm = pl.BlockSpec(memory_space=pltpu.VMEM)
+    hbm = pl.BlockSpec(memory_space=pl.ANY)
+    shape = jax.ShapeDtypeStruct
+    weights = [
+        (width, head_dim),
+        (width, head_dim),
+        (head_dim, width),
+        (width, ff_part),
+        (width, ff_part),
+        (ff_part, width),
+        (width, small_in.shape[1]),
+        (small_out.shape[0], width),
+    ]
+    outs = [
+        shape((own, width), BF),
+        shape((8, width), F32),
+        shape((tokens, width), BF),
+        shape((tokens, head_dim), F32),
+        shape((tokens, head_dim), F32),
+        shape((tokens, head_dim), BF),
+        shape((2, 2 * tokens, head_dim), BF),
+        shape((tokens, 1), F32),
+        shape((8, 128), F32),
+        shape((tokens, head_dim), BF),
+        shape((own, width), F32),
+        shape((own, rank), BF),
+        shape((tokens, width), BF),
+        shape((tokens, ff_part), F32),
+        shape((tokens, ff_part), F32),
+        shape((tokens, ff_part), BF),
+        shape((own, width), F32),
+    ] + [shape(size, BF) for size in weights]
+    scatter_bufs = [
+        pltpu.VMEM((4 * own, width), BF),
+        pltpu.VMEM((4 * own, width), F32),
+        pltpu.VMEM((4 * own, width), BF),
+        pltpu.VMEM((4, own, width), BF),
+        pltpu.VMEM((4, own, width), BF),
+        pltpu.VMEM((4, own, width), BF),
+    ]
+    dma = pltpu.SemaphoreType.DMA
+    return pl.pallas_call(
+        forward_kernel,
+        out_shape=outs,
+        in_specs=[vm, vm, hbm, vm, hbm, hbm, hbm, hbm, hbm, hbm, vm, vm, vm, vm],
+        out_specs=[vm] * 17 + [hbm] * 8,
+        scratch_shapes=[pltpu.VMEM((block, head_dim), BF), pltpu.VMEM((8, block), F32)]
+        + [pltpu.VMEM(size, BF) for size in weights]
+        + scatter_bufs * 2
+        + [
+            dma((8, 10)),
+            dma((4, 8)),
+            dma((4, 8)),
+            dma((4, 4)),
+            dma((4, 4)),
+            dma((12,)),
+            dma((12,)),
+            dma((8,)),
+        ],
+        compiler_params=pltpu.CompilerParams(
+            collective_id=0, has_side_effects=True, vmem_limit_bytes=60 * 2**20
+        ),
+        cost_estimate=pl.CostEstimate(flops=2 * 10**10, bytes_accessed=5 * 10**7, transcendentals=10**6),
+    )(x_in, gains_in, w_query, w_kv, w_out, w_gate, w_up, w_down, small_in, small_out, cosine, sine, start, head_gains)
+
+
+def body_pair(
+    layer_in,
+    per_layer_in,
+    doc_lengths,
+    w_query,
+    w_key,
+    w_value,
+    w_out,
+    w_gate,
+    w_up,
+    w_down,
+    laurel_left,
+    laurel_right,
+    per_gate,
+    per_proj,
+    norm_gains,
+    head_gains,
+    out_grad,
+):
+    core, row, col = lax.axis_index("seq"), lax.axis_index("row"), lax.axis_index("col")
+    rows, cols, cores = lax.axis_size("row"), lax.axis_size("col"), lax.axis_size("seq")
+    seq_count = layer_in.shape[0]
+    head_dim = head_gains.shape[1]
+    key_width = w_key.shape[1]
+    ff_part = w_gate.shape[1] // cores
+    chunk = layer_in.shape[1]
+    halves = rows // seq_count
+    own_tokens = chunk // halves
+    group_tokens = own_tokens * cores * cols
+    even_col = col % 2 == 0
+
+    lengths = doc_lengths[row // halves]
+    count = doc_lengths.shape[1]
+    upto = jnp.tril(jnp.ones((count, count), jnp.int32))
+    doc_ends = jnp.sum(lengths[None, :] * upto, axis=1)
+
+    def places_of(half):
+        token = jnp.arange(group_tokens, dtype=jnp.int32)
+        place = token // own_tokens * chunk + half * own_tokens + token % own_tokens
+        before = (doc_ends[None, :] <= place[:, None]).astype(jnp.int32)
+        start = jnp.sum(before * lengths[None, :], axis=1)
+        return place, start
+
+    half = row % halves
+    place, start = places_of(half)
+    other_place, other_start = places_of(half ^ 1)
+    key_place = jnp.stack([place, other_place])[jnp.array([0, 1]) ^ half].reshape(-1)
+    allowed = (key_place[None, :] <= place[:, None]) & (key_place[None, :] >= start[:, None])
+    cosine_table, sine_table = rotation(place - start, head_dim)
+
+    w_kv = jnp.where(core == 0, w_key, w_value)
+    rank = laurel_left.shape[1]
+    small_in = jnp.concatenate(
+        [laurel_left, jnp.zeros((laurel_left.shape[0], rank), BF), per_gate], axis=1
+    )
+    small_out = jnp.concatenate([laurel_right, per_proj], axis=0)
+    (
+        x_own,
+        gains,
+        x_all,
+        raw_q,
+        raw_kv,
+        q_low,
+        kv,
+        lse,
+        top_tile,
+        o_low,
+        attn_val,
+        lr_low,
+        f_all,
+        gate_val,
+        up_val,
+        hid_low,
+        ff_val,
+        w_q,
+        w_kv_all,
+        w_o,
+        w_g,
+        w_u,
+        w_d,
+        small_in_all,
+        small_out_all,
+    ) = run_forward(
+        layer_in.reshape(rows, own_tokens, -1),
+        norm_gains,
+        w_query,
+        w_kv,
+        w_out,
+        w_gate,
+        w_up,
+        w_down,
+        small_in,
+        small_out,
+        (
+            cosine_table[:, : head_dim // 2],
+            sine_table[:, : head_dim // 2],
+            start[:, None],
+        ),
+        head_gains,
+    )
+    w_gu = jnp.concatenate([w_g, w_u], axis=1)
+    l_left, p_gate = small_in_all[:, :rank], small_in_all[:, 2 * rank :]
+    l_right, p_proj = small_out_all[:rank], small_out_all[rank:]
+    inputs = x_own.astype(jnp.float32)
+    grad_top = to_owner(out_grad).astype(jnp.float32)
+    per_input = per_layer_in.reshape(rows, own_tokens, -1)[row].astype(jnp.float32)
+    x_normed, x_factor = rms(inputs)
+    x_norm = x_normed * gains[0]
+    x_low = x_norm.astype(jnp.bfloat16)
+
+    def head_prep(raw_part, gain_vec):
+        return rotate(head_norm(raw_part, gain_vec), cosine_table, sine_table)
+
+    other_kv = swapped(raw_kv, "seq", 0)
+    raw_k = jnp.where(core == 0, raw_kv, other_kv)
+    raw_v = jnp.where(core == 0, other_kv, raw_kv)
+    other_w = swapped(w_kv_all, "seq", 0)
+    w_heads = jnp.concatenate(
+        [w_q, jnp.where(core == 0, w_kv_all, other_w), jnp.where(core == 0, other_w, w_kv_all)], axis=1
+    )
+    q_rot, query_back = jax.vjp(head_prep, raw_q, head_gains[0])
+    k_rot, key_back = jax.vjp(head_prep, raw_k, head_gains[1])
+    v_rot, value_back = jax.vjp(lambda part: head_norm(part, 1.0), raw_v)
+    keys, values = kv[0], kv[1]
+    scores = jnp.where(allowed, mm_nt(q_low, keys), MASK_FILL)
+    probs = jnp.exp(scores - lse)
+    probs_low = probs.astype(jnp.bfloat16)
+    attn_normed, attn_factor = rms(attn_val)
+    lo_normed, lo_factor = rms(mm(lr_low, l_right))
+    h_two = (inputs + attn_normed * gains[1] + (x_norm + lo_normed * gains[2])) * ROOT_HALF
+    f_normed, f_factor = rms(h_two)
+
+    def geglu(gate_part, up_part):
+        return jax.nn.gelu(gate_part, approximate=True) * up_part
+
+    hidden, geglu_back = jax.vjp(geglu, gate_val, up_val)
+    ff_normed, ff_factor = rms(ff_val)
+    h_three = h_two + ff_normed * gains[4]
+    h_low = h_three.astype(jnp.bfloat16)
+
+    def per_mix(gate_part):
+        return jax.nn.gelu(gate_part, approximate=True) * per_input
+
+    gp_val, per_back = jax.vjp(per_mix, mm(h_low, p_gate))
+    gp_low = gp_val.astype(jnp.bfloat16)
+    pp_normed, pp_factor = rms(mm(gp_low, p_proj))
+    layer_out = from_owner((h_three + pp_normed * gains[5]).astype(jnp.bfloat16), seq_count)
+
+    d_pp, gain_five = rms_back(grad_top, pp_normed, pp_factor, gains[5])
+    d_pp_low = d_pp.astype(jnp.bfloat16)
+    g_per_proj = mm_tn(gp_low, d_pp_low)
+    (d_pg,) = per_back(mm_nt(d_pp_low, p_proj))
+    d_pg_low = d_pg.astype(jnp.bfloat16)
+    g_per_gate = mm_tn(h_low, d_pg_low)
+    d_three = grad_top + mm_nt(d_pg_low, p_gate)
+    d_ff, gain_four = rms_back(d_three, ff_normed, ff_factor, gains[4])
+    d_ff_all = group_gather(d_ff.astype(jnp.bfloat16))
+    d_hidden = mm_nt(d_ff_all, w_d)
+    d_gate, d_up = geglu_back(d_hidden)
+    d_gu = jnp.concatenate([d_gate, d_up], axis=1).astype(jnp.bfloat16)
+    d_f = group_scatter(mm_nt(d_gu, w_gu))
+    g_down = both_cores(scatter_rows(mm_tn(hid_low, d_ff_all), 1), 0)
+    g_gu = scatter_rows(mm_tn(f_all, d_gu), 0)
+    g_gate, g_up = both_cores(g_gu[:, :ff_part], 1), both_cores(g_gu[:, ff_part:], 1)
+    d_f, gain_three = rms_back(d_f, f_normed, f_factor, gains[3])
+    d_half = (d_three + d_f) * ROOT_HALF
+    d_lo, gain_two = rms_back(d_half, lo_normed, lo_factor, gains[2])
+    d_attn, gain_one = rms_back(d_half, attn_normed, attn_factor, gains[1])
+    d_attn_all = group_gather(d_attn.astype(jnp.bfloat16))
+    d_lo_low = d_lo.astype(jnp.bfloat16)
+    g_right = mm_tn(lr_low, d_lo_low)
+    d_lr_low = mm_nt(d_lo_low, l_right).astype(jnp.bfloat16)
+    g_left = mm_tn(x_low, d_lr_low)
+
+    d_o_low = mm_nt(d_attn_all, w_o).astype(jnp.bfloat16)
+    g_out = both_cores(scatter_rows(mm_tn(o_low, d_attn_all), 1), 0)
+    d_probs = mm_nt(d_o_low, values)
+    delta = jnp.sum(probs * d_probs, axis=1, keepdims=True)
+    d_scores = (probs * (d_probs - delta)).astype(jnp.bfloat16)
+    d_query = mm(d_scores, keys)
+    d_kv = jnp.concatenate([mm_tn(d_scores, q_low), mm_tn(probs_low, d_o_low)], axis=1)
+    d_kv = d_kv.reshape(2, group_tokens, -1)
+    d_kv = d_kv[half] + swapped(d_kv[half ^ 1], "row", 0)
+    d_kv = lax.psum(d_kv, "seq")
+    d_kv = d_kv + swapped(d_kv, "col", 0)
+    d_q_raw, d_q_gain = query_back(d_query)
+    d_k_raw, d_k_gain = key_back(d_kv[:, :head_dim])
+    (d_v_raw,) = value_back(d_kv[:, head_dim:])
+    d_kv_low = jnp.concatenate([d_k_raw, d_v_raw], axis=1).astype(jnp.bfloat16)
+    kv_offset = core * head_dim + col % 2 * key_width
+    d_heads = jnp.concatenate(
+        [
+            d_q_raw.astype(jnp.bfloat16),
+            lax.dynamic_slice_in_dim(d_kv_low, kv_offset, key_width, 1),
+        ],
+        axis=1,
+    )
+    w_back = jnp.concatenate(
+        [
+            w_heads[:, :head_dim],
+            lax.dynamic_slice_in_dim(w_heads, head_dim + kv_offset, key_width, 1),
+        ],
+        axis=1,
+    )
+    d_xn = group_scatter(mm_nt(d_heads, w_back)) + mm_nt(d_lr_low, l_left)
+    g_heads = scatter_rows(mm_tn(x_all, d_heads), 0)
+    g_query = both_cores(g_heads[:, :head_dim], 1)
+    g_kv = both_cores(g_heads[:, head_dim:], 1)
+    d_in, gain_zero = rms_back(d_half + d_xn, x_normed, x_factor, gains[0])
+    grad_in = from_owner((d_half + d_in).astype(jnp.bfloat16), seq_count)
+
+    g_gains = jnp.concatenate(
+        [gain_zero, gain_one, gain_two, gain_three, gain_four, gain_five], axis=0
+    )
+    g_small_in = lax.psum_scatter(
+        jnp.concatenate([g_left, g_per_gate], axis=1), "row", scatter_dimension=0, tiled=True
+    )
+    g_small_out = lax.psum_scatter(
+        jnp.concatenate([g_right, g_per_proj, g_gains], axis=0),
+        "row",
+        scatter_dimension=1,
+        tiled=True,
+    )
+    g_small_in, g_small_out = lax.psum((g_small_in, g_small_out), ("seq", "col"))
+    g_head_gains = lax.psum(jnp.stack([d_q_gain, d_k_gain * 0.25]), ("seq", "row", "col"))
+    top = lax.pmax(top_tile[0, 0], "row")
+    tops = lax.all_gather(top, ("seq", "col"))
+    logit_top = tops.reshape(cores, cols).T.reshape(-1)
+    clip_factor = jnp.sqrt(CLIP_LEVEL / jnp.maximum(logit_top, CLIP_LEVEL))
+    clipped_gains = clip_factor[None, :, None] * head_gains[:, None, :]
+    proj_rows = rank + per_proj.shape[0]
+    return (
+        layer_out,
+        grad_in,
+        g_query,
+        g_kv[:, :key_width],
+        g_kv[:, key_width:],
+        g_out,
+        g_gate,
+        g_up,
+        g_down,
+        g_small_in[:, :rank],
+        g_small_out[:rank],
+        g_small_in[:, rank:],
+        g_small_out[rank:proj_rows],
+        g_small_out[proj_rows:],
+        g_head_gains,
+        clipped_gains,
+    )
+
+
 def solution(mesh):
+    sizes = tuple(mesh.shape[axis] for axis in ("seq", "row", "col"))
+    body = body_pair if sizes == (2, 4, 4) else body_any
     return jax.shard_map(
         body,
         mesh=mesh,

time: 1430 us -> 956 us (0.67)
  waiting for transfers between devices: 1010 us -> 493 us
  Pallas kernels: 0 us -> 213 us
  blocking collectives: 172 us -> 65.6 us
  matrix products: 107 us -> 56.1 us
  other arithmetic: 57.9 us -> 33.8 us
    all_gather x10 -> x7, waiting for transfers between devices: 347 us -> 96 us  [the longest x2 56.7 us: group_gather(): return lax.all_gather(values, ('seq', 'col'), axis=0, tiled=True)]
    reduce_scatter x10 -> x8, waiting for transfers between devices: 525 us -> 275 us  [the longest x4 154 us: scatter_rows(): lax.psum_scatter(values.astype(jnp.bfloat16), 'row', scatter_dimension=ax...]
    pallas_call x0 -> x1, Pallas kernels: none -> 213 us  [run_forward(): pl.pallas_call(forward_kernel, out_shape=outs, in_specs=[vm, vm, hbm, vm,...]
    psum x13 -> x1, blocking collectives: 132 us -> 35.8 us  [body_pair(): lax.psum(jnp.stack([d_q_gain, d_k_gain * 0.25]), ('seq', 'row', 'col'))]
    psum x4 -> x2, waiting for transfers between devices: 134 us -> 70.2 us  [the longest x1 62 us: body_pair(): lax.psum((g_small_in, g_small_out), ('seq', 'col'))]
    dot_general x42 -> x24, matrix products: 107 us -> 56.1 us  [the longest x10 26.4 us: mm_tn(): lax.dot_general(left_side, right_side, (((0,), (0,)), ((), ())), preferre...]
    ppermute x4, waiting for transfers between devices: 8.06 us -> 43.5 us  [swapped(): return lax.ppermute(value, axis, pairs)]
    pmax x1, blocking collectives: 39.7 us -> 7.5 us  [body_pair(): top = lax.pmax(top_tile[0, 0], 'row')]
  transfers between devices with their start and end apart: 28 -> 24, of which waited for: 25 -> 16; matrix products, arithmetic and copies ran while one was open for 5% -> 8% of each run, Pallas kernels for 0% -> 23%
where the time goes in v1:
time: 956 us; the launch traced here: 945 us
  waiting for transfers between devices  493 us (52%)
  Pallas kernels  213 us (22%)
  blocking collectives  65.6 us (7%)
  matrix products  56.1 us (6%)
  local copies, waits for them, and re-layouts  52 us (5%)
  other arithmetic  33.8 us (4%)
  starting transfers between devices  16.5 us (2%)
  between operations  15.3 us (2%)
    pallas_call x1, Pallas kernels, run_forward(): pl.pallas_call(forward_kernel, out_shape=outs, in_specs=[vm, vm, hbm, vm,...  213 us
    reduce_scatter x4, waiting for transfers between devices, scatter_rows(): lax.psum_scatter(values.astype(jnp.bfloat16), 'row', scatter_dimension=ax...  154 us
    reduce_scatter x2, waiting for transfers between devices, group_scatter(): lax.psum_scatter(partial.astype(jnp.bfloat16), ('seq', 'col'), scatter_di...  90.7 us
    psum x1, waiting for transfers between devices, body_pair(): lax.psum((g_small_in, g_small_out), ('seq', 'col'))  62 us
    all_gather x2, waiting for transfers between devices, group_gather(): return lax.all_gather(values, ('seq', 'col'), axis=0, tiled=True)  56.7 us
    ppermute x4, waiting for transfers between devices, swapped(): return lax.ppermute(value, axis, pairs)  43.5 us
    all_gather x5, waiting for transfers between devices, both_cores(): return lax.all_gather(values, 'seq', axis=axis, tiled=True)  39.3 us
    psum x1, blocking collectives, body_pair(): lax.psum(jnp.stack([d_q_gain, d_k_gain * 0.25]), ('seq', 'row', 'col'))  35.8 us
  transfers between devices with their start and end apart: 24, of which 16 were waited for; matrix products, arithmetic and copies ran while one was open for 8% of the time, Pallas kernels for 23%

profile of v1, /device:TPU:1, one launch (start us, length us, event | category | flops | bytes accessed | tf_op | source)
XLA Modules:
  0.0 945.1 jit_solution(7418383296492729117)
XLA Ops:
  7.2 4.4 all-to-all-start.1
  14.3 1.7 pad_maximum_fusion.9.small_out
  16.0 1.8 multiply_sine_fusion
  19.3 213.0 %shard_map.297 = (bf16[64,2048]{1,0:T(8,128)(2,1)}, f32[8,2048]{1,0:T(8,128)}, bf16[512,2048]{1,0:T(8,128)(2,1)}, f32[512,256]{1,0:T(8,128)}, f32[512,256]{1,0:T...) custom-call(bf16[4,64,512]{2,1,0:T(8,128)(2,1)} %bitcast.137, ...), custom_call_target="tpu_custom_call" | custom-call | flops 20000000000 | bytes 50000000 | tf_op jit(solution)/shard_map/pallas_call | solution.py:1139
  238.6 1.8 fusion.79
  246.1 29.5 %all-gather.8.cloned.1.call-done = bf16[512,2048]{1,0:T(8,128)(2,1)} async-done(((bf16[64,2048]{1,0:T(8,128)(2,1)}), bf16[512,2048]{1,0:T(8,128)(2,1)}) %all-gather.8.cloned.1.call-update) | async-done | bytes 2097168 | tf_op jit(solution)/shard_map/all_gather | solution.py:402
  275.6 7.9 fusion.14
  284.8 5.9 fusion.4
  291.9 47.7 %reduce-scatter.9.cloned.1.call-done = bf16[64,2048]{1,0:T(8,128)(2,1)} async-done(((bf16[512,2048]{1,0:T(8,128)(2,1)}), bf16[64,2048]{1,0:T(8,128)(2,1)}) %reduce-scatter.9.cloned.1.call-update) | async-done | bytes 262160 | tf_op jit(solution)/shard_map/reduce_scatter | solution.py:406
  342.6 1.7 multiply_convert_fusion.3
  345.4 27.2 %all-gather.10.cloned.1.call-done = bf16[512,2048]{1,0:T(8,128)(2,1)} async-done(((bf16[64,2048]{1,0:T(8,128)(2,1)}), bf16[512,2048]{1,0:T(8,128)(2,1)}) %all-gather.10.cloned.1.call-update) | async-done | bytes 2097168 | tf_op jit(solution)/shard_map/all_gather | solution.py:402
  372.6 2.6 convolution_convert_fusion.5
  380.3 1.9 copy.78
  384.5 23.6 %collective-permute-done = f32[512,512]{1,0:T(8,128)} collective-permute-done((f32[512,512]{1,0:T(8,128)}, f32[512,512]{1,0:T(8,128)}, u32[]{:S(2)}, u32[]{:S(2)}) %collective-permute-start) | collective-permute-done | bytes 1048608 | tf_op jit(solution)/shard_map/ppermute | solution.py:23
  408.1 2.4 bitcast_add_fusion
  410.6 3.5 convolution_convert_fusion.4
  414.2 5.6 convolution_convert_fusion.1
  422.4 8.1 all-reduce.9.cloned.1.call-done
  435.5 19.9 %collective-permute-done.1 = f32[512,512]{1,0:T(8,128)S(1)} collective-permute-done((f32[512,512]{1,0:T(8,128)}, f32[512,512]{1,0:T(8,128)S(1)}, u32[]{:S(2)}, u32[]{:S(2)}) %collective-permute-start.1) | collective-permute-done | bytes 1048608 | tf_op jit(solution)/shard_map/ppermute | solution.py:23
  459.6 2.6 convolution_convert_fusion.2
  462.6 4.1 convolution_convert_fusion.3
  466.8 9.7 %convolution_convert_fusion = bf16[2048,2048]{1,0:T(8,128)(2,1)} fusion(bf16[512,2048]{1,0:T(8,128)(2,1)} %get-tuple-element.63, bf16[512,1024]{1,0:T(8,128)(2,1)} %copy-done.59, bf16[512,1024]{1,0:T(8,128)(2,1)S(1)} %copy-done.58), kind=kOutput, calls=%fused_computation.5 | convolution fusion | flops 4303355904 | bytes 12582912 | tf_op jit(solution)/shard_map/dot_general | solution.py:438
  476.6 1.8 convert_element_type.137
  478.5 40.3 %reduce-scatter.19.cloned.1.call-done = bf16[1024,512]{1,0:T(8,128)(2,1)} async-done(((bf16[1024,2048]{1,0:T(8,128)(2,1)}), bf16[1024,512]{1,0:T(8,128)(2,1)}) %reduce-scatter.19.cloned.1.call-update) | async-done | bytes 1048592 | tf_op jit(solution)/shard_map/reduce_scatter | solution.py:462
  518.8 2.8 convert_element_type.141
  528.3 43.0 %reduce-scatter.11.cloned.1.call-done = bf16[64,2048]{1,0:T(8,128)(2,1)} async-done(((bf16[512,2048]{1,0:T(8,128)(2,1)}), bf16[64,2048]{1,0:T(8,128)(2,1)}) %reduce-scatter.11.cloned.1.call-update) | async-done | bytes 262160 | tf_op jit(solution)/shard_map/reduce_scatter | solution.py:406
  571.4 2.4 fusion.44
  573.7 4.6 concatenate.53
  578.5 25.8 %reduce-scatter.13.cloned.1.call-done = bf16[512,384]{1,0:T(8,128)(2,1)} async-done(((bf16[2048,384]{1,0:T(8,128)(2,1)}), bf16[512,384]{1,0:T(8,128)(2,1)}) %reduce-scatter.13.cloned.1.call-update) | async-done | bytes 393232 | tf_op jit(solution)/shard_map/reduce_scatter | solution.py:462
  604.3 1.8 slice.121
  606.1 87.9 %reduce-scatter.17.cloned.1.call-done = bf16[512,2048]{1,0:T(8,128)(2,1)} async-done(((bf16[2048,2048]{1,0:T(8,128)(2,1)}), bf16[512,2048]{1,0:T(8,128)(2,1)}) %reduce-scatter.17.cloned.1.call-update) | async-done | bytes 2097168 | tf_op jit(solution)/shard_map/reduce_scatter | solution.py:462
  694.0 4.0 fusion.112
  699.9 7.5 pmax.7
  709.4 19.3 %all-reduce.4 = f32[8]{0:T(128)S(1)} all-reduce(f32[8]{0:T(128)S(1)} %dynamic-update-slice), channel_id=1, replica_groups=mesh['seq'=2,'row'=4,'col'=4] {'seq','col'}, use_global_device_ids=true, to_apply=%add.4 | all-reduce | flops 8 | bytes 64
  729.8 3.4 all-to-all-start
  733.9 7.2 all-to-all-done
  741.2 35.8 %psum.31 = f32[2,256]{1,0:T(2,128)} all-reduce(f32[2,256]{1,0:T(2,128)S(1)} %pad_maximum_fusion.12), channel_id=1, replica_groups=mesh['seq'=2,'row'=4,'col'=4] {'seq','row','col'}, use_global_device_ids=true, to_apply=%region_40.41 | all-reduce | flops 512 | bytes 4096 | tf_op jit(solution)/shard_map/psum | solution.py:1388
  776.9 3.0 all_gather.33
  780.0 30.2 %reduce-scatter.23.cloned.1.call-done = f32[326,512]{1,0:T(8,128)} async-done(((f32[326,2048]{1,0:T(8,128)}), f32[326,512]{1,0:T(8,128)}) %reduce-scatter.23.cloned.1.call-update) | async-done | bytes 667664 | tf_op jit(solution)/shard_map/reduce_scatter | solution.py:1381
  811.1 3.4 all-to-all-start.2
  815.4 6.2 all-gather.12.cloned.1.call-done
  821.6 16.8 %all-gather.18.cloned.1.call-done = f32[512,2048]{1,0:T(8,128)} async-done(((f32[512,1024]{1,0:T(8,128)}), f32[512,2048]{1,0:T(8,128)}) %all-gather.18.cloned.1.call-update) | async-done | bytes 4194320 | tf_op jit(solution)/shard_map/all_gather | solution.py:468
  838.4 16.3 %all-gather.16.cloned.1.call-done = f32[512,2048]{1,0:T(8,128)} async-done(((f32[512,1024]{1,0:T(8,128)}), f32[512,2048]{1,0:T(8,128)}) %all-gather.16.cloned.1.call-update) | async-done | bytes 4194320 | tf_op jit(solution)/shard_map/all_gather | solution.py:468
  854.7 62.0 %all-reduce.11.cloned.1.call-done = (f32[512,320]{0,1:T(8,128)}, f32[326,512]{1,0:T(8,128)}) async-done(((f32[512,320]{0,1:T(8,128)}, f32[326,512]{1,0:T(8,128)}), (f32[512,320]{0,1:T(8,128)}, f32[326,512]{1,0:T(8,128)})) %all-reduce.11.cloned.1.call-update) | async-done | bytes 1323024 | tf_op jit(solution)/shard_map/psum | solution.py:1387
  922.4 1.9 slice.130
  928.7 2.1 copy.102
  932.4 2.1 copy.103
  936.1 2.0 copy.104
  (270 shorter events, 69.2 us)
Async XLA Ops:
  7.2 4.5 copy-start
  7.2 10.6 %copy-start.41 = (bf16[512,128]{1,0:T(8,128)(2,1)S(1)}, bf16[512,128]{1,0:T(8,128)(2,1)}, u32[]{:S(2)}) copy-start(bf16[512,128]{1,0:T(8,128)(2,1)} %param.23) | copy-start | bytes 393220
  7.2 10.6 %copy-start.40 = (bf16[512,128]{1,0:T(8,128)(2,1)S(1)}, bf16[512,128]{1,0:T(8,128)(2,1)}, u32[]{:S(2)}) copy-start(bf16[512,128]{1,0:T(8,128)(2,1)} %param.22) | copy-start | bytes 393220
  7.2 11.3 %copy-start.36 = (bf16[512,256]{1,0:T(8,128)(2,1)S(1)}, bf16[512,256]{1,0:T(8,128)(2,1)}, u32[]{:S(2)}) copy-start(bf16[512,256]{1,0:T(8,128)(2,1)} %param.30) | copy-start | bytes 786436
  7.2 233.6 %all-to-all-start.1 = ((bf16[4,64,512]{2,1,0:T(8,128)(2,1)}), bf16[4,64,512]{2,1,0:T(8,128)(2,1)}, u32[]{:S(2)}, u32[]{:S(2)}) async-start(bf16[4,64,512]{2,1,0:T(8,128)(2,1)} %bitcast.103), calls=%async_computation.1 | async-start | bytes 524288 | tf_op jit(solution)/shard_map/all_to_all | solution.py:415
  11.6 264.0 %all-gather.8.cloned.1.call-start = ((), (), s32[]{:S(2)}) async-start(), calls=%async_computation.11 | async-start | bytes 2359296 | tf_op jit(solution)/shard_map/all_gather | solution.py:402
  232.3 5.2 copy-start.2
  232.3 5.2 copy-start.4
  232.4 6.1 copy-start.3
  245.0 38.5 %copy-start.5 = (f32[64,2048]{1,0:T(8,128)}, f32[64,2048]{1,0:T(8,128)S(1)}, u32[]{:S(2)}) copy-start(f32[64,2048]{1,0:T(8,128)S(1)} %get-tuple-element.204) | copy-start | bytes 1572868
  245.9 93.7 %reduce-scatter.9.cloned.1.call-start = ((), (), s32[]{:S(2)}) async-start(), calls=%async_computation.12 | async-start | bytes 2359296 | tf_op jit(solution)/shard_map/reduce_scatter | solution.py:406
  275.6 9.2 copy-start.55
  275.6 9.2 copy-start.56
  290.7 50.2 %copy-start.6 = (f32[64,2048]{1,0:T(8,128)S(1)}, f32[64,2048]{1,0:T(8,128)}, u32[]{:S(2)}) copy-start(f32[64,2048]{1,0:T(8,128)} %copy-done.5) | copy-start | bytes 1572868
  290.7 81.9 %all-gather.10.cloned.1.call-start = ((), (), s32[]{:S(2)}) async-start(), calls=%async_computation.13 | async-start | bytes 2359296 | tf_op jit(solution)/shard_map/all_gather | solution.py:402
  291.9 49.0 %copy-start.51 = (f32[64]{0:T(128)}, f32[64]{0:T(128)S(1)}, u32[]{:S(2)}) copy-start(f32[64]{0:T(128)S(1)} %get-tuple-element.197) | copy-start | bytes 772
  344.3 86.3 %all-reduce.9.cloned.1.call-start = ((), (), s32[]{:S(2)}) async-start(), calls=%async_computation.14 | async-start | bytes 2097152 | tf_op jit(solution)/shard_map/psum | solution.py:1347
  345.2 30.0 %copy-start.38 = (bf16[2,1024,256]{2,1,0:T(8,128)(2,1)S(1)}, bf16[2,1024,256]{2,1,0:T(8,128)(2,1)}, u32[]{:S(2)}) copy-start(bf16[2,1024,256]{2,1,0:T(8,128)(2,1)} %get-tuple-element.54) | copy-start | bytes 3145732
  383.3 24.8 %collective-permute-start = (f32[512,512]{1,0:T(8,128)}, f32[512,512]{1,0:T(8,128)}, u32[]{:S(2)}, u32[]{:S(2)}) collective-permute-start(f32[512,512]{1,0:T(8,128)} %dynamic-slice_bitcast_fusion), channel_id=1, source_target_pairs={{0,4},{4,0},{8,12},{12,8},{1,5},{5,1},{9,13},{13,9},{2,6},{6,2},{1... | collective-permute-start | bytes 3145736 | tf_op jit(solution)/shard_map/ppermute | solution.py:23
  410.5 66.1 %reduce-scatter.15.cloned.1.call-start = ((), (), s32[]{:S(2)}) async-start(), calls=%async_computation.18 | async-start | bytes 1310720 | tf_op jit(solution)/shard_map/reduce_scatter | solution.py:462
  414.1 104.7 %reduce-scatter.19.cloned.1.call-start = ((), (), s32[]{:S(2)}) async-start(), calls=%async_computation.23 | async-start | bytes 5242880 | tf_op jit(solution)/shard_map/reduce_scatter | solution.py:462
  419.8 151.5 %reduce-scatter.11.cloned.1.call-start = ((), (), s32[]{:S(2)}) async-start(), calls=%async_computation.15 | async-start | bytes 2359296 | tf_op jit(solution)/shard_map/reduce_scatter | solution.py:406
  421.0 11.1 %collective-permute-start.3 = (bf16[2048,256]{1,0:T(8,128)(2,1)S(1)}, bf16[2048,256]{1,0:T(8,128)(2,1)}, u32[]{:S(2)}, u32[]{:S(2)}) collective-permute-start(bf16[2048,256]{1,0:T(8,128)(2,1)S(1)} %copy-done.19), channel_id=1, source_target_pairs={{0,16},{16,0},{1,17},{17,1},{2,18},{18,2},{3,19},{19,3},{4,20},{20... | collective-permute-start | bytes 3145736 | tf_op jit(solution)/shard_map/ppermute | solution.py:23
  422.1 33.5 %collective-permute-start.2 = (f32[512,256]{1,0:T(8,128)S(1)}, f32[512,256]{1,0:T(8,128)}, u32[]{:S(2)}, u32[]{:S(2)}) collective-permute-start(f32[512,256]{1,0:T(8,128)S(1)} %copy-done.34), channel_id=1, source_target_pairs={{0,16},{16,0},{1,17},{17,1},{2,18},{18,2},{3,19},{19,3},{4,20},{20... | collective-permute-start | bytes 1572872 | tf_op jit(solution)/shard_map/ppermute | solution.py:23
  430.6 24.8 %collective-permute-start.1 = (f32[512,512]{1,0:T(8,128)}, f32[512,512]{1,0:T(8,128)S(1)}, u32[]{:S(2)}, u32[]{:S(2)}) collective-permute-start(f32[512,512]{1,0:T(8,128)} %all-reduce.9.cloned.1.call-done), channel_id=1, source_target_pairs={{0,1},{1,0},{2,3},{3,2},{4,5},{5,4},{6,7},{7,6},{8,9},{9,8},{10,11... | collective-permute-start | bytes 3145736 | tf_op jit(solution)/shard_map/ppermute | solution.py:23
  433.5 21.9 %copy-start.20 = (f32[512,512]{1,0:T(8,128)S(1)}, f32[512,512]{1,0:T(8,128)}, u32[]{:S(2)}) copy-start(f32[512,512]{1,0:T(8,128)} %all-reduce.9.cloned.1.call-done) | copy-start | bytes 3145732
  462.3 142.0 %reduce-scatter.13.cloned.1.call-start = ((), (), s32[]{:S(2)}) async-start(), calls=%async_computation.16 | async-start | bytes 1966080 | tf_op jit(solution)/shard_map/reduce_scatter | solution.py:462
  466.7 227.3 %reduce-scatter.17.cloned.1.call-start = ((), (), s32[]{:S(2)}) async-start(), calls=%async_computation.20 | async-start | bytes 10485760 | tf_op jit(solution)/shard_map/reduce_scatter | solution.py:462
  476.5 264.6 %all-gather.14.cloned.1.call-start = ((), (), s32[]{:S(2)}) async-start(), calls=%async_computation.19 | async-start | bytes 1572864 | tf_op jit(solution)/shard_map/all_gather | solution.py:468
  478.4 298.5 %all-gather.20.cloned.1.call-start = ((), (), s32[]{:S(2)}) async-start(), calls=%async_computation.24 | async-start | bytes 6291456 | tf_op jit(solution)/shard_map/all_gather | solution.py:468
  521.7 258.3 %reduce-scatter.21.cloned.1.call-start = ((), (), s32[]{:S(2)}) async-start(), calls=%async_computation.25 | async-start | bytes 3276800 | tf_op jit(solution)/shard_map/reduce_scatter | solution.py:1378
  525.7 284.4 %reduce-scatter.23.cloned.1.call-start = ((), (), s32[]{:S(2)}) async-start(), calls=%async_computation.26 | async-start | bytes 3358720 | tf_op jit(solution)/shard_map/reduce_scatter | solution.py:1381
  578.4 243.2 %all-gather.12.cloned.1.call-start = ((), (), s32[]{:S(2)}) async-start(), calls=%async_computation.17 | async-start | bytes 1572864 | tf_op jit(solution)/shard_map/all_gather | solution.py:468
  606.1 232.3 %all-gather.18.cloned.1.call-start = ((), (), s32[]{:S(2)}) async-start(), calls=%async_computation.22 | async-start | bytes 6291456 | tf_op jit(solution)/shard_map/all_gather | solution.py:468
  698.0 9.4 copy-start.54
  698.1 31.0 %copy-start.33 = (bf16[64,2048]{1,0:T(8,128)(2,1)S(1)}, bf16[64,2048]{1,0:T(8,128)(2,1)}, u32[]{:S(2)}) copy-start(bf16[64,2048]{1,0:T(8,128)(2,1)} %get-tuple-element.171) | copy-start | bytes 786436
  698.1 43.1 %copy-start.50 = (f32[256]{0:T(256)S(1)}, f32[256]{0:T(256)}, u32[]{:S(2)}) copy-start(f32[256]{0:T(256)} %get-tuple-element.138) | copy-start | bytes 3076
  698.1 78.8 %copy-start.16 = (bf16[512,384]{1,0:T(8,128)(2,1)S(1)}, bf16[512,384]{1,0:T(8,128)(2,1)}, u32[]{:S(2)}) copy-start(bf16[512,384]{1,0:T(8,128)(2,1)} %reduce-scatter.13.cloned.1.call-done) | copy-start | bytes 1179652
  698.1 156.6 %all-gather.16.cloned.1.call-start = ((), (), s32[]{:S(2)}) async-start(), calls=%async_computation.21 | async-start | bytes 6291456 | tf_op jit(solution)/shard_map/all_gather | solution.py:468
  698.7 111.5 %copy-start.15 = (f32[64,2048]{1,0:T(8,128)S(1)}, f32[64,2048]{1,0:T(8,128)}, u32[]{:S(2)}) copy-start(f32[64,2048]{1,0:T(8,128)} %get-tuple-element.207) | copy-start | bytes 1572868
  729.8 11.3 %all-to-all-start = ((bf16[4,64,512]{2,1,0:T(8,128)(2,1)}), bf16[4,64,512]{2,1,0:T(8,128)(2,1)S(1)}, u32[]{:S(2)}, u32[]{:S(2)}) async-start(bf16[4,64,512]{2,1,0:T(8,128)(2,1)} %bitcast.93), calls=%async_computation | async-start | bytes 524288 | tf_op jit(solution)/shard_map/all_to_all | solution.py:423
  733.2 183.5 %all-reduce.11.cloned.1.call-start = ((), (), s32[]{:S(2)}) async-start(), calls=%async_computation.27 | async-start | bytes 2654208 | tf_op jit(solution)/shard_map/psum | solution.py:1387
  741.1 69.3 %copy-start.26 = (bf16[4,64,512]{2,1,0:T(8,128)(2,1)}, bf16[4,64,512]{2,1,0:T(8,128)(2,1)S(1)}, u32[]{:S(2)}) copy-start(bf16[4,64,512]{2,1,0:T(8,128)(2,1)S(1)} %all-to-all-done) | copy-start | bytes 786436
  811.1 10.4 %all-to-all-start.2 = ((bf16[4,64,512]{2,1,0:T(8,128)(2,1)}), bf16[4,64,512]{2,1,0:T(8,128)(2,1)S(1)}, u32[]{:S(2)}, u32[]{:S(2)}) async-start(bf16[4,64,512]{2,1,0:T(8,128)(2,1)} %bitcast.91), calls=%async_computation.4 | async-start | bytes 524288 | tf_op jit(solution)/shard_map/all_to_all | solution.py:423
  815.4 109.8 %copy-start.27 = (bf16[4,64,512]{2,1,0:T(8,128)(2,1)S(1)}, bf16[4,64,512]{2,1,0:T(8,128)(2,1)}, u32[]{:S(2)}) copy-start(bf16[4,64,512]{2,1,0:T(8,128)(2,1)} %copy-done.26) | copy-start | bytes 786436
  821.6 95.1 %copy-start.28 = (bf16[4,64,512]{2,1,0:T(8,128)(2,1)}, bf16[4,64,512]{2,1,0:T(8,128)(2,1)S(1)}, u32[]{:S(2)}) copy-start(bf16[4,64,512]{2,1,0:T(8,128)(2,1)S(1)} %all-to-all-done.2) | copy-start | bytes 786436
  918.3 7.7 copy-start.29
  918.3 8.4 copy-start.25
  (36 other events, 71.4 us)
Sparse Core Ops, SparseCore 0:
  246.0 29.5 all-gather.7
  290.8 48.6 reduce-scatter.8
  344.4 28.1 all-gather.9
  410.6 19.8 all-reduce.8
  434.1 28.4 reduce-scatter.14
  466.1 52.6 reduce-scatter.18
  521.8 49.5 reduce-scatter.10
  574.6 29.5 reduce-scatter.12
  607.6 86.3 reduce-scatter.16
  696.0 9.4 all-gather.13
  707.0 14.8 all-gather.19
  725.3 41.0 reduce-scatter.20
  770.0 40.1 reduce-scatter.22
  812.1 9.3 all-gather.11
  823.5 14.8 all-gather.17
  839.8 14.8 all-gather.15
  857.0 59.6 all-reduce.10

commit v2 on v1

--- a/solution.py
+++ b/solution.py
@@ -15,6 +15,7 @@
 MESH = pl.DeviceIdType.MESH
 BF = jnp.bfloat16
 F32 = jnp.float32
+VMEM_BYTES = 63 * 2**20
 
 
 def swapped(value, axis, apart):
@@ -621,7 +622,7 @@
         lane = 0 if right else 4
         return remote(
             self.sent.at[dest],
-            (self.left if right else self.right).at[dest],
+            self.left.at[dest - 1] if right else self.right.at[dest],
             self.send_z.at[lane + dest],
             self.recv_z.at[lane + dest],
             (self.core, self.row, self.col + step),
@@ -636,7 +637,7 @@
             @pl.when(inner)
             def _():
                 self.hop(dest, right).wait_recv()
-                came = (self.left if right else self.right)[dest].astype(F32)
+                came = (self.left[dest - 1] if right else self.right[dest]).astype(F32)
                 self.sent[dest] = (self.mine(dest) + came).astype(BF)
 
             @pl.when(jnp.logical_not(inner))
@@ -645,36 +646,38 @@
 
             self.hop(dest, right).start()
 
-    def run(self, result):
+    def run(self, result, work=()):
         col = self.col
+        work = list(work)
         self.sibling().wait_recv()
         for dest in (3, 2, 1):
             self.chain(dest, True)
             self.chain(3 - dest, False)
+            if work:
+                work.pop(0)()
         own = pl.ds(pl.multiple_of(col * self.rows, self.rows), self.rows)
         result[...] = self.keep[own] + self.got[own].astype(F32)
         for dest in range(4):
 
-            @pl.when((col == dest) & (dest > 0))
+            @pl.when(col == dest)
             def _():
-                self.hop(dest, True).wait_recv()
-                result[...] += self.left[dest].astype(F32)
-
-            @pl.when((col == dest) & (dest < 3))
-            def _():
-                self.hop(dest, False).wait_recv()
-                result[...] += self.right[dest].astype(F32)
+                if dest > 0:
+                    self.hop(dest, True).wait_recv()
+                    result[...] += self.left[dest - 1].astype(F32)
+                if dest < 3:
+                    self.hop(dest, False).wait_recv()
+                    result[...] += self.right[dest].astype(F32)
 
         self.sibling().wait_send()
-        for dest in range(4):
+        for dest in (1, 2, 3):
 
             @pl.when(col < dest)
             def _():
                 self.hop(dest, True).wait_send()
 
-            @pl.when(col > dest)
+            @pl.when(col > 3 - dest)
             def _():
-                self.hop(dest, False).wait_send()
+                self.hop(3 - dest, False).wait_send()
 
 
 class RowGather:
@@ -757,9 +760,11 @@
     return block, halves
 
 
-def gelu(values):
+def gelu_both(values):
     inner = 0.7978845608028654 * (values + 0.044715 * values * values * values)
-    return 0.5 * values * (1.0 + jnp.tanh(inner))
+    bend = jnp.tanh(inner)
+    slope = 0.7978845608028654 * (1.0 + 3.0 * 0.044715 * values * values)
+    return 0.5 * values * (1.0 + bend), 0.5 * (1.0 + bend) + 0.5 * values * (1.0 - bend * bend) * slope
 
 
 def head_parts(raw, gain, cosine, sine):
@@ -772,6 +777,7 @@
 
 def forward_kernel(
     x_in,
+    g_in,
     gains_in,
     w_query,
     w_kv,
@@ -786,6 +792,7 @@
     start,
     head_gains,
     x_own,
+    g_own,
     gains,
     xg,
     raw_q,
@@ -864,6 +871,15 @@
             (core, row ^ mask, col),
         )
 
+    def hand_grad(mask):
+        return remote(
+            g_in.at[row ^ mask],
+            g_own.at[:, my_cols],
+            misc_send.at[11 + mask],
+            misc_recv.at[11 + mask],
+            (core, row ^ mask, col),
+        )
+
     def hand_gains(mask):
         return remote(
             gains_pad,
@@ -880,6 +896,7 @@
     for mask in (3, 1, 2):
         hand_gains(mask).start()
     x_own[:, my_cols] = x_in[row]
+    g_own[:, my_cols] = g_in[row]
     gains[:, my_cols] = gains_pad[...]
 
     pair_cols = pl.ds(pl.multiple_of(col % 2 * key_width, key_width), key_width)
@@ -940,6 +957,8 @@
     get_si.start()
     get_so.start()
     get_g.start()
+    for mask in (1, 2, 3):
+        hand_grad(mask).start()
     gather_x.forward()
     gather_x.finish()
     get_q.finish()
@@ -1045,11 +1064,11 @@
 
     def units(index, carry):
         cols = pl.ds(pl.multiple_of(index * tile, tile), tile)
-        gate_part = mm(fg[...], vg[:, cols])
-        gate[:, cols] = gate_part
+        bent, slope = gelu_both(mm(fg[...], vg[:, cols]))
         up_part = mm(fg[...], vu[:, cols])
-        up[:, cols] = up_part
-        hid[:, cols] = (gelu(gate_part) * up_part).astype(BF)
+        gate[:, cols] = (up_part * slope).astype(BF)
+        up[:, cols] = bent.astype(BF)
+        hid[:, cols] = (bent * up_part).astype(BF)
         return carry
 
     lax.fori_loop(0, ff_part // tile, units, 0)
@@ -1081,6 +1100,14 @@
     for mask in (1, 2, 3):
         hand_over(mask).wait_send()
         hand_gains(mask).wait_send()
+        hand_grad(mask).wait_send()
+        remote(
+            g_in.at[row],
+            g_own.at[:, pl.ds(pl.multiple_of((row ^ mask) * block, block), block)],
+            misc_send.at[11 + mask],
+            misc_recv.at[11 + mask],
+            (core, row, col),
+        ).wait_recv()
     pair.wait_send()
     to_x.wait_send()
     to_s.wait_send()
@@ -1089,7 +1116,7 @@
         copy.wait()
 
 
-def run_forward(x_in, gains_in, w_query, w_kv, w_out, w_gate, w_up, w_down, small_in, small_out, tables, head_gains):
+def run_forward(x_in, g_in, gains_in, w_query, w_kv, w_out, w_gate, w_up, w_down, small_in, small_out, tables, head_gains):
     cosine, sine, start = tables
     block = x_in.shape[2]
     own, width = x_in.shape[1], 4 * block
@@ -1110,6 +1137,7 @@
     ]
     outs = [
         shape((own, width), BF),
+        shape((own, width), BF),
         shape((8, width), F32),
         shape((tokens, width), BF),
         shape((tokens, head_dim), F32),
@@ -1122,8 +1150,8 @@
         shape((own, width), F32),
         shape((own, rank), BF),
         shape((tokens, width), BF),
-        shape((tokens, ff_part), F32),
-        shape((tokens, ff_part), F32),
+        shape((tokens, ff_part), BF),
+        shape((tokens, ff_part), BF),
         shape((tokens, ff_part), BF),
         shape((own, width), F32),
     ] + [shape(size, BF) for size in weights]
@@ -1132,15 +1160,15 @@
         pltpu.VMEM((4 * own, width), F32),
         pltpu.VMEM((4 * own, width), BF),
         pltpu.VMEM((4, own, width), BF),
-        pltpu.VMEM((4, own, width), BF),
-        pltpu.VMEM((4, own, width), BF),
+        pltpu.VMEM((3, own, width), BF),
+        pltpu.VMEM((3, own, width), BF),
     ]
     dma = pltpu.SemaphoreType.DMA
     return pl.pallas_call(
         forward_kernel,
         out_shape=outs,
-        in_specs=[vm, vm, hbm, vm, hbm, hbm, hbm, hbm, hbm, hbm, vm, vm, vm, vm],
-        out_specs=[vm] * 17 + [hbm] * 8,
+        in_specs=[vm, vm, vm, hbm, vm, hbm, hbm, hbm, hbm, hbm, hbm, vm, vm, vm, vm],
+        out_specs=[vm] * 18 + [hbm] * 8,
         scratch_shapes=[pltpu.VMEM((block, head_dim), BF), pltpu.VMEM((8, block), F32)]
         + [pltpu.VMEM(size, BF) for size in weights]
         + scatter_bufs * 2
@@ -1150,15 +1178,793 @@
             dma((4, 8)),
             dma((4, 4)),
             dma((4, 4)),
-            dma((12,)),
-            dma((12,)),
+            dma((16,)),
+            dma((16,)),
             dma((8,)),
         ],
         compiler_params=pltpu.CompilerParams(
             collective_id=0, has_side_effects=True, vmem_limit_bytes=60 * 2**20
         ),
         cost_estimate=pl.CostEstimate(flops=2 * 10**10, bytes_accessed=5 * 10**7, transcendentals=10**6),
-    )(x_in, gains_in, w_query, w_kv, w_out, w_gate, w_up, w_down, small_in, small_out, cosine, sine, start, head_gains)
+    )(x_in, g_in, gains_in, w_query, w_kv, w_out, w_gate, w_up, w_down, small_in, small_out, cosine, sine, start, head_gains)
+
+
+class RowScatter:
+    def __init__(self, place, halves, came, sems, stage=None):
+        self.core, self.row, self.col = place
+        self.halves, self.came, self.sems = halves, came, sems
+        self.stage = stage
+
+    def send(self, lane, index, half, mask):
+        return remote(
+            self.halves(index)[half],
+            self.came.at[lane],
+            self.sems.at[lane],
+            self.sems.at[6 + lane],
+            (self.core, self.row ^ mask, self.col),
+        )
+
+    def lane(self, lane):
+        index, half, mask = ((1, 0, 1), (3, 0, 1), (2, 1, 2), (3, 1, 2), (2, 0, 2), (1, 1, 1))[lane]
+        return self.send(lane, self.row ^ index, half, mask)
+
+    def start(self):
+        for lane in (1, 3, 0, 2):
+            self.lane(lane).start()
+
+    def value(self, lane):
+        return (self.came if self.stage is None else self.stage[0])[
+            lane if self.stage is None else lane % 2
+        ].astype(F32)
+
+    def fetch(self, *wanted):
+        for lane in wanted:
+            self.lane(lane).wait_recv()
+        if self.stage is None:
+            return
+        copies = [
+            pltpu.make_async_copy(
+                self.came.at[lane], self.stage[0].at[lane % 2], self.stage[1].at[lane % 2]
+            )
+            for lane in wanted
+        ]
+        for copy in copies:
+            copy.start()
+        for copy in copies:
+            copy.wait()
+
+    def middle(self):
+        row = self.row
+        for lane, out, index, half in ((1, 4, row ^ 2, 0), (3, 5, row ^ 1, 1)):
+            self.fetch(lane)
+            part = self.halves(index)[half]
+            part[...] = (part[...].astype(F32) + self.value(lane)).astype(BF)
+            self.lane(out).start()
+
+    def finish(self):
+        row = self.row
+        for pair, half in (((0, 4), 0), ((2, 5), 1)):
+            part = self.halves(row)[half]
+            total = part[...].astype(F32)
+            for lane in pair:
+                self.fetch(lane)
+                total = total + self.value(lane)
+            part[...] = total.astype(BF)
+
+    def drain(self):
+        for lane in range(6):
+            self.lane(lane).wait_send()
+
+
+def head_back(grad, raw, gain, cosine, sine):
+    factor = lax.rsqrt(jnp.mean(raw * raw, axis=1, keepdims=True) + EPSILON)
+    half = raw.shape[1] // 2
+    normed = raw * factor
+    first, second = grad[:, :half], grad[:, half:]
+    back = jnp.concatenate([first * cosine + second * sine, second * cosine - first * sine], axis=1)
+    gain_grad = jnp.sum(back * normed, axis=0, keepdims=True)
+    inner = back * gain
+    return factor * (inner - normed * jnp.mean(inner * normed, axis=1, keepdims=True)), gain_grad
+
+
+def backward_kernel(
+    x_own,
+    g_own,
+    per_in,
+    gains,
+    head_gains,
+    attn_val,
+    lr_low,
+    ff_val,
+    raw_q,
+    raw_kv,
+    q_low,
+    kv,
+    lse,
+    top,
+    o_low,
+    cosine,
+    sine,
+    start,
+    vsi,
+    vso,
+    xg_in,
+    fg_in,
+    gate_in,
+    up_in,
+    hid_in,
+    wq_in,
+    wkv_in,
+    wo_in,
+    wg_in,
+    wu_in,
+    wd_in,
+    y_out,
+    x_grad,
+    g_gain,
+    tops,
+    small_a,
+    gq,
+    gkv,
+    gout,
+    ggate,
+    gup,
+    gdown,
+    came_g,
+    came_u,
+    came_d,
+    vq,
+    vkv,
+    vo,
+    vg,
+    vu,
+    vd,
+    fg,
+    gate,
+    up,
+    hid,
+    dffg,
+    dattng,
+    dgate,
+    dup,
+    give,
+    keep,
+    got,
+    sent,
+    left,
+    right,
+    own_sum,
+    h_two_ref,
+    d_three_ref,
+    low_ref,
+    gpart,
+    gcame,
+    gpart2,
+    gcame2,
+    small_give,
+    small_keep,
+    small_got,
+    small_row,
+    small_z,
+    d_o,
+    d_kv,
+    kv_give,
+    kv_got,
+    kv_x,
+    kv_x_got,
+    kv_p_got,
+    pkv,
+    came_q,
+    came_kv,
+    came_o,
+    stage_g,
+    stage_d,
+    stage_sems,
+    load_sems,
+    row_sems,
+    z_send,
+    z_recv,
+    s_send,
+    s_recv,
+    misc_send,
+    misc_recv,
+    gain_send,
+    gain_recv,
+    done_sems,
+):
+    core, row, col = lax.axis_index("seq"), lax.axis_index("row"), lax.axis_index("col")
+    place = (core, row, col)
+    own_tokens, width = x_own.shape
+    block = width // 4
+    tokens, head_dim = raw_q.shape
+    ff_part = gate.shape[1]
+    chunk = 2 * own_tokens
+    key_width = head_dim // 2
+    half = row % 2
+    rank = lr_low.shape[1]
+    my_cols = pl.ds(pl.multiple_of(row * block, block), block)
+    mine = pl.ds(pl.multiple_of((core * 4 + col) * own_tokens, own_tokens), own_tokens)
+    away = pl.multiple_of((1 - core) * 4 * own_tokens, 4 * own_tokens)
+    home = pl.multiple_of(core * 4 * own_tokens, 4 * own_tokens)
+
+    barrier = pltpu.get_barrier_semaphore()
+    for mask in (1, 2, 3):
+        pl.semaphore_signal(barrier, inc=1, device_id=(core, row ^ mask, col), device_id_type=MESH)
+        for other in (0, 1):
+            pl.semaphore_signal(
+                barrier, inc=1, device_id=(core ^ other, row, col ^ mask), device_id_type=MESH
+            )
+    pl.semaphore_signal(barrier, inc=1, device_id=(1 - core, row, col), device_id_type=MESH)
+    loads = [
+        pltpu.make_async_copy(source, target, load_sems.at[lane])
+        for lane, (source, target) in enumerate(
+            [
+                (wd_in, vd),
+                (gate_in, gate),
+                (up_in, up),
+                (wg_in, vg),
+                (wu_in, vu),
+                (hid_in, hid),
+                (fg_in, fg),
+                (wo_in, vo),
+                (wq_in, vq),
+                (wkv_in, vkv),
+            ]
+        )
+    ]
+    for load in loads:
+        load.start()
+    pl.semaphore_wait(barrier, 10)
+
+    def gain(index):
+        return gains[pl.ds(index, 1)]
+
+    inputs = x_own[...].astype(F32)
+    x_norm = rms(inputs)[0] * gain(0)
+    attn_normed = rms(attn_val[...])[0]
+    lo_normed = rms(mm(lr_low[...], vso[pl.ds(0, rank)]))[0]
+    h_two = (inputs + attn_normed * gain(1) + (x_norm + lo_normed * gain(2))) * ROOT_HALF
+    h_two_ref[...] = h_two
+    ff_normed, ff_factor = rms(ff_val[...])
+    h_three = h_two + ff_normed * gain(4)
+    h_low = h_three.astype(BF)
+    p_gate = vsi[:, pl.ds(2 * rank, vsi.shape[1] - 2 * rank)]
+    p_proj = vso[pl.ds(rank, vso.shape[0] - rank)]
+    pg_gelu, pg_slope = gelu_both(mm(h_low, p_gate))
+    per_input = per_in[row].astype(F32)
+    gp_low = (pg_gelu * per_input).astype(BF)
+    pp_normed, pp_factor = rms(mm(gp_low, p_proj))
+    low_ref[...] = (h_three + pp_normed * gain(5)).astype(BF)
+
+    def hand_back(source, target, mask, lane):
+        return remote(
+            source.at[:, pl.ds(pl.multiple_of((row ^ mask) * block, block), block)],
+            target.at[row],
+            misc_send.at[lane + mask],
+            misc_recv.at[lane + mask],
+            (core, row ^ mask, col),
+        )
+
+    def came_back(target, mask, lane):
+        return remote(
+            target.at[row ^ mask],
+            target.at[row ^ mask],
+            misc_send.at[lane + mask],
+            misc_recv.at[lane + mask],
+            (core, row, col),
+        )
+
+    for mask in (1, 2, 3):
+        hand_back(low_ref, y_out, mask, 0).start()
+    y_out[row] = low_ref[:, my_cols]
+
+    grad_top = g_own[...].astype(F32)
+    d_pp, gain_five = rms_back(grad_top, pp_normed, pp_factor, gain(5))
+    d_pp_low = d_pp.astype(BF)
+    d_pg_low = (mm_nt(d_pp_low, p_proj) * per_input * pg_slope).astype(BF)
+    d_three = grad_top + mm_nt(d_pg_low, p_gate)
+    d_three_ref[...] = d_three
+    d_ff, gain_four = rms_back(d_three, ff_normed, ff_factor, gain(4))
+    gpart[...] = jnp.zeros(gpart.shape, F32)
+    gpart[pl.ds(5, 1)] = gain_five
+    gpart[pl.ds(4, 1)] = gain_four
+    dffg[mine] = d_ff.astype(BF)
+    sems = lambda lane: (z_send.at[lane], z_recv.at[lane], s_send.at[lane], s_recv.at[lane])
+    gather_ff = Gather(place, dffg, own_tokens, sems(0))
+    gather_ff.start()
+
+    def small(kind, first, value):
+        rows = pl.ds(first, value.shape[0])
+        value = value.astype(BF)
+
+        @pl.when(core == kind)
+        def _():
+            small_keep[rows] = value
+
+        @pl.when(core != kind)
+        def _():
+            small_give[rows] = value
+
+    small(0, rank, mm_tn(gp_low, d_pp_low))
+    small(1, rank, mm_tn(d_pg_low, h_low))
+    gather_ff.forward()
+    gather_ff.finish()
+
+    tile = 256
+    for load in loads[:3]:
+        load.wait()
+
+    def units(index, carry):
+        cols = pl.ds(pl.multiple_of(index * tile, tile), tile)
+        d_hid = mm_nt(dffg[...], vd[cols])
+        dgate[:, cols] = (d_hid * gate[:, cols].astype(F32)).astype(BF)
+        dup[:, cols] = (d_hid * up[:, cols].astype(F32)).astype(BF)
+        return carry
+
+    lax.fori_loop(0, ff_part // tile, units, 0)
+    for load in loads[3:5]:
+        load.wait()
+
+    def back_ff(target, first):
+        rows = pl.ds(first, 4 * own_tokens)
+
+        def step(index, carry):
+            cols = pl.ds(pl.multiple_of(index * block, block), block)
+            value = mm_nt(dgate[rows], vg[cols]) + mm_nt(dup[rows], vu[cols])
+            target[:, cols] = value.astype(target.dtype)
+            return carry
+
+        lax.fori_loop(0, width // block, step, 0)
+
+    scatter_f = Scatter(place, own_tokens, (give, keep, got, sent, left, right), sems(1))
+    back_ff(give, away)
+    scatter_f.sibling().start()
+    back_ff(keep, home)
+
+    put_d = RowScatter(place, by_cols(vd, block)[1], came_d, row_sems.at[0], (stage_d, stage_sems))
+    put_g = RowScatter(place, by_rows(vg, block)[1], came_g, row_sems.at[1], (stage_g, stage_sems))
+    put_u = RowScatter(place, by_rows(vu, block)[1], came_u, row_sems.at[2], (stage_g, stage_sems))
+
+    def down_grad():
+        loads[5].wait()
+
+        def step(index, carry):
+            cols = pl.ds(pl.multiple_of(index * tile, tile), tile)
+            for part in range(2):
+                wide = pl.ds(part * (width // 2), width // 2)
+                vd[cols, wide] = mm_tn(hid[:, cols], dffg[:, wide]).astype(BF)
+            return carry
+
+        lax.fori_loop(0, ff_part // tile, step, 0)
+        put_d.start()
+
+    def gate_grad(target, grad, put):
+        def step(index, carry):
+            rows = pl.ds(pl.multiple_of(index * tile, tile), tile)
+            target[rows] = mm_tn(fg[:, rows], grad[...]).astype(BF)
+            return carry
+
+        lax.fori_loop(0, width // tile, step, 0)
+        put.start()
+
+    def both_gates():
+        loads[6].wait()
+        gate_grad(vg, dgate, put_g)
+
+    scatter_f.run(own_sum, [down_grad, both_gates, lambda: gate_grad(vu, dup, put_u)])
+
+    f_normed, f_factor = rms(h_two_ref[...])
+    d_f, gain_three = rms_back(own_sum[...], f_normed, f_factor, gain(3))
+    d_half = (d_three_ref[...] + d_f) * ROOT_HALF
+    d_three_ref[...] = d_half
+    attn_normed, attn_factor = rms(attn_val[...])
+    d_attn, gain_one = rms_back(d_half, attn_normed, attn_factor, gain(1))
+    dattng[mine] = d_attn.astype(BF)
+    gather_a = Gather(place, dattng, own_tokens, sems(2))
+    gather_a.start()
+    lo_normed, lo_factor = rms(mm(lr_low[...], vso[pl.ds(0, rank)]))
+    d_lo, gain_two = rms_back(d_half, lo_normed, lo_factor, gain(2))
+    d_lo_low = d_lo.astype(BF)
+    d_lr_low = mm_nt(d_lo_low, vso[pl.ds(0, rank)]).astype(BF)
+    small(0, 0, mm_tn(lr_low[...], d_lo_low))
+    x_low = (rms(x_own[...].astype(F32))[0] * gain(0)).astype(BF)
+    small(1, 0, mm_tn(d_lr_low, x_low))
+    own_sum[...] = d_half + mm_nt(d_lr_low, vsi[:, pl.ds(0, rank)])
+    gpart[pl.ds(3, 1)] = gain_three
+    gpart[pl.ds(2, 1)] = gain_two
+    gpart[pl.ds(1, 1)] = gain_one
+    small_swap = remote(
+        small_give, small_got, misc_send.at[8], misc_recv.at[8], (1 - core, row, col)
+    )
+    small_swap.start()
+    gather_a.forward()
+    put_d.middle()
+    gather_a.finish()
+
+    loads[7].wait()
+    d_o[...] = mm_nt(dattng[...], vo[...]).astype(BF)
+    q_rows = 128
+    key_token = lax.broadcasted_iota(jnp.int32, (1, 2 * tokens), 1)
+    in_half = key_token % tokens
+    key_place = in_half // own_tokens * chunk + key_token // tokens * own_tokens + in_half % own_tokens
+    d_kv[...] = jnp.zeros(d_kv.shape, F32)
+
+    def attend(step, carry):
+        first = pl.multiple_of(step * q_rows, q_rows)
+        rows = pl.ds(first, q_rows)
+        token = first + lax.broadcasted_iota(jnp.int32, (q_rows, 1), 0)
+        q_place = token // own_tokens * chunk + half * own_tokens + token % own_tokens
+        allowed = (key_place <= q_place) & (key_place >= start[rows])
+        scores = jnp.where(allowed, mm_nt(q_low[rows], kv[0]), MASK_FILL)
+        probs = jnp.exp(scores - lse[rows])
+        d_probs = mm_nt(d_o[rows], kv[1])
+        delta = jnp.sum(probs * d_probs, axis=1, keepdims=True)
+        d_scores = (probs * (d_probs - delta)).astype(BF)
+        d_kv[0] += mm_tn(d_scores, q_low[rows])
+        d_kv[1] += mm_tn(probs.astype(BF), d_o[rows])
+        d_raw, gain_part = head_back(
+            mm(d_scores, kv[0]), raw_q[rows], head_gains[pl.ds(0, 1)], cosine[rows], sine[rows]
+        )
+        d_o[rows] = d_raw.astype(BF)
+        return carry + gain_part
+
+    gain_q = lax.fori_loop(0, tokens // q_rows, attend, jnp.zeros((1, head_dim), F32))
+
+    kv_give[...] = d_kv[1 - core].astype(BF)
+    swap_kv = remote(kv_give, kv_got, misc_send.at[9], misc_recv.at[9], (1 - core, row, col))
+    swap_kv.start()
+
+    def out_grad():
+        for part in range(2):
+            wide = pl.ds(part * (width // 2), width // 2)
+            vo[:, wide] = mm_tn(o_low[...], dattng[:, wide]).astype(BF)
+
+    put_o = RowScatter(place, by_cols(vo, block)[1], came_o, row_sems.at[3])
+    swap_kv.wait_recv()
+    theirs = pl.ds(pl.multiple_of((half ^ 1) * tokens, tokens), tokens)
+    ours = pl.ds(pl.multiple_of(half * tokens, tokens), tokens)
+    kv_x[...] = (d_kv[core, theirs] + kv_got[theirs].astype(F32)).astype(BF)
+    over_x = remote(kv_x, kv_x_got, misc_send.at[10], misc_recv.at[10], (core, row ^ 1, col))
+    over_x.start()
+    load_x = pltpu.make_async_copy(xg_in, dffg, load_sems.at[10])
+    load_x.start()
+    out_grad()
+    put_o.start()
+    loads[8].wait()
+    loads[9].wait()
+    over_x.wait_recv()
+    d_kind = d_kv[core, ours] + kv_got[ours].astype(F32) + kv_x_got[...].astype(F32)
+    kv_p = kv_got.at[pl.ds(0, tokens)]
+    kv_p[...] = d_kind.astype(BF)
+    over_p = remote(kv_p, kv_p_got, misc_send.at[11], misc_recv.at[11], (core, row, col ^ 1))
+    over_p.start()
+    put_g.middle()
+    over_p.wait()
+    d_kind = kv_p[...].astype(F32) + kv_p_got[...].astype(F32)
+    is_key = core == 0
+    d_kind_raw, gain_k = head_back(
+        d_kind,
+        raw_kv[...],
+        jnp.where(is_key, head_gains[pl.ds(1, 1)], 1.0),
+        jnp.where(is_key, cosine[...], 1.0),
+        jnp.where(is_key, sine[...], 0.0),
+    )
+    for part in range(4):
+        gpart[pl.ds(6, 1), pl.ds(part * block, head_dim)] = gain_q
+        gpart[pl.ds(6, 1), pl.ds(part * block + head_dim, head_dim)] = gain_k * jnp.where(
+            is_key, 0.5, 0.0
+        )
+    kv_p[...] = d_kind_raw.astype(BF)
+    pair_cols = pl.ds(pl.multiple_of(col % 2 * key_width, key_width), key_width)
+
+    def back_heads(target, first):
+        rows = pl.ds(first, 4 * own_tokens)
+
+        def step(index, carry):
+            cols = pl.ds(pl.multiple_of(index * block, block), block)
+            value = mm_nt(d_o[rows], vq[cols]) + mm_nt(kv_p[rows, pair_cols], vkv[cols, pair_cols])
+            target[:, cols] = value.astype(target.dtype)
+            return carry
+
+        lax.fori_loop(0, width // block, step, 0)
+
+    scatter_x = Scatter(place, own_tokens, (give, keep, got, sent, left, right), sems(3))
+    back_heads(give, away)
+    scatter_x.sibling().start()
+    back_heads(keep, home)
+    put_q = RowScatter(place, by_rows(vq, block)[1], came_q, row_sems.at[4])
+    put_kv = RowScatter(place, by_rows(pkv, block)[1], came_kv, row_sems.at[5])
+    put_s = RowScatter(place, by_cols(small_keep, block)[1], small_row, row_sems.at[6])
+
+    def query_grad():
+        load_x.wait()
+
+        def step(index, carry):
+            rows = pl.ds(pl.multiple_of(index * tile, tile), tile)
+            vq[rows] = mm_tn(dffg[:, rows], d_o[...]).astype(BF)
+            pkv[rows] = mm_tn(dffg[:, rows], kv_p[:, pair_cols]).astype(BF)
+            return carry
+
+        lax.fori_loop(0, width // tile, step, 0)
+        put_q.start()
+        put_kv.start()
+
+    def small_sum():
+        small_swap.wait_recv()
+        small_keep[...] = (small_keep[...].astype(F32) + small_got[...].astype(F32)).astype(BF)
+        put_s.start()
+
+    d_half_here = d_three_ref
+    scatter_x.run(h_two_ref, [query_grad, small_sum, put_u.middle])
+    d_xn = own_sum[...] + h_two_ref[...]
+    x_normed, x_factor = rms(x_own[...].astype(F32))
+    d_in, gain_zero = rms_back(d_xn, x_normed, x_factor, gain(0))
+    gpart[pl.ds(0, 1)] = gain_zero
+    for mask in (1, 2, 3):
+        hand_back(low_ref, y_out, mask, 0).wait_send()
+    low_ref[...] = (d_half_here[...] + d_in).astype(BF)
+    for mask in (1, 2, 3):
+        hand_back(low_ref, x_grad, mask, 4).start()
+    x_grad[row] = low_ref[:, my_cols]
+
+    gpart[pl.ds(8, 8)] = jnp.full((8, width), jnp.max(top[...]), F32)
+
+    def gain_row(mask):
+        return remote(
+            gpart.at[:, pl.ds(pl.multiple_of((row ^ mask) * block, block), block)],
+            gcame.at[mask],
+            gain_send.at[mask],
+            gain_recv.at[mask],
+            (core, row ^ mask, col),
+        )
+
+    for mask in (1, 2, 3):
+        gain_row(mask).start()
+    gcame[0] = gpart[:, my_cols]
+    for mask in (1, 2, 3):
+        gain_row(mask).wait_recv()
+    summed = gcame[0] + gcame[1] + gcame[2] + gcame[3]
+    largest = jnp.maximum(jnp.maximum(gcame[0], gcame[1]), jnp.maximum(gcame[2], gcame[3]))
+    gpart2[pl.ds(0, 8)] = summed[:8]
+    gpart2[pl.ds(8, 8)] = largest[8:]
+    me = core * 4 + col
+    members = [(other, mask) for other in (0, 1) for mask in range(4) if other or mask]
+
+    def gain_group(other, mask):
+        lane = 4 + other * 4 + mask
+        return remote(
+            gpart2,
+            gcame2.at[me],
+            gain_send.at[lane],
+            gain_recv.at[lane],
+            (core ^ other, row, col ^ mask),
+        )
+
+    for other, mask in members:
+        gain_group(other, mask).start()
+    gcame2[me] = gpart2[...]
+    put_s.middle()
+    put_kv.middle()
+    put_o.middle()
+    put_q.middle()
+
+    def deliver(lane, source, target):
+        local = pltpu.make_async_copy(source, target, done_sems.at[lane])
+        over = remote(
+            source, target, done_sems.at[8 + lane], done_sems.at[16 + lane], (1 - core, row, col)
+        )
+        local.start()
+        over.start()
+        return local, over
+
+    core_ff = pl.ds(pl.multiple_of(core * ff_part, ff_part), ff_part)
+    core_head = pl.ds(pl.multiple_of(core * head_dim, head_dim), head_dim)
+    sib_ff = pl.ds(pl.multiple_of((1 - core) * ff_part, ff_part), ff_part)
+    sib_head = pl.ds(pl.multiple_of((1 - core) * head_dim, head_dim), head_dim)
+    row_block = pl.ds(pl.multiple_of(row * block, block), block)
+    done = []
+    put_d.finish()
+    done.append(deliver(0, vd.at[:, row_block], gdown.at[core_ff]))
+    put_g.finish()
+    done.append(deliver(1, vg.at[row_block], ggate.at[:, core_ff]))
+    put_s.finish()
+
+    quarter = block // 4
+
+    def small_quarter(mask):
+        return remote(
+            small_keep.at[
+                :, pl.ds(pl.multiple_of(row * block + (col ^ mask) * quarter, quarter), quarter)
+            ],
+            small_z.at[mask],
+            misc_send.at[11 + mask],
+            misc_recv.at[11 + mask],
+            (core, row, col ^ mask),
+        )
+
+    def small_share(other, mask):
+        lane = 16 + other * 4 + mask
+        return remote(
+            kv_x.at[pl.ds(0, small_keep.shape[0]), pl.ds(0, quarter)],
+            small_a.at[core, col],
+            misc_send.at[lane],
+            misc_recv.at[lane],
+            (core ^ other, row, col ^ mask),
+        )
+
+    for mask in (1, 2, 3):
+        small_quarter(mask).start()
+    put_u.finish()
+    done.append(deliver(2, vu.at[row_block], gup.at[:, core_ff]))
+    for mask in (1, 2, 3):
+        small_quarter(mask).wait_recv()
+    small_total = small_keep[
+        :, pl.ds(pl.multiple_of(row * block + col * quarter, quarter), quarter)
+    ].astype(F32)
+    for mask in (1, 2, 3):
+        small_total = small_total + small_z[mask].astype(F32)
+    over_x.wait_send()
+    kv_x[pl.ds(0, small_keep.shape[0]), pl.ds(0, quarter)] = small_total.astype(BF)
+    for other, mask in members:
+        small_share(other, mask).start()
+    small_a[core, col] = small_total.astype(BF)
+    put_kv.finish()
+    done.append(deliver(3, pkv.at[row_block], gkv.at[core]))
+    put_o.finish()
+    done.append(deliver(4, vo.at[:, row_block], gout.at[core_head]))
+    put_q.finish()
+    done.append(deliver(5, vq.at[row_block], gq.at[:, core_head]))
+
+    for other, mask in members:
+        who = (core ^ other) * 4 + (col ^ mask)
+        lane = 4 + other * 4 + mask
+        remote(
+            gpart2, gcame2.at[who], gain_send.at[lane], gain_recv.at[lane], (core, row, col)
+        ).wait_recv()
+    total = gcame2[0]
+    for who in range(1, 8):
+        total = total + gcame2[who]
+    g_gain[...] = total[:8]
+    for who in range(8):
+        head = 2 * (who % 4) + who // 4
+        tops[pl.ds(head, 1)] = gcame2[who, pl.ds(8, 1), pl.ds(0, 128)]
+
+    for other, mask in members:
+        part = small_a.at[core ^ other, col ^ mask]
+        lane = 16 + other * 4 + mask
+        remote(part, part, misc_send.at[lane], misc_recv.at[lane], (core, row, col)).wait_recv()
+        small_share(other, mask).wait_send()
+        gain_group(other, mask).wait_send()
+    for mask in (1, 2, 3):
+        came_back(y_out, mask, 0).wait_recv()
+        came_back(x_grad, mask, 4).wait_recv()
+        hand_back(low_ref, x_grad, mask, 4).wait_send()
+        gain_row(mask).wait_send()
+        small_quarter(mask).wait_send()
+    small_swap.wait_send()
+    swap_kv.wait_send()
+    for put in (put_d, put_g, put_u, put_o, put_q, put_kv, put_s):
+        put.drain()
+    sib_targets = [
+        gdown.at[sib_ff],
+        ggate.at[:, sib_ff],
+        gup.at[:, sib_ff],
+        gkv.at[1 - core],
+        gout.at[sib_head],
+        gq.at[:, sib_head],
+    ]
+    for lane, (local, over) in enumerate(done):
+        local.wait()
+        over.wait_send()
+        target = sib_targets[lane]
+        remote(
+            target, target, done_sems.at[8 + lane], done_sems.at[16 + lane], (core, row, col)
+        ).wait_recv()
+
+
+def run_backward(small_args, big_args):
+    x_own, per_in, head_gains = small_args[0], small_args[2], small_args[4]
+    own, width = x_own.shape
+    block = width // 4
+    gate = big_args[2]
+    tokens, ff_part = gate.shape
+    head_dim = head_gains.shape[1]
+    rank = small_args[6].shape[1]
+    small_rows = small_args[19].shape[0]
+    vm = pl.BlockSpec(memory_space=pltpu.VMEM)
+    hbm = pl.BlockSpec(memory_space=pl.ANY)
+    shape = jax.ShapeDtypeStruct
+    vmem = pltpu.VMEM
+    dma = pltpu.SemaphoreType.DMA
+    outs = [
+        shape((4, own, block), BF),
+        shape((4, own, block), BF),
+        shape((8, block), F32),
+        shape((8, 128), F32),
+        shape((2, 4, small_rows, block // 4), BF),
+        shape((block, 2 * head_dim), BF),
+        shape((2, block, head_dim // 2), BF),
+        shape((2 * head_dim, block), BF),
+        shape((block, 2 * ff_part), BF),
+        shape((block, 2 * ff_part), BF),
+        shape((2 * ff_part, block), BF),
+        shape((6, block // 2, ff_part), BF),
+        shape((6, block // 2, ff_part), BF),
+        shape((6, ff_part // 2, block), BF),
+    ]
+    scratch = [
+        vmem((width, head_dim), BF),
+        vmem((width, head_dim), BF),
+        vmem((head_dim, width), BF),
+        vmem((width, ff_part), BF),
+        vmem((width, ff_part), BF),
+        vmem((ff_part, width), BF),
+        vmem((tokens, width), BF),
+        vmem((tokens, ff_part), BF),
+        vmem((tokens, ff_part), BF),
+        vmem((tokens, ff_part), BF),
+        vmem((tokens, width), BF),
+        vmem((tokens, width), BF),
+        vmem((tokens, ff_part), BF),
+        vmem((tokens, ff_part), BF),
+        vmem((4 * own, width), BF),
+        vmem((4 * own, width), F32),
+        vmem((4 * own, width), BF),
+        vmem((4, own, width), BF),
+        vmem((3, own, width), BF),
+        vmem((3, own, width), BF),
+        vmem((own, width), F32),
+        vmem((own, width), F32),
+        vmem((own, width), F32),
+        vmem((own, width), BF),
+        vmem((16, width), F32),
+        vmem((4, 16, block), F32),
+        vmem((16, block), F32),
+        vmem((8, 16, block), F32),
+        vmem((small_rows, width), BF),
+        vmem((small_rows, width), BF),
+        vmem((small_rows, width), BF),
+        vmem((6, small_rows // 2, block), BF),
+        vmem((4, small_rows, block // 4), BF),
+        vmem((tokens, head_dim), BF),
+        vmem((2, 2 * tokens, head_dim), F32),
+        vmem((2 * tokens, head_dim), BF),
+        vmem((2 * tokens, head_dim), BF),
+        vmem((tokens, head_dim), BF),
+        vmem((tokens, head_dim), BF),
+        vmem((tokens, head_dim), BF),
+        vmem((width, head_dim // 2), BF),
+        vmem((6, block // 2, head_dim), BF),
+        vmem((6, block // 2, head_dim // 2), BF),
+        vmem((6, head_dim // 2, block), BF),
+        vmem((2, block // 2, ff_part), BF),
+        vmem((2, ff_part // 2, block), BF),
+        dma((2,)),
+        dma((11,)),
+        dma((7, 12)),
+        dma((4, 8)),
+        dma((4, 8)),
+        dma((4, 4)),
+        dma((4, 4)),
+        dma((24,)),
+        dma((24,)),
+        dma((12,)),
+        dma((12,)),
+        dma((24,)),
+    ]
+    return pl.pallas_call(
+        backward_kernel,
+        out_shape=outs,
+        in_specs=[vm] * 20 + [hbm] * 11,
+        out_specs=[vm] * 5 + [hbm] * 9,
+        scratch_shapes=scratch,
+        compiler_params=pltpu.CompilerParams(
+            collective_id=1, has_side_effects=True, vmem_limit_bytes=VMEM_BYTES
+        ),
+        cost_estimate=pl.CostEstimate(
+            flops=4 * 10**10, bytes_accessed=10**8, transcendentals=2 * 10**6
+        ),
+    )(*small_args, *big_args)
 
 
 def body_pair(
@@ -1219,6 +2025,7 @@
     small_out = jnp.concatenate([laurel_right, per_proj], axis=0)
     (
         x_own,
+        g_own,
         gains,
         x_all,
         raw_q,
@@ -1245,6 +2052,7 @@
         small_out_all,
     ) = run_forward(
         layer_in.reshape(rows, own_tokens, -1),
+        out_grad.reshape(rows, own_tokens, -1),
         norm_gains,
         w_query,
         w_kv,
@@ -1261,153 +2069,66 @@
         ),
         head_gains,
     )
-    w_gu = jnp.concatenate([w_g, w_u], axis=1)
-    l_left, p_gate = small_in_all[:, :rank], small_in_all[:, 2 * rank :]
-    l_right, p_proj = small_out_all[:rank], small_out_all[rank:]
-    inputs = x_own.astype(jnp.float32)
-    grad_top = to_owner(out_grad).astype(jnp.float32)
-    per_input = per_layer_in.reshape(rows, own_tokens, -1)[row].astype(jnp.float32)
-    x_normed, x_factor = rms(inputs)
-    x_norm = x_normed * gains[0]
-    x_low = x_norm.astype(jnp.bfloat16)
-
-    def head_prep(raw_part, gain_vec):
-        return rotate(head_norm(raw_part, gain_vec), cosine_table, sine_table)
-
-    other_kv = swapped(raw_kv, "seq", 0)
-    raw_k = jnp.where(core == 0, raw_kv, other_kv)
-    raw_v = jnp.where(core == 0, other_kv, raw_kv)
-    other_w = swapped(w_kv_all, "seq", 0)
-    w_heads = jnp.concatenate(
-        [w_q, jnp.where(core == 0, w_kv_all, other_w), jnp.where(core == 0, other_w, w_kv_all)], axis=1
-    )
-    q_rot, query_back = jax.vjp(head_prep, raw_q, head_gains[0])
-    k_rot, key_back = jax.vjp(head_prep, raw_k, head_gains[1])
-    v_rot, value_back = jax.vjp(lambda part: head_norm(part, 1.0), raw_v)
-    keys, values = kv[0], kv[1]
-    scores = jnp.where(allowed, mm_nt(q_low, keys), MASK_FILL)
-    probs = jnp.exp(scores - lse)
-    probs_low = probs.astype(jnp.bfloat16)
-    attn_normed, attn_factor = rms(attn_val)
-    lo_normed, lo_factor = rms(mm(lr_low, l_right))
-    h_two = (inputs + attn_normed * gains[1] + (x_norm + lo_normed * gains[2])) * ROOT_HALF
-    f_normed, f_factor = rms(h_two)
-
-    def geglu(gate_part, up_part):
-        return jax.nn.gelu(gate_part, approximate=True) * up_part
-
-    hidden, geglu_back = jax.vjp(geglu, gate_val, up_val)
-    ff_normed, ff_factor = rms(ff_val)
-    h_three = h_two + ff_normed * gains[4]
-    h_low = h_three.astype(jnp.bfloat16)
-
-    def per_mix(gate_part):
-        return jax.nn.gelu(gate_part, approximate=True) * per_input
-
-    gp_val, per_back = jax.vjp(per_mix, mm(h_low, p_gate))
-    gp_low = gp_val.astype(jnp.bfloat16)
-    pp_normed, pp_factor = rms(mm(gp_low, p_proj))
-    layer_out = from_owner((h_three + pp_normed * gains[5]).astype(jnp.bfloat16), seq_count)
-
-    d_pp, gain_five = rms_back(grad_top, pp_normed, pp_factor, gains[5])
-    d_pp_low = d_pp.astype(jnp.bfloat16)
-    g_per_proj = mm_tn(gp_low, d_pp_low)
-    (d_pg,) = per_back(mm_nt(d_pp_low, p_proj))
-    d_pg_low = d_pg.astype(jnp.bfloat16)
-    g_per_gate = mm_tn(h_low, d_pg_low)
-    d_three = grad_top + mm_nt(d_pg_low, p_gate)
-    d_ff, gain_four = rms_back(d_three, ff_normed, ff_factor, gains[4])
-    d_ff_all = group_gather(d_ff.astype(jnp.bfloat16))
-    d_hidden = mm_nt(d_ff_all, w_d)
-    d_gate, d_up = geglu_back(d_hidden)
-    d_gu = jnp.concatenate([d_gate, d_up], axis=1).astype(jnp.bfloat16)
-    d_f = group_scatter(mm_nt(d_gu, w_gu))
-    g_down = both_cores(scatter_rows(mm_tn(hid_low, d_ff_all), 1), 0)
-    g_gu = scatter_rows(mm_tn(f_all, d_gu), 0)
-    g_gate, g_up = both_cores(g_gu[:, :ff_part], 1), both_cores(g_gu[:, ff_part:], 1)
-    d_f, gain_three = rms_back(d_f, f_normed, f_factor, gains[3])
-    d_half = (d_three + d_f) * ROOT_HALF
-    d_lo, gain_two = rms_back(d_half, lo_normed, lo_factor, gains[2])
-    d_attn, gain_one = rms_back(d_half, attn_normed, attn_factor, gains[1])
-    d_attn_all = group_gather(d_attn.astype(jnp.bfloat16))
-    d_lo_low = d_lo.astype(jnp.bfloat16)
-    g_right = mm_tn(lr_low, d_lo_low)
-    d_lr_low = mm_nt(d_lo_low, l_right).astype(jnp.bfloat16)
-    g_left = mm_tn(x_low, d_lr_low)
-
-    d_o_low = mm_nt(d_attn_all, w_o).astype(jnp.bfloat16)
-    g_out = both_cores(scatter_rows(mm_tn(o_low, d_attn_all), 1), 0)
-    d_probs = mm_nt(d_o_low, values)
-    delta = jnp.sum(probs * d_probs, axis=1, keepdims=True)
-    d_scores = (probs * (d_probs - delta)).astype(jnp.bfloat16)
-    d_query = mm(d_scores, keys)
-    d_kv = jnp.concatenate([mm_tn(d_scores, q_low), mm_tn(probs_low, d_o_low)], axis=1)
-    d_kv = d_kv.reshape(2, group_tokens, -1)
-    d_kv = d_kv[half] + swapped(d_kv[half ^ 1], "row", 0)
-    d_kv = lax.psum(d_kv, "seq")
-    d_kv = d_kv + swapped(d_kv, "col", 0)
-    d_q_raw, d_q_gain = query_back(d_query)
-    d_k_raw, d_k_gain = key_back(d_kv[:, :head_dim])
-    (d_v_raw,) = value_back(d_kv[:, head_dim:])
-    d_kv_low = jnp.concatenate([d_k_raw, d_v_raw], axis=1).astype(jnp.bfloat16)
-    kv_offset = core * head_dim + col % 2 * key_width
-    d_heads = jnp.concatenate(
-        [
-            d_q_raw.astype(jnp.bfloat16),
-            lax.dynamic_slice_in_dim(d_kv_low, kv_offset, key_width, 1),
-        ],
-        axis=1,
-    )
-    w_back = jnp.concatenate(
-        [
-            w_heads[:, :head_dim],
-            lax.dynamic_slice_in_dim(w_heads, head_dim + kv_offset, key_width, 1),
-        ],
-        axis=1,
-    )
-    d_xn = group_scatter(mm_nt(d_heads, w_back)) + mm_nt(d_lr_low, l_left)
-    g_heads = scatter_rows(mm_tn(x_all, d_heads), 0)
-    g_query = both_cores(g_heads[:, :head_dim], 1)
-    g_kv = both_cores(g_heads[:, head_dim:], 1)
-    d_in, gain_zero = rms_back(d_half + d_xn, x_normed, x_factor, gains[0])
-    grad_in = from_owner((d_half + d_in).astype(jnp.bfloat16), seq_count)
-
-    g_gains = jnp.concatenate(
-        [gain_zero, gain_one, gain_two, gain_three, gain_four, gain_five], axis=0
-    )
-    g_small_in = lax.psum_scatter(
-        jnp.concatenate([g_left, g_per_gate], axis=1), "row", scatter_dimension=0, tiled=True
-    )
-    g_small_out = lax.psum_scatter(
-        jnp.concatenate([g_right, g_per_proj, g_gains], axis=0),
-        "row",
-        scatter_dimension=1,
-        tiled=True,
-    )
-    g_small_in, g_small_out = lax.psum((g_small_in, g_small_out), ("seq", "col"))
-    g_head_gains = lax.psum(jnp.stack([d_q_gain, d_k_gain * 0.25]), ("seq", "row", "col"))
-    top = lax.pmax(top_tile[0, 0], "row")
-    tops = lax.all_gather(top, ("seq", "col"))
-    logit_top = tops.reshape(cores, cols).T.reshape(-1)
+    half_table = head_dim // 2
+    (
+        y_out,
+        x_grad,
+        g_gain,
+        tops,
+        small_sums,
+        g_q,
+        g_kv,
+        g_o,
+        g_g,
+        g_u,
+        g_d,
+        *came,
+    ) = run_backward(
+        (
+            x_own,
+            g_own,
+            per_layer_in.reshape(rows, own_tokens, -1),
+            gains,
+            head_gains,
+            attn_val,
+            lr_low,
+            ff_val,
+            raw_q,
+            raw_kv,
+            q_low,
+            kv,
+            lse,
+            top_tile,
+            o_low,
+            cosine_table[:, :half_table],
+            sine_table[:, :half_table],
+            start[:, None],
+            small_in_all,
+            small_out_all,
+        ),
+        (x_all, f_all, gate_val, up_val, hid_low, w_q, w_kv_all, w_o, w_g, w_u, w_d),
+    )
+    sums_a = small_sums[0].transpose(1, 0, 2).reshape(small_sums.shape[2], -1).astype(F32)
+    sums_b = small_sums[1].transpose(0, 2, 1).reshape(-1, small_sums.shape[2]).astype(F32)
+    logit_top = tops[:, 0]
     clip_factor = jnp.sqrt(CLIP_LEVEL / jnp.maximum(logit_top, CLIP_LEVEL))
     clipped_gains = clip_factor[None, :, None] * head_gains[:, None, :]
-    proj_rows = rank + per_proj.shape[0]
     return (
-        layer_out,
-        grad_in,
-        g_query,
-        g_kv[:, :key_width],
-        g_kv[:, key_width:],
-        g_out,
-        g_gate,
-        g_up,
-        g_down,
-        g_small_in[:, :rank],
-        g_small_out[:rank],
-        g_small_in[:, rank:],
-        g_small_out[rank:proj_rows],
-        g_small_out[proj_rows:],
-        g_head_gains,
+        y_out.reshape(layer_in.shape),
+        x_grad.reshape(layer_in.shape),
+        g_q.astype(F32),
+        g_kv[0].astype(F32),
+        g_kv[1].astype(F32),
+        g_o.astype(F32),
+        g_g.astype(F32),
+        g_u.astype(F32),
+        g_d.astype(F32),
+        sums_b[:, :rank],
+        sums_a[:rank],
+        sums_b[:, rank:],
+        sums_a[rank:],
+        g_gain[:6],
+        g_gain[6].reshape(head_gains.shape),
         clipped_gains,
     )
 

time: 956 us -> 504 us (0.53); the launches traced: 945 us -> 503 us
  waiting for transfers between devices: 493 us -> 0 us
  Pallas kernels: 213 us -> 471 us
  blocking collectives: 65.6 us -> 0 us
  matrix products: 56.1 us -> 0 us
  local copies, waits for them, and re-layouts: 52 us -> 9.61 us
  starting transfers between devices: 16.5 us -> 0 us
  between operations: 15.3 us -> 0.8 us
  other arithmetic: 33.8 us -> 21.5 us
    reduce_scatter x8 -> x0, waiting for transfers between devices: 275 us -> none  [the longest x4 154 us: scatter_rows(): lax.psum_scatter(values.astype(jnp.bfloat16), 'row', scatter_dimension=ax...]
    pallas_call x1 -> x2, Pallas kernels: 213 us -> 471 us  [the longest x1 256 us: run_backward(): pl.pallas_call(backward_kernel, out_shape=outs, in_specs=[vm] * 20 + [hbm...]
    all_gather x7 -> x0, waiting for transfers between devices: 96 us -> none  [the longest x2 56.7 us: group_gather(): return lax.all_gather(values, ('seq', 'col'), axis=0, tiled=True)]
    psum x2 -> x0, waiting for transfers between devices: 70.2 us -> none  [the longest x1 62 us: body_pair(): lax.psum((g_small_in, g_small_out), ('seq', 'col'))]
    dot_general x24 -> x0, matrix products: 56.1 us -> none  [the longest x10 26.4 us: mm_tn(): lax.dot_general(left_side, right_side, (((0,), (0,)), ((), ())), preferre...]
    ppermute x4 -> x0, waiting for transfers between devices: 43.5 us -> none  [swapped(): return lax.ppermute(value, axis, pairs)]
    psum x1 -> x0, blocking collectives: 35.8 us -> none  [body_pair(): lax.psum(jnp.stack([d_q_gain, d_k_gain * 0.25]), ('seq', 'row', 'col'))]
    unnamed x1 -> x0, blocking collectives: 19.3 us -> none
  transfers between devices with their start and end apart: 24 -> 0, of which waited for: 16 -> 0; matrix products, arithmetic and copies ran while one was open for 8% -> 0% of each run, Pallas kernels for 23% -> 0%
where the time goes in v2:
time: 504 us; the launch traced here: 503 us
  Pallas kernels  471 us (93%)
  other arithmetic  21.5 us (4%)
  local copies, waits for them, and re-layouts  9.61 us (2%)
    pallas_call x1, Pallas kernels, run_backward(): pl.pallas_call(backward_kernel, out_shape=outs, in_specs=[vm] * 20 + [hbm...  256 us
    pallas_call x1, Pallas kernels, run_forward(): pl.pallas_call(forward_kernel, out_shape=outs, in_specs=[vm, vm, vm, hbm,...  215 us

profile of v2, /device:TPU:1, one launch (start us, length us, event | category | flops | bytes accessed | tf_op | source)
XLA Modules:
  0.0 502.9 jit_solution(8798739843151224497)
XLA Ops:
  0.6 0.0 copy-start
  0.7 0.6 copy-done
  1.3 0.1 multiply_reduce_fusion
  1.5 0.1 pad.3.clone
  1.6 0.1 select_reduce_fusion
  1.7 1.6 broadcast_select_fusion.w_kv
  3.2 1.0 copy.43
  4.2 1.8 pad_maximum_fusion.small_in
  6.0 0.9 copy.44.start
  6.8 1.7 pad_maximum_fusion.1.small_out
  8.5 1.8 multiply_sine_fusion
  10.3 215.4 %shard_map.288 = (bf16[64,2048]{1,0:T(8,128)(2,1)}, bf16[64,2048]{1,0:T(8,128)(2,1)}, f32[8,2048]{1,0:T(8,128)}, bf16[512,2048]{1,0:T(8,128)(2,1)}, f32[512,256]...) custom-call(bf16[4,64,512]{2,1,0:T(8,128)(2,1)} %bitcast.42, ...), custom_call_target="tpu_custom_call" | custom-call | flops 20000000000 | bytes 50000000 | tf_op jit(solution)/shard_map/pallas_call | solution.py:1167
  225.8 0.0 copy-start.10
  225.8 255.6 %shard_map.289 = (bf16[4,64,512]{2,1,0:T(8,128)(2,1)}, bf16[4,64,512]{2,1,0:T(8,128)(2,1)}, f32[8,512]{1,0:T(8,128)}, f32[8,128]{1,0:T(8,128)}, bf16[2,4,320,128...) custom-call(bf16[64,2048]{1,0:T(8,128)(2,1)} %get-tuple-element.53.x, ...), custom_call_target="tpu_custom_call" | custom-call | flops 40000000000 | bytes 100000000 | tf_op jit(solution)/shard_map/pallas_call | solution.py:1955
  481.4 0.0 copy-start.6
  481.4 0.0 copy-start.5
  481.4 0.9 sqrt_reduce_fusion
  482.3 0.7 slice_reduce_fusion
  483.0 0.6 reshape_squeeze.3
  483.6 0.0 copy-done.10
  483.6 0.7 broadcast_multiply_fusion
  484.3 1.8 bitcast_convert_fusion
  486.1 2.1 convert_element_type.58
  488.2 0.0 copy-done.6
  488.2 1.1 convert_element_type.63
  489.3 0.0 copy-done.5
  489.3 0.1 convert_bitcast_fusion.1
  489.4 0.1 copy.55
  489.5 0.7 slice.52
  490.2 0.0 copy-start.4
  490.2 1.0 copy.49
  491.2 0.7 copy_bitcast_fusion.1
  491.9 0.2 copy.48
  492.1 1.0 copy.50
  493.1 0.0 copy-done.4
  493.1 2.5 convert_element_type.64
  495.7 0.0 copy-done.3
  495.7 2.5 convert_element_type.65
  498.2 0.0 copy-done.2
  498.2 0.0 copy-start.1
  498.2 2.6 convert_element_type.66
  500.8 0.0 copy-done.8
  500.8 0.7 copy.59
  501.6 0.0 copy-done.7
  501.6 0.7 copy.60
  502.3 0.0 copy-done.9
  502.3 0.6 copy.61
  502.9 0.0 copy-done.1
  (12 shorter events, 0.1 us)
Async XLA Ops:
  0.6 0.7 copy-start
  225.8 257.8 %copy-start.10 = (f32[2,256]{1,0:T(2,128)S(1)}, f32[2,256]{1,0:T(2,128)}, u32[]{:S(2)}) copy-start(f32[2,256]{1,0:T(2,128)} %head_gains.3) | copy-start | bytes 6148
  481.4 6.9 %copy-start.6 = (bf16[512,512]{1,0:T(8,128)(2,1)S(1)}, bf16[512,512]{1,0:T(8,128)(2,1)}, u32[]{:S(2)}) copy-start(bf16[512,512]{1,0:T(8,128)(2,1)} %get-tuple-element.83) | copy-start | bytes 1572868
  481.4 8.0 %copy-start.5 = (bf16[2,4,320,128]{3,2,1,0:T(8,128)(2,1)S(1)}, bf16[2,4,320,128]{3,2,1,0:T(8,128)(2,1)}, u32[]{:S(2)}) copy-start(bf16[2,4,320,128]{3,2,1,0:T(8,128)(2,1)} %get-tuple-element.87) | copy-start | bytes 1966084
  490.2 2.9 copy-start.4
  493.1 2.5 copy-start.3
  495.7 2.5 copy-start.2
  498.2 2.6 copy-start.8
  498.2 3.3 copy-start.7
  498.2 4.0 copy-start.9
  498.2 4.6 copy-start.1

commit v3 on v2

--- a/solution.py
+++ b/solution.py
@@ -542,8 +542,9 @@
 
         self.to_sibling(col).start()
 
-    def forward(self):
+    def forward(self, work=()):
         col = self.col
+        work = list(work)
         for dist in (1, 2, 3):
 
             @pl.when(col >= dist)
@@ -577,6 +578,9 @@
                         self.to_left(dist).start()
 
                 self.to_sibling(col + dist).start()
+
+            if work:
+                work.pop(0)()
 
     def finish(self):
         for col in range(4):
@@ -747,6 +751,22 @@
     return block, halves
 
 
+def by_core_rows(core):
+    def split(buf, block_rows):
+        own = block_rows // 2
+
+        def piece(index, part, count):
+            first = index * block_rows + core * own + part * (own // count)
+            return buf.at[pl.ds(pl.multiple_of(first, own // count), own // count)]
+
+        return (
+            lambda index: piece(index, 0, 1),
+            lambda index: [piece(index, part, 2) for part in range(2)],
+        )
+
+    return split
+
+
 def by_cols(buf, block_cols):
     rows = buf.shape[0] // 2
 
@@ -785,8 +805,10 @@
     w_gate,
     w_up,
     w_down,
-    small_in,
-    small_out,
+    laurel_left,
+    laurel_right,
+    per_gate,
+    per_proj,
     cosine,
     sine,
     start,
@@ -794,7 +816,6 @@
     x_own,
     g_own,
     gains,
-    xg,
     raw_q,
     raw_kv,
     q_low,
@@ -804,19 +825,22 @@
     o_low,
     attn_val,
     lr_low,
-    fg,
-    gate,
-    up,
-    hid,
     ff_val,
+    vll,
+    vlr,
+    vpg,
+    vpp,
     wq_all,
     wkv_all,
     wo_all,
     wg_all,
     wu_all,
     wd_all,
-    si_all,
-    so_all,
+    xg_all,
+    fg_all,
+    gate_all,
+    up_all,
+    turned_all,
     w_kv_pair,
     gains_pad,
     vq,
@@ -825,8 +849,12 @@
     vg,
     vu,
     vd,
-    vsi,
-    vso,
+    xg,
+    fg,
+    gate,
+    up,
+    hid,
+    turned,
     give,
     keep,
     got,
@@ -906,24 +934,70 @@
     pair.start()
     w_kv_pair[:, pair_cols] = w_kv[...]
 
-    def rows_of(array, source, buf, lane, split=by_rows, size=None):
+    lanes = iter(range(32))
+
+    def rows_of(source, buf, split=by_rows, size=block):
         block_of, halves_of = split(buf, size)
-        return RowGather(place, source, block_of, halves_of, row_sems.at[lane])
-
+        return RowGather(place, source, block_of, halves_of, row_sems.at[next(lanes)])
+
+    tile = 256
     core_head = pl.ds(pl.multiple_of(core * head_dim, head_dim), head_dim)
-    core_ff = pl.ds(pl.multiple_of(core * ff_part, ff_part), ff_part)
-    get_q = rows_of(0, w_query.at[:, core_head], vq, 0, by_rows, block)
-    get_kv = rows_of(0, w_kv_pair, vkv, 1, by_rows, block)
-    get_o = rows_of(0, w_out.at[core_head], vo, 2, by_cols, block)
-    get_g = rows_of(0, w_gate.at[:, core_ff], vg, 3, by_rows, block)
-    get_u = rows_of(0, w_up.at[:, core_ff], vu, 4, by_rows, block)
-    get_d = rows_of(0, w_down.at[core_ff], vd, 5, by_cols, block)
-    get_si = rows_of(0, small_in, vsi, 6, by_rows, block)
-    get_so = rows_of(0, small_out, vso, 7, by_cols, block)
+
+    def core_tile(index):
+        return pl.ds(pl.multiple_of(core * ff_part + index * tile, tile), tile)
+
+    get_q = rows_of(w_query.at[:, core_head], vq)
+    get_kv = rows_of(w_kv_pair, vkv)
+    get_o = rows_of(w_out.at[core_head], vo, by_cols)
+    get_laurel = [rows_of(laurel_left, vll), rows_of(laurel_right, vlr, by_cols)]
+    per_rows, per_cols = per_gate.shape[0] // 2, per_proj.shape[0] // 2
+    own_rows = pl.ds(pl.multiple_of(core * per_rows, per_rows), per_rows)
+    own_cols = pl.ds(pl.multiple_of(core * per_cols, per_cols), per_cols)
+    get_per = [
+        rows_of(per_gate.at[own_rows], vpg, by_core_rows(core)),
+        rows_of(per_proj.at[own_cols], vpp.at[own_cols], by_cols),
+    ]
+    tiles = ff_part // tile
+    get_gu = [
+        [
+            rows_of(whole.at[:, core_tile(index)], buf.at[:, pl.ds(index * tile, tile)])
+            for whole, buf in ((w_gate, vg), (w_up, vu))
+        ]
+        for index in range(tiles)
+    ]
+    half_ff = ff_part // 2
+    get_d = [
+        rows_of(
+            w_down.at[pl.ds(pl.multiple_of(core * ff_part + part * half_ff, half_ff), half_ff)],
+            vd.at[pl.ds(part * half_ff, half_ff)],
+            by_cols,
+        )
+        for part in range(2)
+    ]
+
+    def per_parts(which, lane):
+        parts = [
+            vpg.at[pl.ds(pl.multiple_of(index * block + which * per_rows, per_rows), per_rows)]
+            for index in range(4)
+        ]
+        parts.append(vpp.at[pl.ds(pl.multiple_of(which * per_cols, per_cols), per_cols)])
+        return list(enumerate(parts, lane))
+
+    def begin(jobs):
+        for job in jobs:
+            job.start()
+
+    def push(jobs):
+        for job in jobs:
+            job.forward()
+
+    def complete(jobs):
+        for job in jobs:
+            job.finish()
+
     get_q.start()
     pair.wait_recv()
     get_kv.start()
-    get_o.start()
 
     for mask in (1, 2, 3):
         remote(
@@ -951,18 +1025,15 @@
     sems = lambda lane: (z_send.at[lane], z_recv.at[lane], s_send.at[lane], s_recv.at[lane])
     gather_x = Gather(place, xg, own_tokens, sems(0))
     gather_x.start()
-    get_q.forward()
-    get_kv.forward()
-    get_o.forward()
-    get_si.start()
-    get_so.start()
-    get_g.start()
-    for mask in (1, 2, 3):
-        hand_grad(mask).start()
-    gather_x.forward()
+    gather_x.forward(
+        [
+            lambda: begin([get_o] + get_laurel),
+            lambda: push([get_q, get_kv]),
+            lambda: push([get_o] + get_laurel),
+        ]
+    )
     gather_x.finish()
-    get_q.finish()
-    get_kv.finish()
+    complete([get_q, get_kv])
 
     raw_q[...] = mm(xg[...], vq[...])
     raw_kv[...] = mm(xg[...], vkv[...])
@@ -984,6 +1055,8 @@
     to_s = remote(here, here, misc_send.at[9], misc_recv.at[9], (1 - core, row, col))
     to_x.start()
     to_s.start()
+    begin(get_gu[0])
+    begin(get_gu[1])
     came = kv_part(core, half ^ 1)
     remote(here, came, misc_send.at[8], misc_recv.at[8], (core, row, col)).wait_recv()
     on_s = remote(came, came, misc_send.at[10], misc_recv.at[10], (1 - core, row, col))
@@ -1016,10 +1089,6 @@
         return carry
 
     lax.fori_loop(0, tokens // q_rows, attend, 0)
-    get_si.forward()
-    get_so.forward()
-    get_g.forward()
-    get_u.start()
     get_o.finish()
 
     away = pl.multiple_of((1 - core) * 4 * own_tokens, 4 * own_tokens)
@@ -1037,42 +1106,51 @@
 
     project(o_low, vo, give, away)
     scatter.sibling().start()
+    push(get_gu[0])
+    begin(get_gu[2])
     project(o_low, vo, keep, home)
-    scatter.run(attn_val)
-
-    get_si.finish()
-    get_so.finish()
+    scatter.run(
+        attn_val,
+        [lambda: None, lambda: push(get_gu[1]), lambda: begin(get_gu[3])],
+    )
+
+    complete(get_laurel)
     inputs, x_norm = own_norm()
     attn_normed = rms(attn_val[...])[0]
-    rank = lr_low.shape[1]
-    lr_low[...] = mm(xg[mine], vsi[:, pl.ds(0, rank)]).astype(BF)
-    lo_normed = rms(mm(lr_low[...], vso[pl.ds(0, rank)]))[0]
+    lr_low[...] = mm(xg[mine], vll[...]).astype(BF)
+    lo_normed = rms(mm(lr_low[...], vlr[...]))[0]
     h_two = (
         inputs + attn_normed * gains[pl.ds(1, 1)] + (x_norm + lo_normed * gains[pl.ds(2, 1)])
     ) * ROOT_HALF
     fg[mine] = (rms(h_two)[0] * gains[pl.ds(3, 1)]).astype(BF)
     gather_f = Gather(place, fg, own_tokens, sems(2))
     gather_f.start()
-    get_u.forward()
-    get_d.start()
-    get_g.finish()
-    gather_f.forward()
+    gather_f.forward(
+        [
+            lambda: push(get_gu[2]),
+            lambda: None,
+            lambda: None,
+        ]
+    )
     gather_f.finish()
-    get_u.finish()
-
-    tile = 256
-
-    def units(index, carry):
-        cols = pl.ds(pl.multiple_of(index * tile, tile), tile)
+
+    def unit_tile(index):
+        complete(get_gu[index])
+        cols = pl.ds(index * tile, tile)
         bent, slope = gelu_both(mm(fg[...], vg[:, cols]))
         up_part = mm(fg[...], vu[:, cols])
         gate[:, cols] = (up_part * slope).astype(BF)
         up[:, cols] = bent.astype(BF)
         hid[:, cols] = (bent * up_part).astype(BF)
-        return carry
-
-    lax.fori_loop(0, ff_part // tile, units, 0)
-    get_d.forward()
+
+    for index in range(tiles):
+        if index == 1:
+            push(get_gu[3])
+            begin(get_d)
+        unit_tile(index)
+    turned[...] = hid[...].T
+    for job in get_d:
+        job.forward()
     keep_weights = [
         pltpu.make_async_copy(source, target, out_sems.at[lane])
         for lane, (source, target) in enumerate(
@@ -1083,19 +1161,36 @@
                 (vg, wg_all),
                 (vu, wu_all),
                 (vd, wd_all),
-                (vsi, si_all),
-                (vso, so_all),
+                (xg, xg_all),
+                (fg, fg_all),
+                (gate, gate_all),
+                (up, up_all),
+                (turned, turned_all),
             ]
         )
     ]
-    get_d.finish()
+    begin(get_per)
+    for mask in (1, 2, 3):
+        hand_grad(mask).start()
+    complete(get_d)
     for copy in keep_weights:
         copy.start()
     scatter_ff = Scatter(place, own_tokens, (give2, keep2, got2, sent2, left2, right2), sems(3))
     project(hid, vd, give2, away)
     scatter_ff.sibling().start()
     project(hid, vd, keep2, home)
-    scatter_ff.run(ff_val)
+    scatter_ff.run(ff_val, [lambda: None, lambda: push(get_per)])
+    complete(get_per)
+    share = [
+        remote(part, part, misc_send.at[lane], misc_recv.at[lane], (1 - core, row, col))
+        for lane, part in per_parts(core, 16)
+    ]
+    for copy in share:
+        copy.start()
+    for lane, part in per_parts(1 - core, 16):
+        remote(part, part, misc_send.at[lane], misc_recv.at[lane], (core, row, col)).wait_recv()
+    for copy in share:
+        copy.wait_send()
 
     for mask in (1, 2, 3):
         hand_over(mask).wait_send()
@@ -1116,12 +1211,13 @@
         copy.wait()
 
 
-def run_forward(x_in, g_in, gains_in, w_query, w_kv, w_out, w_gate, w_up, w_down, small_in, small_out, tables, head_gains):
+def run_forward(x_in, g_in, gains_in, weights_in, tables, head_gains):
     cosine, sine, start = tables
+    w_gate, laurel_left, per_gate, per_proj = (weights_in[i] for i in (3, 6, 8, 9))
     block = x_in.shape[2]
     own, width = x_in.shape[1], 4 * block
     tokens, head_dim, ff_part = 8 * own, head_gains.shape[1], w_gate.shape[1] // 2
-    rank = small_in.shape[1] - small_out.shape[0]
+    rank = laurel_left.shape[1]
     vm = pl.BlockSpec(memory_space=pltpu.VMEM)
     hbm = pl.BlockSpec(memory_space=pl.ANY)
     shape = jax.ShapeDtypeStruct
@@ -1132,14 +1228,17 @@
         (width, ff_part),
         (width, ff_part),
         (ff_part, width),
-        (width, small_in.shape[1]),
-        (small_out.shape[0], width),
+    ]
+    acts = [
+        (tokens, width),
+        (tokens, width),
+        (tokens, ff_part),
+        (tokens, ff_part),
     ]
     outs = [
         shape((own, width), BF),
         shape((own, width), BF),
         shape((8, width), F32),
-        shape((tokens, width), BF),
         shape((tokens, head_dim), F32),
         shape((tokens, head_dim), F32),
         shape((tokens, head_dim), BF),
@@ -1149,12 +1248,12 @@
         shape((tokens, head_dim), BF),
         shape((own, width), F32),
         shape((own, rank), BF),
-        shape((tokens, width), BF),
-        shape((tokens, ff_part), BF),
-        shape((tokens, ff_part), BF),
-        shape((tokens, ff_part), BF),
         shape((own, width), F32),
-    ] + [shape(size, BF) for size in weights]
+        shape((width, rank), BF),
+        shape((rank, width), BF),
+        shape((width, per_gate.shape[1]), BF),
+        shape((per_proj.shape[0], width), BF),
+    ] + [shape(size, BF) for size in weights + acts + [(ff_part, tokens)]]
     scatter_bufs = [
         pltpu.VMEM((4 * own, width), BF),
         pltpu.VMEM((4 * own, width), F32),
@@ -1167,26 +1266,27 @@
     return pl.pallas_call(
         forward_kernel,
         out_shape=outs,
-        in_specs=[vm, vm, vm, hbm, vm, hbm, hbm, hbm, hbm, hbm, hbm, vm, vm, vm, vm],
-        out_specs=[vm] * 18 + [hbm] * 8,
+        in_specs=[vm, vm, vm, hbm, vm] + [hbm] * 8 + [vm] * 4,
+        out_specs=[vm] * 17 + [hbm] * 11,
         scratch_shapes=[pltpu.VMEM((block, head_dim), BF), pltpu.VMEM((8, block), F32)]
-        + [pltpu.VMEM(size, BF) for size in weights]
+        + [pltpu.VMEM(size, BF) for size in weights + acts]
+        + [pltpu.VMEM((tokens, ff_part), BF), pltpu.VMEM((ff_part, tokens), BF)]
         + scatter_bufs * 2
         + [
-            dma((8, 10)),
+            dma((17, 10)),
             dma((4, 8)),
             dma((4, 8)),
             dma((4, 4)),
             dma((4, 4)),
-            dma((16,)),
-            dma((16,)),
-            dma((8,)),
+            dma((24,)),
+            dma((24,)),
+            dma((11,)),
         ],
         compiler_params=pltpu.CompilerParams(
-            collective_id=0, has_side_effects=True, vmem_limit_bytes=60 * 2**20
+            collective_id=0, has_side_effects=True, vmem_limit_bytes=VMEM_BYTES
         ),
         cost_estimate=pl.CostEstimate(flops=2 * 10**10, bytes_accessed=5 * 10**7, transcendentals=10**6),
-    )(x_in, g_in, gains_in, w_query, w_kv, w_out, w_gate, w_up, w_down, small_in, small_out, cosine, sine, start, head_gains)
+    )(x_in, g_in, gains_in, *weights_in, cosine, sine, start, head_gains)
 
 
 class RowScatter:
@@ -1208,48 +1308,44 @@
         index, half, mask = ((1, 0, 1), (3, 0, 1), (2, 1, 2), (3, 1, 2), (2, 0, 2), (1, 1, 1))[lane]
         return self.send(lane, self.row ^ index, half, mask)
 
-    def start(self):
-        for lane in (1, 3, 0, 2):
+    def start(self, lanes=(1, 3, 0, 2)):
+        for lane in lanes:
             self.lane(lane).start()
 
-    def value(self, lane):
-        return (self.came if self.stage is None else self.stage[0])[
-            lane if self.stage is None else lane % 2
-        ].astype(F32)
-
-    def fetch(self, *wanted):
-        for lane in wanted:
+    def load(self, lane):
+        slot = {0: 0, 1: 0, 4: 0, 2: 1, 3: 1, 5: 1}[lane]
+        return slot, pltpu.make_async_copy(
+            self.came.at[lane], self.stage[0].at[slot], self.stage[1].at[slot]
+        )
+
+    def fetch(self, *lanes):
+        for lane in lanes:
             self.lane(lane).wait_recv()
+            if self.stage is not None:
+                self.load(lane)[1].start()
+
+    def add(self, lane, index, half):
         if self.stage is None:
-            return
-        copies = [
-            pltpu.make_async_copy(
-                self.came.at[lane], self.stage[0].at[lane % 2], self.stage[1].at[lane % 2]
-            )
-            for lane in wanted
-        ]
-        for copy in copies:
-            copy.start()
-        for copy in copies:
+            value = self.came[lane]
+        else:
+            slot, copy = self.load(lane)
             copy.wait()
+            value = self.stage[0][slot]
+        part = self.halves(self.row ^ index)[half]
+        part[...] = (part[...].astype(F32) + value.astype(F32)).astype(BF)
 
     def middle(self):
-        row = self.row
-        for lane, out, index, half in ((1, 4, row ^ 2, 0), (3, 5, row ^ 1, 1)):
-            self.fetch(lane)
-            part = self.halves(index)[half]
-            part[...] = (part[...].astype(F32) + self.value(lane)).astype(BF)
+        for lane, out, index, half in ((1, 4, 2, 0), (3, 5, 1, 1)):
+            self.add(lane, index, half)
             self.lane(out).start()
 
+    def early(self):
+        self.add(0, 0, 0)
+        self.add(2, 0, 1)
+
     def finish(self):
-        row = self.row
-        for pair, half in (((0, 4), 0), ((2, 5), 1)):
-            part = self.halves(row)[half]
-            total = part[...].astype(F32)
-            for lane in pair:
-                self.fetch(lane)
-                total = total + self.value(lane)
-            part[...] = total.astype(BF)
+        self.add(4, 0, 0)
+        self.add(5, 0, 1)
 
     def drain(self):
         for lane in range(6):
@@ -1286,13 +1382,15 @@
     cosine,
     sine,
     start,
-    vsi,
-    vso,
+    vll,
+    vlr,
+    vpg,
+    vpp,
     xg_in,
     fg_in,
     gate_in,
     up_in,
-    hid_in,
+    turned_in,
     wq_in,
     wkv_in,
     wo_in,
@@ -1312,7 +1410,7 @@
     gdown,
     came_g,
     came_u,
-    came_d,
+    turned_all,
     vq,
     vkv,
     vo,
@@ -1322,7 +1420,8 @@
     fg,
     gate,
     up,
-    hid,
+    dff_all,
+    down_stage,
     dffg,
     dattng,
     dgate,
@@ -1350,7 +1449,6 @@
     d_kv,
     kv_give,
     kv_got,
-    kv_x,
     kv_x_got,
     kv_p_got,
     pkv,
@@ -1358,7 +1456,6 @@
     came_kv,
     came_o,
     stage_g,
-    stage_d,
     stage_sems,
     load_sems,
     row_sems,
@@ -1371,6 +1468,8 @@
     gain_send,
     gain_recv,
     done_sems,
+    ff_sems,
+    down_sems,
 ):
     core, row, col = lax.axis_index("seq"), lax.axis_index("row"), lax.axis_index("col")
     place = (core, row, col)
@@ -1404,7 +1503,6 @@
                 (up_in, up),
                 (wg_in, vg),
                 (wu_in, vu),
-                (hid_in, hid),
                 (fg_in, fg),
                 (wo_in, vo),
                 (wq_in, vq),
@@ -1415,6 +1513,9 @@
     for load in loads:
         load.start()
     pl.semaphore_wait(barrier, 10)
+    block_of, halves_of = by_cols(turned_all, tokens)
+    get_turned = RowGather(place, turned_in, block_of, halves_of, row_sems.at[0])
+    get_turned.start()
 
     def gain(index):
         return gains[pl.ds(index, 1)]
@@ -1422,14 +1523,13 @@
     inputs = x_own[...].astype(F32)
     x_norm = rms(inputs)[0] * gain(0)
     attn_normed = rms(attn_val[...])[0]
-    lo_normed = rms(mm(lr_low[...], vso[pl.ds(0, rank)]))[0]
+    lo_normed = rms(mm(lr_low[...], vlr[...]))[0]
     h_two = (inputs + attn_normed * gain(1) + (x_norm + lo_normed * gain(2))) * ROOT_HALF
     h_two_ref[...] = h_two
     ff_normed, ff_factor = rms(ff_val[...])
     h_three = h_two + ff_normed * gain(4)
     h_low = h_three.astype(BF)
-    p_gate = vsi[:, pl.ds(2 * rank, vsi.shape[1] - 2 * rank)]
-    p_proj = vso[pl.ds(rank, vso.shape[0] - rank)]
+    p_gate, p_proj = vpg[...], vpp[...]
     pg_gelu, pg_slope = gelu_both(mm(h_low, p_gate))
     per_input = per_in[row].astype(F32)
     gp_low = (pg_gelu * per_input).astype(BF)
@@ -1487,8 +1587,41 @@
 
     small(0, rank, mm_tn(gp_low, d_pp_low))
     small(1, rank, mm_tn(d_pg_low, h_low))
-    gather_ff.forward()
+    gather_ff.forward([lambda: None, lambda: None, get_turned.forward])
     gather_ff.finish()
+
+    part_rows = tokens // 2
+
+    def ff_piece(group, which):
+        return dff_all.at[
+            pl.ds(pl.multiple_of(group * tokens + which * part_rows, part_rows), part_rows)
+        ]
+
+    def ff_over(mask):
+        return remote(
+            dffg.at[
+                pl.ds(pl.multiple_of(core * part_rows, part_rows), part_rows),
+                pl.ds(pl.multiple_of((row ^ mask) * block, block), block),
+            ],
+            ff_piece(row, core),
+            ff_sems.at[mask],
+            ff_sems.at[4 + mask],
+            (core, row ^ mask, col),
+        )
+
+    def ff_came(mask):
+        part = ff_piece(row ^ mask, core)
+        return remote(part, part, ff_sems.at[mask], ff_sems.at[4 + mask], (core, row, col))
+
+    def ff_share(mask, which):
+        part = ff_piece(row ^ mask, which)
+        return remote(
+            part, part, ff_sems.at[8 + mask], ff_sems.at[12 + mask], (1 - core, row, col)
+        )
+
+    for mask in (1, 2, 3):
+        ff_over(mask).start()
+    dff_all[pl.ds(pl.multiple_of(row * tokens, tokens), tokens)] = dffg[:, my_cols]
 
     tile = 256
     for load in loads[:3]:
@@ -1521,22 +1654,45 @@
     scatter_f.sibling().start()
     back_ff(keep, home)
 
-    put_d = RowScatter(place, by_cols(vd, block)[1], came_d, row_sems.at[0], (stage_d, stage_sems))
     put_g = RowScatter(place, by_rows(vg, block)[1], came_g, row_sems.at[1], (stage_g, stage_sems))
     put_u = RowScatter(place, by_rows(vu, block)[1], came_u, row_sems.at[2], (stage_g, stage_sems))
 
+    load_turned = pltpu.make_async_copy(turned_all, vd, load_sems.at[5])
+
+    def down_ready():
+        get_turned.finish()
+        load_turned.start()
+        for mask in (1, 2, 3):
+            ff_came(mask).wait_recv()
+            ff_share(mask, core).start()
+
+    def down_tile(index):
+        slot = index % 2
+        rows = pl.ds(index * tile, tile)
+        target = gdown.at[pl.ds(pl.multiple_of(core * ff_part + index * tile, tile), tile)]
+        local = pltpu.make_async_copy(down_stage.at[slot], target, down_sems.at[index])
+        over = remote(
+            down_stage.at[slot],
+            target,
+            down_sems.at[4 + index],
+            down_sems.at[8 + index],
+            (1 - core, row, col),
+        )
+        return slot, rows, local, over
+
     def down_grad():
-        loads[5].wait()
-
-        def step(index, carry):
-            cols = pl.ds(pl.multiple_of(index * tile, tile), tile)
-            for part in range(2):
-                wide = pl.ds(part * (width // 2), width // 2)
-                vd[cols, wide] = mm_tn(hid[:, cols], dffg[:, wide]).astype(BF)
-            return carry
-
-        lax.fori_loop(0, ff_part // tile, step, 0)
-        put_d.start()
+        load_turned.wait()
+        for mask in (1, 2, 3):
+            ff_share(mask, 1 - core).wait_recv()
+        for index in range(ff_part // tile):
+            slot, rows, local, over = down_tile(index)
+            if index >= 2:
+                before = down_tile(index - 2)
+                before[2].wait()
+                before[3].wait_send()
+            down_stage[slot] = mm(vd[rows], dff_all[...]).astype(BF)
+            local.start()
+            over.start()
 
     def gate_grad(target, grad, put):
         def step(index, carry):
@@ -1545,13 +1701,17 @@
             return carry
 
         lax.fori_loop(0, width // tile, step, 0)
-        put.start()
-
-    def both_gates():
-        loads[6].wait()
+
+    def start_gate():
+        loads[5].wait()
         gate_grad(vg, dgate, put_g)
-
-    scatter_f.run(own_sum, [down_grad, both_gates, lambda: gate_grad(vu, dup, put_u)])
+        put_g.start()
+
+    def start_up():
+        gate_grad(vu, dup, put_u)
+        put_u.start((1, 3))
+
+    scatter_f.run(own_sum, [start_gate, start_up, down_ready])
 
     f_normed, f_factor = rms(h_two_ref[...])
     d_f, gain_three = rms_back(own_sum[...], f_normed, f_factor, gain(3))
@@ -1562,14 +1722,14 @@
     dattng[mine] = d_attn.astype(BF)
     gather_a = Gather(place, dattng, own_tokens, sems(2))
     gather_a.start()
-    lo_normed, lo_factor = rms(mm(lr_low[...], vso[pl.ds(0, rank)]))
+    lo_normed, lo_factor = rms(mm(lr_low[...], vlr[...]))
     d_lo, gain_two = rms_back(d_half, lo_normed, lo_factor, gain(2))
     d_lo_low = d_lo.astype(BF)
-    d_lr_low = mm_nt(d_lo_low, vso[pl.ds(0, rank)]).astype(BF)
+    d_lr_low = mm_nt(d_lo_low, vlr[...]).astype(BF)
     small(0, 0, mm_tn(lr_low[...], d_lo_low))
     x_low = (rms(x_own[...].astype(F32))[0] * gain(0)).astype(BF)
     small(1, 0, mm_tn(d_lr_low, x_low))
-    own_sum[...] = d_half + mm_nt(d_lr_low, vsi[:, pl.ds(0, rank)])
+    own_sum[...] = d_half + mm_nt(d_lr_low, vll[...])
     gpart[pl.ds(3, 1)] = gain_three
     gpart[pl.ds(2, 1)] = gain_two
     gpart[pl.ds(1, 1)] = gain_one
@@ -1577,11 +1737,27 @@
         small_give, small_got, misc_send.at[8], misc_recv.at[8], (1 - core, row, col)
     )
     small_swap.start()
-    gather_a.forward()
-    put_d.middle()
+    put_s = RowScatter(place, by_cols(small_keep, block)[1], small_row, row_sems.at[6])
+
+    def small_sum():
+        small_swap.wait_recv()
+        small_keep[...] = (small_keep[...].astype(F32) + small_got[...].astype(F32)).astype(BF)
+        put_s.start()
+
+    def middle_gate():
+        put_g.fetch(1, 3)
+        down_grad()
+        put_g.middle()
+
+    def more_up():
+        put_u.start((0, 2))
+        small_sum()
+        put_g.fetch(0, 2)
+
+    gather_a.forward([middle_gate, more_up, put_g.early])
     gather_a.finish()
 
-    loads[7].wait()
+    loads[6].wait()
     d_o[...] = mm_nt(dattng[...], vo[...]).astype(BF)
     q_rows = 128
     key_token = lax.broadcasted_iota(jnp.int32, (1, 2 * tokens), 1)
@@ -1620,25 +1796,33 @@
             vo[:, wide] = mm_tn(o_low[...], dattng[:, wide]).astype(BF)
 
     put_o = RowScatter(place, by_cols(vo, block)[1], came_o, row_sems.at[3])
-    swap_kv.wait_recv()
+    swap_kv.wait()
+    kv_x = kv_give.at[pl.ds(0, tokens)]
     theirs = pl.ds(pl.multiple_of((half ^ 1) * tokens, tokens), tokens)
     ours = pl.ds(pl.multiple_of(half * tokens, tokens), tokens)
     kv_x[...] = (d_kv[core, theirs] + kv_got[theirs].astype(F32)).astype(BF)
     over_x = remote(kv_x, kv_x_got, misc_send.at[10], misc_recv.at[10], (core, row ^ 1, col))
     over_x.start()
     load_x = pltpu.make_async_copy(xg_in, dffg, load_sems.at[10])
+    for mask in (1, 2, 3):
+        ff_over(mask).wait_send()
     load_x.start()
+    put_u.fetch(1, 3)
     out_grad()
+    put_u.middle()
     put_o.start()
+    put_s.fetch(1, 3)
+    put_s.middle()
+    loads[7].wait()
     loads[8].wait()
-    loads[9].wait()
     over_x.wait_recv()
     d_kind = d_kv[core, ours] + kv_got[ours].astype(F32) + kv_x_got[...].astype(F32)
     kv_p = kv_got.at[pl.ds(0, tokens)]
     kv_p[...] = d_kind.astype(BF)
     over_p = remote(kv_p, kv_p_got, misc_send.at[11], misc_recv.at[11], (core, row, col ^ 1))
     over_p.start()
-    put_g.middle()
+    put_u.fetch(0, 2)
+    put_u.early()
     over_p.wait()
     d_kind = kv_p[...].astype(F32) + kv_p_got[...].astype(F32)
     is_key = core == 0
@@ -1674,7 +1858,6 @@
     back_heads(keep, home)
     put_q = RowScatter(place, by_rows(vq, block)[1], came_q, row_sems.at[4])
     put_kv = RowScatter(place, by_rows(pkv, block)[1], came_kv, row_sems.at[5])
-    put_s = RowScatter(place, by_cols(small_keep, block)[1], small_row, row_sems.at[6])
 
     def query_grad():
         load_x.wait()
@@ -1689,13 +1872,51 @@
         put_q.start()
         put_kv.start()
 
-    def small_sum():
-        small_swap.wait_recv()
-        small_keep[...] = (small_keep[...].astype(F32) + small_got[...].astype(F32)).astype(BF)
-        put_s.start()
+    def deliver(lane, source, target):
+        local = pltpu.make_async_copy(source, target, done_sems.at[lane])
+        over = remote(
+            source, target, done_sems.at[8 + lane], done_sems.at[16 + lane], (1 - core, row, col)
+        )
+        local.start()
+        over.start()
+        done.append((local, over))
+
+    core_ff = pl.ds(pl.multiple_of(core * ff_part, ff_part), ff_part)
+    core_head = pl.ds(pl.multiple_of(core * head_dim, head_dim), head_dim)
+    sib_ff = pl.ds(pl.multiple_of((1 - core) * ff_part, ff_part), ff_part)
+    sib_head = pl.ds(pl.multiple_of((1 - core) * head_dim, head_dim), head_dim)
+    row_block = pl.ds(pl.multiple_of(row * block, block), block)
+    done = []
+
+    quarter = block // 4
+
+    def small_quarter(mask):
+        return remote(
+            small_keep.at[
+                :, pl.ds(pl.multiple_of(row * block + (col ^ mask) * quarter, quarter), quarter)
+            ],
+            small_z.at[mask],
+            misc_send.at[11 + mask],
+            misc_recv.at[11 + mask],
+            (core, row, col ^ mask),
+        )
+
+    def small_finish():
+        put_s.fetch(0, 2, 4, 5)
+        put_s.early()
+        put_s.finish()
+        for mask in (1, 2, 3):
+            small_quarter(mask).start()
+
+    def gate_finish():
+        put_o.fetch(1, 3)
+        put_o.middle()
+        put_g.fetch(4, 5)
+        put_g.finish()
+        deliver(1, vg.at[row_block], ggate.at[:, core_ff])
 
     d_half_here = d_three_ref
-    scatter_x.run(h_two_ref, [query_grad, small_sum, put_u.middle])
+    scatter_x.run(h_two_ref, [query_grad, small_finish, gate_finish])
     d_xn = own_sum[...] + h_two_ref[...]
     x_normed, x_factor = rms(x_own[...].astype(F32))
     d_in, gain_zero = rms_back(d_xn, x_normed, x_factor, gain(0))
@@ -1743,44 +1964,11 @@
     for other, mask in members:
         gain_group(other, mask).start()
     gcame2[me] = gpart2[...]
-    put_s.middle()
+    put_kv.fetch(1, 3)
     put_kv.middle()
-    put_o.middle()
+    put_q.fetch(1, 3)
     put_q.middle()
-
-    def deliver(lane, source, target):
-        local = pltpu.make_async_copy(source, target, done_sems.at[lane])
-        over = remote(
-            source, target, done_sems.at[8 + lane], done_sems.at[16 + lane], (1 - core, row, col)
-        )
-        local.start()
-        over.start()
-        return local, over
-
-    core_ff = pl.ds(pl.multiple_of(core * ff_part, ff_part), ff_part)
-    core_head = pl.ds(pl.multiple_of(core * head_dim, head_dim), head_dim)
-    sib_ff = pl.ds(pl.multiple_of((1 - core) * ff_part, ff_part), ff_part)
-    sib_head = pl.ds(pl.multiple_of((1 - core) * head_dim, head_dim), head_dim)
-    row_block = pl.ds(pl.multiple_of(row * block, block), block)
-    done = []
-    put_d.finish()
-    done.append(deliver(0, vd.at[:, row_block], gdown.at[core_ff]))
-    put_g.finish()
-    done.append(deliver(1, vg.at[row_block], ggate.at[:, core_ff]))
-    put_s.finish()
-
-    quarter = block // 4
-
-    def small_quarter(mask):
-        return remote(
-            small_keep.at[
-                :, pl.ds(pl.multiple_of(row * block + (col ^ mask) * quarter, quarter), quarter)
-            ],
-            small_z.at[mask],
-            misc_send.at[11 + mask],
-            misc_recv.at[11 + mask],
-            (core, row, col ^ mask),
-        )
+    put_u.fetch(4, 5)
 
     def small_share(other, mask):
         lane = 16 + other * 4 + mask
@@ -1792,10 +1980,8 @@
             (core ^ other, row, col ^ mask),
         )
 
-    for mask in (1, 2, 3):
-        small_quarter(mask).start()
     put_u.finish()
-    done.append(deliver(2, vu.at[row_block], gup.at[:, core_ff]))
+    deliver(2, vu.at[row_block], gup.at[:, core_ff])
     for mask in (1, 2, 3):
         small_quarter(mask).wait_recv()
     small_total = small_keep[
@@ -1808,12 +1994,15 @@
     for other, mask in members:
         small_share(other, mask).start()
     small_a[core, col] = small_total.astype(BF)
-    put_kv.finish()
-    done.append(deliver(3, pkv.at[row_block], gkv.at[core]))
-    put_o.finish()
-    done.append(deliver(4, vo.at[:, row_block], gout.at[core_head]))
-    put_q.finish()
-    done.append(deliver(5, vq.at[row_block], gq.at[:, core_head]))
+    for put, lane, source, target in (
+        (put_o, 4, vo.at[:, row_block], gout.at[core_head]),
+        (put_kv, 3, pkv.at[row_block], gkv.at[core]),
+        (put_q, 5, vq.at[row_block], gq.at[:, core_head]),
+    ):
+        put.fetch(0, 2, 4, 5)
+        put.early()
+        put.finish()
+        deliver(lane, source, target)
 
     for other, mask in members:
         who = (core ^ other) * 4 + (col ^ mask)
@@ -1842,21 +2031,30 @@
         gain_row(mask).wait_send()
         small_quarter(mask).wait_send()
     small_swap.wait_send()
-    swap_kv.wait_send()
-    for put in (put_d, put_g, put_u, put_o, put_q, put_kv, put_s):
+    for put in (put_g, put_u, put_o, put_q, put_kv, put_s):
         put.drain()
-    sib_targets = [
-        gdown.at[sib_ff],
-        ggate.at[:, sib_ff],
-        gup.at[:, sib_ff],
-        gkv.at[1 - core],
-        gout.at[sib_head],
-        gq.at[:, sib_head],
-    ]
-    for lane, (local, over) in enumerate(done):
+    for mask in (1, 2, 3):
+        ff_share(mask, core).wait_send()
+    for index in range(ff_part // tile):
+        slot, rows, local, over = down_tile(index)
+        if index >= 2:
+            local.wait()
+            over.wait_send()
+        target = gdown.at[pl.ds(pl.multiple_of((1 - core) * ff_part + index * tile, tile), tile)]
+        remote(
+            target, target, down_sems.at[4 + index], down_sems.at[8 + index], (core, row, col)
+        ).wait_recv()
+    theirs_at = {
+        1: ggate.at[:, sib_ff],
+        2: gup.at[:, sib_ff],
+        3: gkv.at[1 - core],
+        4: gout.at[sib_head],
+        5: gq.at[:, sib_head],
+    }
+    for lane, (local, over) in zip((1, 2, 4, 3, 5), done):
         local.wait()
         over.wait_send()
-        target = sib_targets[lane]
+        target = theirs_at[lane]
         remote(
             target, target, done_sems.at[8 + lane], done_sems.at[16 + lane], (core, row, col)
         ).wait_recv()
@@ -1870,7 +2068,7 @@
     tokens, ff_part = gate.shape
     head_dim = head_gains.shape[1]
     rank = small_args[6].shape[1]
-    small_rows = small_args[19].shape[0]
+    small_rows = sum(small_args[lane].shape[0] for lane in (19, 21))
     vm = pl.BlockSpec(memory_space=pltpu.VMEM)
     hbm = pl.BlockSpec(memory_space=pl.ANY)
     shape = jax.ShapeDtypeStruct
@@ -1890,7 +2088,7 @@
         shape((2 * ff_part, block), BF),
         shape((6, block // 2, ff_part), BF),
         shape((6, block // 2, ff_part), BF),
-        shape((6, ff_part // 2, block), BF),
+        shape((ff_part, 4 * tokens), BF),
     ]
     scratch = [
         vmem((width, head_dim), BF),
@@ -1902,7 +2100,8 @@
         vmem((tokens, width), BF),
         vmem((tokens, ff_part), BF),
         vmem((tokens, ff_part), BF),
-        vmem((tokens, ff_part), BF),
+        vmem((4 * tokens, block), BF),
+        vmem((2, 256, block), BF),
         vmem((tokens, width), BF),
         vmem((tokens, width), BF),
         vmem((tokens, ff_part), BF),
@@ -1932,13 +2131,11 @@
         vmem((2 * tokens, head_dim), BF),
         vmem((tokens, head_dim), BF),
         vmem((tokens, head_dim), BF),
-        vmem((tokens, head_dim), BF),
         vmem((width, head_dim // 2), BF),
         vmem((6, block // 2, head_dim), BF),
         vmem((6, block // 2, head_dim // 2), BF),
         vmem((6, head_dim // 2, block), BF),
         vmem((2, block // 2, ff_part), BF),
-        vmem((2, ff_part // 2, block), BF),
         dma((2,)),
         dma((11,)),
         dma((7, 12)),
@@ -1951,11 +2148,13 @@
         dma((12,)),
         dma((12,)),
         dma((24,)),
+        dma((16,)),
+        dma((12,)),
     ]
     return pl.pallas_call(
         backward_kernel,
         out_shape=outs,
-        in_specs=[vm] * 20 + [hbm] * 11,
+        in_specs=[vm] * 22 + [hbm] * 11,
         out_specs=[vm] * 5 + [hbm] * 9,
         scratch_shapes=scratch,
         compiler_params=pltpu.CompilerParams(
@@ -2019,49 +2218,22 @@
 
     w_kv = jnp.where(core == 0, w_key, w_value)
     rank = laurel_left.shape[1]
-    small_in = jnp.concatenate(
-        [laurel_left, jnp.zeros((laurel_left.shape[0], rank), BF), per_gate], axis=1
-    )
-    small_out = jnp.concatenate([laurel_right, per_proj], axis=0)
-    (
-        x_own,
-        g_own,
-        gains,
-        x_all,
-        raw_q,
-        raw_kv,
-        q_low,
-        kv,
-        lse,
-        top_tile,
-        o_low,
-        attn_val,
-        lr_low,
-        f_all,
-        gate_val,
-        up_val,
-        hid_low,
-        ff_val,
-        w_q,
-        w_kv_all,
-        w_o,
-        w_g,
-        w_u,
-        w_d,
-        small_in_all,
-        small_out_all,
-    ) = run_forward(
+    saved = run_forward(
         layer_in.reshape(rows, own_tokens, -1),
         out_grad.reshape(rows, own_tokens, -1),
         norm_gains,
-        w_query,
-        w_kv,
-        w_out,
-        w_gate,
-        w_up,
-        w_down,
-        small_in,
-        small_out,
+        (
+            w_query,
+            w_kv,
+            w_out,
+            w_gate,
+            w_up,
+            w_down,
+            laurel_left,
+            laurel_right,
+            per_gate,
+            per_proj,
+        ),
         (
             cosine_table[:, : head_dim // 2],
             sine_table[:, : head_dim // 2],
@@ -2069,6 +2241,11 @@
         ),
         head_gains,
     )
+    (x_own, g_own, gains, raw_q, raw_kv, q_low, kv, lse, top_tile, o_low, attn_val, lr_low, ff_val) = saved[
+        :13
+    ]
+    l_left, l_right, p_gate, p_proj = saved[13:17]
+    w_q, w_kv_all, w_o, w_g, w_u, w_d, x_all, f_all, gate_val, up_val, turned = saved[17:]
     half_table = head_dim // 2
     (
         y_out,
@@ -2103,10 +2280,12 @@
             cosine_table[:, :half_table],
             sine_table[:, :half_table],
             start[:, None],
-            small_in_all,
-            small_out_all,
+            l_left,
+            l_right,
+            p_gate,
+            p_proj,
         ),
-        (x_all, f_all, gate_val, up_val, hid_low, w_q, w_kv_all, w_o, w_g, w_u, w_d),
+        (x_all, f_all, gate_val, up_val, turned, w_q, w_kv_all, w_o, w_g, w_u, w_d),
     )
     sums_a = small_sums[0].transpose(1, 0, 2).reshape(small_sums.shape[2], -1).astype(F32)
     sums_b = small_sums[1].transpose(0, 2, 1).reshape(-1, small_sums.shape[2]).astype(F32)

time: 504 us -> 435 us (0.86)
  Pallas kernels: 471 us -> 400 us
    pallas_call x1, Pallas kernels: 256 us -> 208 us  [run_backward(): pl.pallas_call(backward_kernel, out_shape=outs, in_specs=[vm] * 22 + [hbm...]
    pallas_call x1, Pallas kernels: 215 us -> 192 us  [run_forward(): pl.pallas_call(forward_kernel, out_shape=outs, in_specs=[vm, vm, vm, hbm,...]
where the time goes in v3:
time: 435 us; the launch traced here: 430 us
  Pallas kernels  400 us (92%)
  other arithmetic  19 us (4%)
  local copies, waits for them, and re-layouts  10.2 us (2%)
    pallas_call x1, Pallas kernels, run_backward(): pl.pallas_call(backward_kernel, out_shape=outs, in_specs=[vm] * 22 + [hbm...  208 us
    pallas_call x1, Pallas kernels, run_forward(): pl.pallas_call(forward_kernel, out_shape=outs, in_specs=[vm, vm, vm, hbm,...  192 us

profile of v3, /device:TPU:1, one launch (start us, length us, event | category | flops | bytes accessed | tf_op | source)
XLA Modules:
  0.0 429.7 jit_solution(17393039864533160832)
XLA Ops:
  0.6 0.0 copy-start
  0.7 0.6 copy-done
  1.3 0.1 multiply_reduce_fusion
  1.5 0.1 select_reduce_fusion
  1.6 1.6 broadcast_select_fusion.w_kv
  3.2 1.6 copy.43.laurel_left
  4.8 0.9 copy.44.start
  5.6 1.8 multiply_sine_fusion
  7.4 191.8 %shard_map.288 = (bf16[64,2048]{1,0:T(8,128)(2,1)}, bf16[64,2048]{1,0:T(8,128)(2,1)}, f32[8,2048]{1,0:T(8,128)}, f32[512,256]{1,0:T(8,128)}, f32[512,256]{1,0:T(...) custom-call(bf16[4,64,512]{2,1,0:T(8,128)(2,1)} %bitcast.42, ...), custom_call_target="tpu_custom_call" | custom-call | flops 20000000000 | bytes 50000000 | tf_op jit(solution)/shard_map/pallas_call | solution.py:1266
  199.2 0.0 copy-start.9
  199.3 207.9 %shard_map.289 = (bf16[4,64,512]{2,1,0:T(8,128)(2,1)}, bf16[4,64,512]{2,1,0:T(8,128)(2,1)}, f32[8,512]{1,0:T(8,128)}, f32[8,128]{1,0:T(8,128)}, bf16[2,4,320,128...) custom-call(bf16[64,2048]{1,0:T(8,128)(2,1)} %get-tuple-element.55.x, ...), custom_call_target="tpu_custom_call" | custom-call | flops 40000000000 | bytes 100000000 | tf_op jit(solution)/shard_map/pallas_call | solution.py:2154
  407.2 0.0 copy-start.5
  407.2 0.9 sqrt_reduce_fusion
  408.1 0.7 slice_reduce_fusion
  408.8 0.6 reshape_squeeze.3
  409.4 0.0 copy-done.9
  409.4 0.7 broadcast_multiply_fusion
  410.1 1.8 bitcast_convert_fusion
  411.9 2.1 convert_element_type.58
  414.0 2.1 convert_element_type.63
  416.2 0.0 copy-done.5
  416.2 0.1 convert_bitcast_fusion.1
  416.3 0.1 copy.55
  416.3 0.0 copy-start.4
  416.3 0.7 slice.52
  417.0 1.0 copy.49
  418.0 0.7 copy_bitcast_fusion.1
  418.7 0.2 copy.48
  418.9 1.0 copy.50
  419.9 0.0 copy-done.4
  419.9 0.0 copy-start.3
  419.9 2.5 convert_element_type.64
  422.5 0.0 copy-done.3
  422.5 0.0 copy-start.2
  422.5 0.0 copy-start.1
  422.5 2.5 convert_element_type.65
  425.0 0.0 copy-done.2
  425.0 0.0 copy-start.7
  425.0 0.0 copy-start.6
  425.0 0.0 copy-start.8
  425.0 2.6 convert_element_type.66
  427.7 0.0 copy-done.7
  427.7 0.7 copy.59
  428.4 0.0 copy-done.6
  428.4 0.7 copy.60
  429.1 0.0 copy-done.8
  429.1 0.6 copy.61
  429.7 0.0 copy-done.1
  (6 shorter events, 0.1 us)
Async XLA Ops:
  0.6 0.7 copy-start
  199.2 210.2 %copy-start.9 = (f32[2,256]{1,0:T(2,128)S(1)}, f32[2,256]{1,0:T(2,128)}, u32[]{:S(2)}) copy-start(f32[2,256]{1,0:T(2,128)} %head_gains.3) | copy-start | bytes 6148
  407.2 9.0 %copy-start.5 = (bf16[2,4,320,128]{3,2,1,0:T(8,128)(2,1)S(1)}, bf16[2,4,320,128]{3,2,1,0:T(8,128)(2,1)}, u32[]{:S(2)}) copy-start(bf16[2,4,320,128]{3,2,1,0:T(8,128)(2,1)} %get-tuple-element.91) | copy-start | bytes 1966084
  416.3 3.6 copy-start.4
  419.9 2.5 copy-start.3
  422.5 2.5 copy-start.2
  422.5 7.2 %copy-start.1 = (s32[2,4]{1,0:T(2,128)S(1)}, s32[2,4]{1,0:T(2,128)}, u32[]{:S(2)}) copy-start(s32[2,4]{1,0:T(2,128)} %param.19) | copy-start | bytes 100
  425.0 2.6 copy-start.7
  425.0 3.3 copy-start.6
  425.0 4.0 copy-start.8

commit v4 on v3

--- a/solution.py
+++ b/solution.py
@@ -16,6 +16,7 @@
 BF = jnp.bfloat16
 F32 = jnp.float32
 VMEM_BYTES = 63 * 2**20
+PIECES = 4
 
 
 def swapped(value, axis, apart):
@@ -504,101 +505,104 @@
         self.buf, self.rows = buf, rows
         self.send_z, self.recv_z, self.send_s, self.recv_s = sems
 
-    def part(self, core, col):
-        return self.buf.at[pl.ds(pl.multiple_of((core * 4 + col) * self.rows, self.rows), self.rows)]
-
-    def to_right(self, dist):
-        part = self.part(self.core, self.col - dist)
-        return remote(
-            part, part, self.send_z.at[dist], self.recv_z.at[dist], (self.core, self.row, self.col + 1)
-        )
-
-    def to_left(self, dist):
-        part = self.part(self.core, self.col + dist)
+    def part(self, core, col, piece):
+        rows = self.rows // PIECES
+        first = (core * 4 + col) * self.rows + piece * rows
+        return self.buf.at[pl.ds(pl.multiple_of(first, rows), rows)]
+
+    def hop(self, dist, right, piece):
+        part = self.part(self.core, self.col - dist if right else self.col + dist, piece)
+        lane = ((0 if right else 3) + dist) * PIECES + piece
         return remote(
             part,
             part,
-            self.send_z.at[3 + dist],
-            self.recv_z.at[3 + dist],
-            (self.core, self.row, self.col - 1),
-        )
-
-    def to_sibling(self, col):
-        part = self.part(self.core, col)
+            self.send_z.at[lane],
+            self.recv_z.at[lane],
+            (self.core, self.row, self.col + (1 if right else -1)),
+        )
+
+    def came(self, dist, right, piece):
+        part = self.part(self.core, self.col - dist if right else self.col + dist, piece)
+        lane = ((0 if right else 3) + dist - 1) * PIECES + piece
         return remote(
-            part, part, self.send_s.at[col], self.recv_s.at[col], (1 - self.core, self.row, self.col)
+            part, part, self.send_z.at[lane], self.recv_z.at[lane], (self.core, self.row, self.col)
+        )
+
+    def to_sibling(self, col, piece, core=None):
+        part = self.part(self.core if core is None else core, col, piece)
+        lane = col * PIECES + piece
+        return remote(
+            part,
+            part,
+            self.send_s.at[lane],
+            self.recv_s.at[lane],
+            (1 - self.core, self.row, self.col),
         )
 
     def start(self):
         col = self.col
-
-        @pl.when(col < 3)
-        def _():
-            self.to_right(0).start()
-
-        @pl.when(col > 0)
-        def _():
-            self.to_left(0).start()
-
-        self.to_sibling(col).start()
+        for piece in range(PIECES):
+
+            @pl.when(col < 3)
+            def _():
+                self.hop(0, True, piece).start()
+
+            @pl.when(col > 0)
+            def _():
+                self.hop(0, False, piece).start()
+
+        for piece in range(PIECES):
+            self.to_sibling(col, piece).start()
 
     def forward(self, work=()):
         col = self.col
         work = list(work)
         for dist in (1, 2, 3):
-
-            @pl.when(col >= dist)
-            def _():
-                part = self.part(self.core, col - dist)
-                remote(
-                    part, part, self.send_z.at[0], self.recv_z.at[dist - 1], (self.core, self.row, col)
-                ).wait_recv()
-
-                @pl.when(col < 3)
+            for piece in range(PIECES):
+
+                @pl.when(col >= dist)
                 def _():
+                    self.came(dist, True, piece).wait_recv()
                     if dist < 3:
-                        self.to_right(dist).start()
-
-                self.to_sibling(col - dist).start()
-
-            @pl.when(col + dist <= 3)
-            def _():
-                part = self.part(self.core, col + dist)
-                remote(
-                    part,
-                    part,
-                    self.send_z.at[0],
-                    self.recv_z.at[3 + dist - 1],
-                    (self.core, self.row, col),
-                ).wait_recv()
-
-                @pl.when(col > 0)
+
+                        @pl.when(col < 3)
+                        def _():
+                            self.hop(dist, True, piece).start()
+
+                    self.to_sibling(col - dist, piece).start()
+
+                @pl.when(col + dist <= 3)
                 def _():
+                    self.came(dist, False, piece).wait_recv()
                     if dist < 3:
-                        self.to_left(dist).start()
-
-                self.to_sibling(col + dist).start()
+
+                        @pl.when(col > 0)
+                        def _():
+                            self.hop(dist, False, piece).start()
+
+                    self.to_sibling(col + dist, piece).start()
 
             if work:
                 work.pop(0)()
 
     def finish(self):
-        for col in range(4):
-            part = self.part(1 - self.core, col)
-            remote(
-                part, part, self.send_s.at[col], self.recv_s.at[col], (1 - self.core, self.row, self.col)
-            ).wait_recv()
-        for col in range(4):
-            self.to_sibling(col).wait_send()
-        for dist in (0, 1, 2):
-
-            @pl.when((self.col < 3) & (self.col >= dist))
-            def _():
-                self.to_right(dist).wait_send()
-
-            @pl.when((self.col > 0) & (self.col + dist <= 3))
-            def _():
-                self.to_left(dist).wait_send()
+        for piece in range(PIECES):
+            for col in range(4):
+                self.to_sibling(col, piece, 1 - self.core).wait_recv()
+
+    def drain(self):
+        for piece in range(PIECES):
+            for col in range(4):
+                self.to_sibling(col, piece).wait_send()
+            for dist in (0, 1, 2):
+
+                @pl.when((self.col < 3) & (self.col >= dist))
+                def _():
+                    self.hop(dist, True, piece).wait_send()
+
+                @pl.when((self.col > 0) & (self.col + dist <= 3))
+                def _():
+                    self.hop(dist, False, piece).wait_send()
 
 
 class Scatter:
@@ -608,80 +612,112 @@
         self.give, self.keep, self.got, self.sent, self.left, self.right = bufs
         self.send_z, self.recv_z, self.send_s, self.recv_s = sems
 
-    def sibling(self):
+    def sibling(self, dest):
+        rows = pl.ds(dest * self.rows, self.rows)
         return remote(
-            self.give,
-            self.got,
-            self.send_s.at[0],
-            self.recv_s.at[0],
+            self.give.at[rows],
+            self.got.at[rows],
+            self.send_s.at[dest],
+            self.recv_s.at[dest],
             (1 - self.core, self.row, self.col),
         )
 
-    def mine(self, dest):
-        rows = pl.ds(dest * self.rows, self.rows)
-        return self.keep[rows] + self.got[rows].astype(F32)
-
-    def hop(self, dest, right):
-        step = 1 if right else -1
-        lane = 0 if right else 4
+    def start(self):
+        for dest in (3, 0, 2, 1):
+            self.sibling(dest).start()
+
+    def piece(self, piece):
+        rows = self.rows // PIECES
+        return pl.ds(piece * rows, rows)
+
+    def mine(self, dest, piece):
+        count = self.rows // PIECES
+        rows = pl.ds(dest * self.rows + piece * count, count)
+        return self.keep[rows].astype(F32) + self.got[rows].astype(F32)
+
+    def inbox(self, dest, right):
+        return self.left.at[dest - 1] if right else self.right.at[dest]
+
+    def hop(self, dest, right, piece):
+        lane = ((0 if right else 4) + dest) * PIECES + piece
         return remote(
-            self.sent.at[dest],
-            self.left.at[dest - 1] if right else self.right.at[dest],
-            self.send_z.at[lane + dest],
-            self.recv_z.at[lane + dest],
-            (self.core, self.row, self.col + step),
-        )
-
-    def chain(self, dest, right):
-        col = self.col
-        inner = (col > 0) if right else (col < 3)
-
-        @pl.when((col < dest) if right else (col > dest))
-        def _():
-            @pl.when(inner)
+            self.sent.at[dest, self.piece(piece)],
+            self.inbox(dest, right).at[self.piece(piece)],
+            self.send_z.at[lane],
+            self.recv_z.at[lane],
+            (self.core, self.row, self.col + (1 if right else -1)),
+        )
+
+    def step(self, col, dest, right, piece):
+        rows = self.piece(piece)
+        if piece == 0:
+            self.sibling(dest).wait_recv()
+        total = self.mine(dest, piece)
+        if col != (0 if right else 3):
+            self.hop(dest, right, piece).wait_recv()
+            total = total + self.inbox(dest, right)[rows].astype(F32)
+        self.sent[dest, rows] = total.astype(BF)
+        self.hop(dest, right, piece).start()
+
+    def steps(self, col):
+        if col > 1:
+            return [
+                [(3 - dest, not right, piece) for dest, right, piece in part]
+                for part in self.steps(3 - col)
+            ]
+        full = lambda dest, right: [(dest, right, piece) for piece in range(PIECES)]
+        if col == 0:
+            return [full(3, True) + full(2, True), full(1, True)]
+        near, far = full(3, True) + full(2, True), full(0, False)
+        lag, order = PIECES - 1, []
+        for index, item in enumerate(near):
+            order.append(item)
+            if index + 1 >= lag and far:
+                order.append(far.pop(0))
+        cut = PIECES + 2
+        return [order[:cut], order[cut:] + far]
+
+    def run(self, result, work=()):
+        work = list(work)
+        for part in range(2):
+            for col in range(4):
+
+                @pl.when(self.col == col)
+                def _():
+                    for dest, right, piece in self.steps(col)[part]:
+                        self.step(col, dest, right, piece)
+
+            for call in work[part : part + 1]:
+                call()
+        for call in work[2:]:
+            call()
+        for dest in range(4):
+
+            @pl.when(self.col == dest)
             def _():
-                self.hop(dest, right).wait_recv()
-                came = (self.left[dest - 1] if right else self.right[dest]).astype(F32)
-                self.sent[dest] = (self.mine(dest) + came).astype(BF)
-
-            @pl.when(jnp.logical_not(inner))
-            def _():
-                self.sent[dest] = self.mine(dest).astype(BF)
-
-            self.hop(dest, right).start()
-
-    def run(self, result, work=()):
-        col = self.col
-        work = list(work)
-        self.sibling().wait_recv()
-        for dest in (3, 2, 1):
-            self.chain(dest, True)
-            self.chain(3 - dest, False)
-            if work:
-                work.pop(0)()
-        own = pl.ds(pl.multiple_of(col * self.rows, self.rows), self.rows)
-        result[...] = self.keep[own] + self.got[own].astype(F32)
+                self.sibling(dest).wait_recv()
+                for piece in range(PIECES):
+                    rows = self.piece(piece)
+                    total = self.mine(dest, piece)
+                    for right in (True, False):
+                        if dest != (0 if right else 3):
+                            self.hop(dest, right, piece).wait_recv()
+                            total = total + self.inbox(dest, right)[rows].astype(F32)
+                    result[rows] = total
+
+    def drain(self):
         for dest in range(4):
-
-            @pl.when(col == dest)
-            def _():
-                if dest > 0:
-                    self.hop(dest, True).wait_recv()
-                    result[...] += self.left[dest - 1].astype(F32)
-                if dest < 3:
-                    self.hop(dest, False).wait_recv()
-                    result[...] += self.right[dest].astype(F32)
-
-        self.sibling().wait_send()
-        for dest in (1, 2, 3):
-
-            @pl.when(col < dest)
-            def _():
-                self.hop(dest, True).wait_send()
-
-            @pl.when(col > 3 - dest)
-            def _():
-                self.hop(3 - dest, False).wait_send()
+            self.sibling(dest).wait_send()
+        for piece in range(PIECES):
+            for dest in (1, 2, 3):
+
+                @pl.when(self.col < dest)
+                def _():
+                    self.hop(dest, True, piece).wait_send()
+
+                @pl.when(self.col > 3 - dest)
+                def _():
+                    self.hop(3 - dest, False, piece).wait_send()
 
 
 class RowGather:
@@ -716,6 +752,12 @@
         self.first(1).start()
         self.first(2).start()
         self.own().start()
+
+    def finish_first(self):
+        for mask in (1, 2):
+            self.first(mask, self.block(self.row ^ mask)).wait_recv()
+            self.first(mask).wait_send()
+        self.own().wait()
 
     def forward(self):
         self.first(1, self.block(self.row ^ 1)).wait_recv()
@@ -800,7 +842,8 @@
     g_in,
     gains_in,
     w_query,
-    w_kv,
+    w_key,
+    w_value,
     w_out,
     w_gate,
     w_up,
@@ -884,7 +927,7 @@
     tokens = xg.shape[0]
     ff_part = gate.shape[1]
     chunk = 2 * own_tokens
-    key_width = w_kv.shape[1]
+    key_width = w_key.shape[1]
     half = row % 2
     greet(core, row, col)
 
@@ -928,11 +971,10 @@
     gains[:, my_cols] = gains_pad[...]
 
     pair_cols = pl.ds(pl.multiple_of(col % 2 * key_width, key_width), key_width)
-    pair = remote(
-        w_kv, w_kv_pair.at[:, pair_cols], misc_send.at[7], misc_recv.at[7], (core, row, col ^ 1)
-    )
+    w_kv_own = w_kv_pair.at[:, pair_cols]
+    w_kv_own[...] = jnp.where(core == 0, w_key[...].astype(F32), w_value[...].astype(F32)).astype(BF)
+    pair = remote(w_kv_own, w_kv_own, misc_send.at[7], misc_recv.at[7], (core, row, col ^ 1))
     pair.start()
-    w_kv_pair[:, pair_cols] = w_kv[...]
 
     lanes = iter(range(32))
 
@@ -1027,9 +1069,8 @@
     gather_x.start()
     gather_x.forward(
         [
-            lambda: begin([get_o] + get_laurel),
-            lambda: push([get_q, get_kv]),
-            lambda: push([get_o] + get_laurel),
+            lambda: None,
+            lambda: (push([get_q, get_kv]), begin([get_o])),
         ]
     )
     gather_x.finish()
@@ -1055,8 +1096,8 @@
     to_s = remote(here, here, misc_send.at[9], misc_recv.at[9], (1 - core, row, col))
     to_x.start()
     to_s.start()
-    begin(get_gu[0])
-    begin(get_gu[1])
+    push([get_o])
+    begin(get_gu[0] + get_laurel + get_gu[1])
     came = kv_part(core, half ^ 1)
     remote(here, came, misc_send.at[8], misc_recv.at[8], (core, row, col)).wait_recv()
     on_s = remote(came, came, misc_send.at[10], misc_recv.at[10], (1 - core, row, col))
@@ -1105,14 +1146,14 @@
         lax.fori_loop(0, width // block, step, 0)
 
     project(o_low, vo, give, away)
-    scatter.sibling().start()
-    push(get_gu[0])
-    begin(get_gu[2])
+    scatter.start()
     project(o_low, vo, keep, home)
     scatter.run(
         attn_val,
-        [lambda: None, lambda: push(get_gu[1]), lambda: begin(get_gu[3])],
-    )
+        [lambda: (push(get_gu[0]), push(get_laurel)), lambda: begin(get_gu[2])],
+    )
+    push(get_gu[1])
+    begin(get_gu[3])
 
     complete(get_laurel)
     inputs, x_norm = own_norm()
@@ -1127,9 +1168,9 @@
     gather_f.start()
     gather_f.forward(
         [
+            lambda: None,
             lambda: push(get_gu[2]),
-            lambda: None,
-            lambda: None,
+            lambda: begin(get_d[:1]),
         ]
     )
     gather_f.finish()
@@ -1146,7 +1187,7 @@
     for index in range(tiles):
         if index == 1:
             push(get_gu[3])
-            begin(get_d)
+            begin(get_d[1:])
         unit_tile(index)
     turned[...] = hid[...].T
     for job in get_d:
@@ -1165,7 +1206,6 @@
                 (fg, fg_all),
                 (gate, gate_all),
                 (up, up_all),
-                (turned, turned_all),
             ]
         )
     ]
@@ -1177,9 +1217,19 @@
         copy.start()
     scatter_ff = Scatter(place, own_tokens, (give2, keep2, got2, sent2, left2, right2), sems(3))
     project(hid, vd, give2, away)
-    scatter_ff.sibling().start()
+    scatter_ff.start()
     project(hid, vd, keep2, home)
-    scatter_ff.run(ff_val, [lambda: None, lambda: push(get_per)])
+    get_turned = rows_of(
+        turned.at[pl.ds(0, half_ff)], turned_all.at[pl.ds(0, half_ff)], by_cols, tokens
+    )
+    rest = pl.ds(half_ff, half_ff)
+    keep_rest = pltpu.make_async_copy(
+        turned.at[rest],
+        turned_all.at[rest, pl.ds(pl.multiple_of(row * tokens, tokens), tokens)],
+        out_sems.at[10],
+    )
+    keep_rest.start()
+    scatter_ff.run(ff_val, [lambda: (push(get_per), get_turned.start())])
     complete(get_per)
     share = [
         remote(part, part, misc_send.at[lane], misc_recv.at[lane], (1 - core, row, col))
@@ -1191,6 +1241,8 @@
         remote(part, part, misc_send.at[lane], misc_recv.at[lane], (core, row, col)).wait_recv()
     for copy in share:
         copy.wait_send()
+    get_turned.finish_first()
+    keep_rest.wait()
 
     for mask in (1, 2, 3):
         hand_over(mask).wait_send()
@@ -1203,6 +1255,10 @@
             misc_recv.at[11 + mask],
             (core, row, col),
         ).wait_recv()
+    gather_x.drain()
+    scatter.drain()
+    gather_f.drain()
+    scatter_ff.drain()
     pair.wait_send()
     to_x.wait_send()
     to_s.wait_send()
@@ -1213,7 +1269,7 @@
 
 def run_forward(x_in, g_in, gains_in, weights_in, tables, head_gains):
     cosine, sine, start = tables
-    w_gate, laurel_left, per_gate, per_proj = (weights_in[i] for i in (3, 6, 8, 9))
+    w_gate, laurel_left, per_gate, per_proj = (weights_in[i] for i in (4, 7, 9, 10))
     block = x_in.shape[2]
     own, width = x_in.shape[1], 4 * block
     tokens, head_dim, ff_part = 8 * own, head_gains.shape[1], w_gate.shape[1] // 2
@@ -1253,7 +1309,7 @@
         shape((rank, width), BF),
         shape((width, per_gate.shape[1]), BF),
         shape((per_proj.shape[0], width), BF),
-    ] + [shape(size, BF) for size in weights + acts + [(ff_part, tokens)]]
+    ] + [shape(size, BF) for size in weights + acts + [(ff_part, 4 * tokens)]]
     scatter_bufs = [
         pltpu.VMEM((4 * own, width), BF),
         pltpu.VMEM((4 * own, width), F32),
@@ -1266,18 +1322,18 @@
     return pl.pallas_call(
         forward_kernel,
         out_shape=outs,
-        in_specs=[vm, vm, vm, hbm, vm] + [hbm] * 8 + [vm] * 4,
+        in_specs=[vm, vm, vm, hbm, vm, vm] + [hbm] * 8 + [vm] * 4,
         out_specs=[vm] * 17 + [hbm] * 11,
         scratch_shapes=[pltpu.VMEM((block, head_dim), BF), pltpu.VMEM((8, block), F32)]
         + [pltpu.VMEM(size, BF) for size in weights + acts]
         + [pltpu.VMEM((tokens, ff_part), BF), pltpu.VMEM((ff_part, tokens), BF)]
         + scatter_bufs * 2
         + [
-            dma((17, 10)),
-            dma((4, 8)),
-            dma((4, 8)),
-            dma((4, 4)),
-            dma((4, 4)),
+            dma((18, 10)),
+            dma((4, 8 * PIECES)),
+            dma((4, 8 * PIECES)),
+            dma((4, 4 * PIECES)),
+            dma((4, 4 * PIECES)),
             dma((24,)),
             dma((24,)),
             dma((11,)),
@@ -1410,7 +1466,8 @@
     gdown,
     came_g,
     came_u,
-    turned_all,
+    turned_far,
+    turned_near,
     vq,
     vkv,
     vo,
@@ -1470,6 +1527,7 @@
     done_sems,
     ff_sems,
     down_sems,
+    turned_sems,
 ):
     core, row, col = lax.axis_index("seq"), lax.axis_index("row"), lax.axis_index("col")
     place = (core, row, col)
@@ -1513,9 +1571,45 @@
     for load in loads:
         load.start()
     pl.semaphore_wait(barrier, 10)
-    block_of, halves_of = by_cols(turned_all, tokens)
-    get_turned = RowGather(place, turned_in, block_of, halves_of, row_sems.at[0])
-    get_turned.start()
+    half_ff = ff_part // 2
+
+    def turned_on(part, mask):
+        rows = pl.ds(part * half_ff + (mask - 1) * (half_ff // 2), half_ff // 2)
+        first = pl.multiple_of((row ^ (3 - mask)) * tokens, tokens)
+        if part == 0:
+            source = turned_in.at[rows, pl.ds(first, tokens)]
+        else:
+            source = turned_near.at[2 - mask, pl.ds((mask - 1) * (half_ff // 2), half_ff // 2)]
+        lane = part * 2 + mask - 1
+        return remote(
+            source,
+            turned_far.at[rows],
+            row_sems.at[0, lane],
+            row_sems.at[0, 6 + lane],
+            (core, row ^ mask, col),
+        )
+
+    def turned_over(mask):
+        return remote(
+            turned_in.at[
+                pl.ds(half_ff, half_ff), pl.ds(pl.multiple_of(row * tokens, tokens), tokens)
+            ],
+            turned_near.at[mask - 1],
+            row_sems.at[0, 3 + mask],
+            row_sems.at[0, 9 + mask],
+            (core, row ^ mask, col),
+        )
+
+    for mask in (1, 2):
+        turned_on(0, mask).start()
+        turned_over(mask).start()
+
+    def turned_rest():
+        for mask in (1, 2):
+            turned_over(mask).wait_recv()
+        for mask in (1, 2):
+            turned_on(1, mask).start()
+
 
     def gain(index):
         return gains[pl.ds(index, 1)]
@@ -1587,7 +1681,7 @@
 
     small(0, rank, mm_tn(gp_low, d_pp_low))
     small(1, rank, mm_tn(d_pg_low, h_low))
-    gather_ff.forward([lambda: None, lambda: None, get_turned.forward])
+    gather_ff.forward([lambda: None, turned_rest])
     gather_ff.finish()
 
     part_rows = tokens // 2
@@ -1651,17 +1745,30 @@
 
     scatter_f = Scatter(place, own_tokens, (give, keep, got, sent, left, right), sems(1))
     back_ff(give, away)
-    scatter_f.sibling().start()
+    scatter_f.start()
     back_ff(keep, home)
 
     put_g = RowScatter(place, by_rows(vg, block)[1], came_g, row_sems.at[1], (stage_g, stage_sems))
     put_u = RowScatter(place, by_rows(vu, block)[1], came_u, row_sems.at[2], (stage_g, stage_sems))
 
-    load_turned = pltpu.make_async_copy(turned_all, vd, load_sems.at[5])
+    def load_turned(lane):
+        mask, part = ((0, None), (3, None), (1, 0), (1, 1), (2, 0), (2, 1))[lane]
+        cols = pl.ds(pl.multiple_of((row ^ mask) * tokens, tokens), tokens)
+        if part is None:
+            source = turned_far if mask else turned_in.at[:, cols]
+            target = vd.at[:, cols]
+        else:
+            rows = pl.ds(part * half_ff, half_ff)
+            source = turned_near.at[mask - 1] if part else turned_in.at[rows, cols]
+            target = vd.at[rows, cols]
+        return pltpu.make_async_copy(source, target, turned_sems.at[lane])
 
     def down_ready():
-        get_turned.finish()
-        load_turned.start()
+        for mask in (1, 2):
+            for part in range(2):
+                turned_on(part, mask).wait_recv()
+        for lane in range(6):
+            load_turned(lane).start()
         for mask in (1, 2, 3):
             ff_came(mask).wait_recv()
             ff_share(mask, core).start()
@@ -1681,7 +1788,8 @@
         return slot, rows, local, over
 
     def down_grad():
-        load_turned.wait()
+        for lane in range(6):
+            load_turned(lane).wait()
         for mask in (1, 2, 3):
             ff_share(mask, 1 - core).wait_recv()
         for index in range(ff_part // tile):
@@ -1713,6 +1821,7 @@
 
     scatter_f.run(own_sum, [start_gate, start_up, down_ready])
 
+    gather_ff.drain()
     f_normed, f_factor = rms(h_two_ref[...])
     d_f, gain_three = rms_back(own_sum[...], f_normed, f_factor, gain(3))
     d_half = (d_three_ref[...] + d_f) * ROOT_HALF
@@ -1742,20 +1851,19 @@
     def small_sum():
         small_swap.wait_recv()
         small_keep[...] = (small_keep[...].astype(F32) + small_got[...].astype(F32)).astype(BF)
-        put_s.start()
 
     def middle_gate():
         put_g.fetch(1, 3)
         down_grad()
         put_g.middle()
 
-    def more_up():
-        put_u.start((0, 2))
+    def more_small():
         small_sum()
         put_g.fetch(0, 2)
 
-    gather_a.forward([middle_gate, more_up, put_g.early])
+    gather_a.forward([middle_gate, more_small, put_g.early])
     gather_a.finish()
+    scatter_f.drain()
 
     loads[6].wait()
     d_o[...] = mm_nt(dattng[...], vo[...]).astype(BF)
@@ -1803,6 +1911,7 @@
     kv_x[...] = (d_kv[core, theirs] + kv_got[theirs].astype(F32)).astype(BF)
     over_x = remote(kv_x, kv_x_got, misc_send.at[10], misc_recv.at[10], (core, row ^ 1, col))
     over_x.start()
+    put_u.start((0, 2))
     load_x = pltpu.make_async_copy(xg_in, dffg, load_sems.at[10])
     for mask in (1, 2, 3):
         ff_over(mask).wait_send()
@@ -1810,9 +1919,8 @@
     put_u.fetch(1, 3)
     out_grad()
     put_u.middle()
+    put_s.start()
     put_o.start()
-    put_s.fetch(1, 3)
-    put_s.middle()
     loads[7].wait()
     loads[8].wait()
     over_x.wait_recv()
@@ -1821,8 +1929,6 @@
     kv_p[...] = d_kind.astype(BF)
     over_p = remote(kv_p, kv_p_got, misc_send.at[11], misc_recv.at[11], (core, row, col ^ 1))
     over_p.start()
-    put_u.fetch(0, 2)
-    put_u.early()
     over_p.wait()
     d_kind = kv_p[...].astype(F32) + kv_p_got[...].astype(F32)
     is_key = core == 0
@@ -1854,7 +1960,7 @@
 
     scatter_x = Scatter(place, own_tokens, (give, keep, got, sent, left, right), sems(3))
     back_heads(give, away)
-    scatter_x.sibling().start()
+    scatter_x.start()
     back_heads(keep, home)
     put_q = RowScatter(place, by_rows(vq, block)[1], came_q, row_sems.at[4])
     put_kv = RowScatter(place, by_rows(pkv, block)[1], came_kv, row_sems.at[5])
@@ -1901,22 +2007,15 @@
             (core, row, col ^ mask),
         )
 
-    def small_finish():
-        put_s.fetch(0, 2, 4, 5)
-        put_s.early()
-        put_s.finish()
-        for mask in (1, 2, 3):
-            small_quarter(mask).start()
-
     def gate_finish():
-        put_o.fetch(1, 3)
-        put_o.middle()
         put_g.fetch(4, 5)
         put_g.finish()
         deliver(1, vg.at[row_block], ggate.at[:, core_ff])
+        put_u.fetch(0, 2)
+        put_u.early()
 
     d_half_here = d_three_ref
-    scatter_x.run(h_two_ref, [query_grad, small_finish, gate_finish])
+    scatter_x.run(h_two_ref, [query_grad, gate_finish])
     d_xn = own_sum[...] + h_two_ref[...]
     x_normed, x_factor = rms(x_own[...].astype(F32))
     d_in, gain_zero = rms_back(d_xn, x_normed, x_factor, gain(0))
@@ -1964,11 +2063,17 @@
     for other, mask in members:
         gain_group(other, mask).start()
     gcame2[me] = gpart2[...]
-    put_kv.fetch(1, 3)
-    put_kv.middle()
-    put_q.fetch(1, 3)
-    put_q.middle()
+    for put in (put_s, put_o, put_q, put_kv):
+        put.fetch(1, 3)
+        put.middle()
     put_u.fetch(4, 5)
+    put_u.finish()
+    deliver(2, vu.at[row_block], gup.at[:, core_ff])
+    put_s.fetch(0, 2, 4, 5)
+    put_s.early()
+    put_s.finish()
+    for mask in (1, 2, 3):
+        small_quarter(mask).start()
 
     def small_share(other, mask):
         lane = 16 + other * 4 + mask
@@ -1980,8 +2085,6 @@
             (core ^ other, row, col ^ mask),
         )
 
-    put_u.finish()
-    deliver(2, vu.at[row_block], gup.at[:, core_ff])
     for mask in (1, 2, 3):
         small_quarter(mask).wait_recv()
     small_total = small_keep[
@@ -2018,6 +2121,8 @@
         head = 2 * (who % 4) + who // 4
         tops[pl.ds(head, 1)] = gcame2[who, pl.ds(8, 1), pl.ds(0, 128)]
 
+    gather_a.drain()
+    scatter_x.drain()
     for other, mask in members:
         part = small_a.at[core ^ other, col ^ mask]
         lane = 16 + other * 4 + mask
@@ -2033,6 +2138,10 @@
     small_swap.wait_send()
     for put in (put_g, put_u, put_o, put_q, put_kv, put_s):
         put.drain()
+    for mask in (1, 2):
+        turned_over(mask).wait_send()
+        for part in range(2):
+            turned_on(part, mask).wait_send()
     for mask in (1, 2, 3):
         ff_share(mask, core).wait_send()
     for index in range(ff_part // tile):
@@ -2088,7 +2197,8 @@
         shape((2 * ff_part, block), BF),
         shape((6, block // 2, ff_part), BF),
         shape((6, block // 2, ff_part), BF),
-        shape((ff_part, 4 * tokens), BF),
+        shape((ff_part, tokens), BF),
+        shape((2, ff_part // 2, tokens), BF),
     ]
     scratch = [
         vmem((width, head_dim), BF),
@@ -2139,10 +2249,10 @@
         dma((2,)),
         dma((11,)),
         dma((7, 12)),
-        dma((4, 8)),
-        dma((4, 8)),
-        dma((4, 4)),
-        dma((4, 4)),
+        dma((4, 8 * PIECES)),
+        dma((4, 8 * PIECES)),
+        dma((4, 4 * PIECES)),
+        dma((4, 4 * PIECES)),
         dma((24,)),
         dma((24,)),
         dma((12,)),
@@ -2150,12 +2260,13 @@
         dma((24,)),
         dma((16,)),
         dma((12,)),
+        dma((6,)),
     ]
     return pl.pallas_call(
         backward_kernel,
         out_shape=outs,
         in_specs=[vm] * 22 + [hbm] * 11,
-        out_specs=[vm] * 5 + [hbm] * 9,
+        out_specs=[vm] * 5 + [hbm] * 10,
         scratch_shapes=scratch,
         compiler_params=pltpu.CompilerParams(
             collective_id=1, has_side_effects=True, vmem_limit_bytes=VMEM_BYTES
@@ -2164,6 +2275,127 @@
             flops=4 * 10**10, bytes_accessed=10**8, transcendentals=2 * 10**6
         ),
     )(*small_args, *big_args)
+
+
+def finish_kernel(
+    y_in,
+    x_in,
+    gains,
+    tops,
+    small,
+    gq,
+    gkv,
+    gout,
+    ggate,
+    gup,
+    gdown,
+    head_gains,
+    y_out,
+    x_out,
+    o_query,
+    o_key,
+    o_value,
+    o_out,
+    o_gate,
+    o_up,
+    o_down,
+    o_left,
+    o_right,
+    o_per_gate,
+    o_per_proj,
+    o_gains,
+    o_head,
+    o_clip,
+):
+    o_query[...] = gq[...].astype(F32)
+    o_key[...] = gkv[0].astype(F32)
+    o_value[...] = gkv[1].astype(F32)
+    o_out[...] = gout[...].astype(F32)
+    o_gate[...] = ggate[...].astype(F32)
+    o_up[...] = gup[...].astype(F32)
+    o_down[...] = gdown[...].astype(F32)
+    head_dim = head_gains.shape[1]
+    quarter = small.shape[3]
+    rank = o_right.shape[0]
+
+    @pl.when(pl.program_id(0) == 0)
+    def _():
+        own = y_in.shape[1]
+        for part in range(4):
+            rows = pl.ds(part % 2 * own, own)
+            y_out[part // 2, rows] = y_in[part]
+            x_out[part // 2, rows] = x_in[part]
+
+    @pl.when(pl.program_id(0) == 1)
+    def _():
+        for part in range(4):
+            cols = pl.ds(part * quarter, quarter)
+            first = small[0, part].astype(F32)
+            o_right[:, cols] = first[:rank]
+            o_per_proj[:, cols] = first[rank:]
+            second = small[1, part].astype(F32)
+            o_left[cols] = second[:rank].T
+            o_per_gate[cols] = second[rank:].T
+
+    @pl.when(pl.program_id(0) == 2)
+    def _():
+        o_gains[...] = gains[pl.ds(0, 6)]
+        o_head[pl.ds(0, 1)] = gains[pl.ds(6, 1), pl.ds(0, head_dim)]
+        o_head[pl.ds(1, 1)] = gains[pl.ds(6, 1), pl.ds(head_dim, head_dim)]
+        factor = jnp.sqrt(CLIP_LEVEL / jnp.maximum(tops[...], CLIP_LEVEL))[:, :1]
+        o_clip[0] = factor * head_gains[pl.ds(0, 1)]
+        o_clip[1] = factor * head_gains[pl.ds(1, 1)]
+
+
+def run_finish(results, head_gains, rank):
+    y_out, x_grad, g_gain, tops, small, gq, gkv, gout, ggate, gup, gdown = results
+    steps = 8
+    shape = jax.ShapeDtypeStruct
+
+    def whole(array):
+        dims = len(array.shape)
+        return pl.BlockSpec(array.shape, lambda step: (0,) * dims)
+
+    def rows(array):
+        size = (array.shape[0] // steps, array.shape[1])
+        return pl.BlockSpec(size, lambda step: (step, 0))
+
+    own, block = y_out.shape[1:]
+    key_width = gkv.shape[2]
+    proj = small.shape[2] - rank
+    tokens_shape = shape((2, 2 * own, block), BF)
+    by_rows_out = [
+        shape(gq.shape, F32),
+        shape(gkv.shape[1:], F32),
+        shape(gkv.shape[1:], F32),
+        shape(gout.shape, F32),
+        shape(ggate.shape, F32),
+        shape(gup.shape, F32),
+        shape(gdown.shape, F32),
+    ]
+    whole_out = [
+        shape((block, rank), F32),
+        shape((rank, block), F32),
+        shape((block, proj), F32),
+        shape((proj, block), F32),
+        shape((6, block), F32),
+        shape(head_gains.shape, F32),
+        shape((2, tops.shape[0], head_gains.shape[1]), F32),
+    ]
+    kv_spec = pl.BlockSpec((2, block // steps, key_width), lambda step: (0, step, 0))
+    return pl.pallas_call(
+        finish_kernel,
+        grid=(steps,),
+        out_shape=[tokens_shape, tokens_shape] + by_rows_out + whole_out,
+        in_specs=[whole(y_out), whole(x_grad), whole(g_gain), whole(tops), whole(small), rows(gq), kv_spec]
+        + [rows(array) for array in (gout, ggate, gup, gdown)]
+        + [whole(head_gains)],
+        out_specs=[whole(tokens_shape)] * 2
+        + [rows(array) for array in by_rows_out]
+        + [whole(array) for array in whole_out],
+        compiler_params=pltpu.CompilerParams(vmem_limit_bytes=VMEM_BYTES),
+        cost_estimate=pl.CostEstimate(flops=10**7, bytes_accessed=3 * 10**7, transcendentals=0),
+    )(*results, head_gains)
 
 
 def body_pair(
@@ -2216,7 +2448,6 @@
     allowed = (key_place[None, :] <= place[:, None]) & (key_place[None, :] >= start[:, None])
     cosine_table, sine_table = rotation(place - start, head_dim)
 
-    w_kv = jnp.where(core == 0, w_key, w_value)
     rank = laurel_left.shape[1]
     saved = run_forward(
         layer_in.reshape(rows, own_tokens, -1),
@@ -2224,7 +2455,8 @@
         norm_gains,
         (
             w_query,
-            w_kv,
+            w_key,
+            w_value,
             w_out,
             w_gate,
             w_up,
@@ -2247,20 +2479,7 @@
     l_left, l_right, p_gate, p_proj = saved[13:17]
     w_q, w_kv_all, w_o, w_g, w_u, w_d, x_all, f_all, gate_val, up_val, turned = saved[17:]
     half_table = head_dim // 2
-    (
-        y_out,
-        x_grad,
-        g_gain,
-        tops,
-        small_sums,
-        g_q,
-        g_kv,
-        g_o,
-        g_g,
-        g_u,
-        g_d,
-        *came,
-    ) = run_backward(
+    results = run_backward(
         (
             x_own,
             g_own,
@@ -2287,29 +2506,7 @@
         ),
         (x_all, f_all, gate_val, up_val, turned, w_q, w_kv_all, w_o, w_g, w_u, w_d),
     )
-    sums_a = small_sums[0].transpose(1, 0, 2).reshape(small_sums.shape[2], -1).astype(F32)
-    sums_b = small_sums[1].transpose(0, 2, 1).reshape(-1, small_sums.shape[2]).astype(F32)
-    logit_top = tops[:, 0]
-    clip_factor = jnp.sqrt(CLIP_LEVEL / jnp.maximum(logit_top, CLIP_LEVEL))
-    clipped_gains = clip_factor[None, :, None] * head_gains[:, None, :]
-    return (
-        y_out.reshape(layer_in.shape),
-        x_grad.reshape(layer_in.shape),
-        g_q.astype(F32),
-        g_kv[0].astype(F32),
-        g_kv[1].astype(F32),
-        g_o.astype(F32),
-        g_g.astype(F32),
-        g_u.astype(F32),
-        g_d.astype(F32),
-        sums_b[:, :rank],
-        sums_a[:rank],
-        sums_b[:, rank:],
-        sums_a[rank:],
-        g_gain[:6],
-        g_gain[6].reshape(head_gains.shape),
-        clipped_gains,
-    )
+    return tuple(run_finish(results[:11], head_gains, rank))
 
 
 def solution(mesh):

time: 435 us -> 391 us (0.90)
  Pallas kernels: 400 us -> 378 us
  other arithmetic: 19 us -> 2.02 us
  local copies, waits for them, and re-layouts: 10.2 us -> 4.85 us
    pallas_call x1, Pallas kernels: 208 us -> 185 us  [run_backward(): pl.pallas_call(backward_kernel, out_shape=outs, in_specs=[vm] * 22 + [hbm...]
    convert_element_type x7 -> x0, other arithmetic: 13.9 us -> none  [the longest x1 2.61 us: body_pair(): g_d.astype(F32)]
    pallas_call x0 -> x1, Pallas kernels: none -> 11.1 us  [run_finish(): pl.pallas_call(finish_kernel, grid=(steps,), out_shape=[tokens_shape, tok...]
    pallas_call x1, Pallas kernels: 192 us -> 182 us  [run_forward(): pl.pallas_call(forward_kernel, out_shape=outs, in_specs=[vm, vm, vm, hbm,...]
where the time goes in v4:
time: 391 us; the launch traced here: 386 us
  Pallas kernels  378 us (97%)
  local copies, waits for them, and re-layouts  4.85 us (1%)
    pallas_call x1, Pallas kernels, run_backward(): pl.pallas_call(backward_kernel, out_shape=outs, in_specs=[vm] * 22 + [hbm...  185 us
    pallas_call x1, Pallas kernels, run_forward(): pl.pallas_call(forward_kernel, out_shape=outs, in_specs=[vm, vm, vm, hbm,...  182 us
    pallas_call x1, Pallas kernels, run_finish(): pl.pallas_call(finish_kernel, grid=(steps,), out_shape=[tokens_shape, tok...  11.1 us

profile of v4, /device:TPU:1, one launch (start us, length us, event | category | flops | bytes accessed | tf_op | source)
XLA Modules:
  0.0 385.9 jit_solution(6790898102495328399)
XLA Ops:
  0.6 0.0 copy-start
  0.7 0.6 copy-done
  1.3 0.1 multiply_reduce_fusion
  1.5 0.1 select_reduce_fusion
  1.6 1.6 copy.39.laurel_left
  3.2 0.9 copy.40.start
  4.0 1.8 multiply_sine_fusion
  5.8 181.9 %shard_map.288 = (bf16[64,2048]{1,0:T(8,128)(2,1)}, bf16[64,2048]{1,0:T(8,128)(2,1)}, f32[8,2048]{1,0:T(8,128)}, f32[512,256]{1,0:T(8,128)}, f32[512,256]{1,0:T(...) custom-call(bf16[4,64,512]{2,1,0:T(8,128)(2,1)} %bitcast.7, ...), custom_call_target="tpu_custom_call" | custom-call | flops 20000000000 | bytes 50000000 | tf_op jit(solution)/shard_map/pallas_call | solution.py:1322
  187.7 185.1 %shard_map.289 = (bf16[4,64,512]{2,1,0:T(8,128)(2,1)}, bf16[4,64,512]{2,1,0:T(8,128)(2,1)}, f32[8,512]{1,0:T(8,128)}, f32[8,128]{1,0:T(8,128)}, bf16[2,4,320,128...) custom-call(bf16[64,2048]{1,0:T(8,128)(2,1)} %get-tuple-element.55.x, ...), custom_call_target="tpu_custom_call" | custom-call | flops 40000000000 | bytes 100000000 | tf_op jit(solution)/shard_map/pallas_call | solution.py:2265
  372.8 0.0 copy-start.1
  372.8 11.1 %shard_map.290 = (bf16[2,128,512]{2,1,0:T(8,128)(2,1)}, bf16[2,128,512]{2,1,0:T(8,128)(2,1)}, f32[512,512]{1,0:T(8,128)}, f32[512,128]{1,0:T(8,128)}, f32[512,12...) custom-call(bf16[4,64,512]{2,1,0:T(8,128)(2,1)} %get-tuple-element.8, ...), custom_call_target="tpu_custom_call" | custom-call | flops 10000000 | bytes 30000000 | tf_op jit(solution)/shard_map/pallas_call | solution.py:2386
  383.9 1.7 copy.42
  385.7 0.0 copy-done.1
  (4 shorter events, 0.0 us)
Async XLA Ops:
  0.6 0.7 copy-start
  372.8 12.8 %copy-start.1 = (s32[2,4]{1,0:T(2,128)S(1)}, s32[2,4]{1,0:T(2,128)}, u32[]{:S(2)}) copy-start(s32[2,4]{1,0:T(2,128)} %param.19) | copy-start | bytes 100
